TPU v7x, 32 devices: a whole 2x2x4 slice. The times are simulated.
32 devices in a mesh: row: 4 (over x, core), col: 8 (over z, y).
Axes of the slice: x: 2, y: 2, z: 4, core: 2. Of those that a mesh axis runs over, the one named last changes fastest.
Arguments:
- hamiltonian: float32 [4096, 1024], P('row', 'col'), may hold values from -0.09375 to 0.09375
- pattern: int32 [128, 32], P('row', 'col'), may hold values 0 or 1
- onsite: float32 [4096], P('row'), may hold values from -1 to 1
- members: int32 [32, 32], replicated, may hold values from 0 to 31, as said below
- orders: int32 [32], replicated, may hold values from 16 to 32, as said below
- intersection_inv: bfloat16 [4096, 3, 1024], P(('row', 'col')), may hold values from -6 to 6
Outputs:
- density: float32 [4096, 3, 1024], P(('row', 'col'))
Inputs may be any that keep to these rules, and one draw needn't show every extreme that they name: `members`: each row holds 32 distinct team block indices; the first 4 of row g are (g mod 8) * 4 onward in rising order. `orders`: some group has all 32 members active.
All inputs are finite; a program needn't handle non-finite values. No bound on the sum of `pattern` on one device may be relied on, other than what follows from the above.
Results may differ from a plain program's by a relative error of at most 0.0027.
Values may be sent and summed in bfloat16 or wider, within the bound.
No kernel may reach another device: no remote copies, remote signals or barrier semaphores. Data moves between devices by JAX's collectives and lax.ppermute only.
A program may use at most 256 MiB of HBM per device.

v0:
```python
import jax
import jax.numpy as jnp
from jax import lax
from jax.sharding import PartitionSpec as P

BLOCK = 32
OWN_BLOCKS = 4
MEMBERS = 32


def with_halo(shard, sides, width):
    for axis, dim in sides:
        count, length = (lax.axis_size(axis), shard.shape[dim])
        up = [(i, (i + 1) % count) for i in range(count)]
        down = [(j, i) for i, j in up]
        last = lax.slice_in_dim(shard, length - width, length, axis=dim)
        first = lax.slice_in_dim(shard, 0, width, axis=dim)
        before = lax.ppermute(last, axis, up)
        after = lax.ppermute(first, axis, down)
        shard = jnp.concatenate([before, shard, after], axis=dim)
    return shard


def sign_columns(submatrix, active_count, own_width):
    squares = jnp.sum(submatrix * submatrix)
    factor = jnp.sqrt(active_count.astype(jnp.float32) * BLOCK / (4.0 * (squares + 1e-06)))
    initial = factor * submatrix
    square = jnp.dot(
        initial, initial, precision=lax.Precision.HIGHEST, preferred_element_type=jnp.float32
    )
    first_step = 0.5 * (
        3.0 * initial
        - jnp.dot(
            initial, square, precision=lax.Precision.HIGHEST, preferred_element_type=jnp.float32
        )
    )
    left_cols = first_step[:, :own_width]
    inner_prod = jnp.dot(
        first_step, left_cols, precision=lax.Precision.HIGHEST, preferred_element_type=jnp.float32
    )
    return 0.5 * (
        3.0 * left_cols
        - jnp.dot(
            first_step,
            inner_prod,
            precision=lax.Precision.HIGHEST,
            preferred_element_type=jnp.float32,
        )
    )


def shards(hamiltonian, pattern, onsite, members, orders, intersection_inv):
    slot_count = lax.axis_size("col")
    team_count = lax.axis_size("row")
    team_index = lax.axis_index("row")
    slot_index = lax.axis_index("col")
    own_width = OWN_BLOCKS * BLOCK
    sub_width = MEMBERS * BLOCK
    team_blocks = slot_count * OWN_BLOCKS
    team_width = team_blocks * BLOCK
    team_members = lax.dynamic_slice_in_dim(members, team_index * slot_count, slot_count, 0)
    team_orders = lax.dynamic_slice_in_dim(orders, team_index * slot_count, slot_count, 0)
    group_members = lax.dynamic_index_in_dim(team_members, slot_index, 0, keepdims=False)
    group_order = lax.dynamic_index_in_dim(team_orders, slot_index, 0, keepdims=False)
    weights = jnp.broadcast_to(
        pattern.astype(jnp.float32)[:, None, :, None],
        (pattern.shape[0], BLOCK, pattern.shape[1], BLOCK),
    ).reshape(hamiltonian.shape)
    masked = hamiltonian * weights
    row_blocks = masked.reshape(team_blocks, BLOCK, own_width)
    outgoing = jnp.take(row_blocks, team_members.reshape(-1), axis=0).reshape(
        slot_count * sub_width, own_width
    )
    incoming = lax.all_to_all(outgoing, "col", split_axis=0, concat_axis=0, tiled=True)
    by_block = (
        incoming.reshape(slot_count, sub_width, OWN_BLOCKS, BLOCK)
        .transpose(0, 2, 1, 3)
        .reshape(slot_count * OWN_BLOCKS, sub_width, BLOCK)
    )
    picked = jnp.take(by_block, group_members, axis=0)
    coupling = picked.transpose(1, 0, 2).reshape(sub_width, sub_width)
    active = jnp.repeat((jnp.arange(MEMBERS) < group_order).astype(jnp.float32), BLOCK)
    coupling = coupling * active[:, None] * active[None, :]
    diag_vals = (
        jnp.take(onsite.reshape(team_blocks, BLOCK), group_members, axis=0).reshape(sub_width)
        * active
    )
    submatrix = 0.5 * (coupling + coupling.T) + jnp.diag(diag_vals)
    sign_cols = sign_columns(submatrix, group_order, own_width).astype(jnp.bfloat16)
    shifts = jnp.arange(3, dtype=jnp.int32) - 1
    near_team_ids = (team_index + shifts) % team_count
    near_members = jnp.take(members.reshape(team_count, slot_count, MEMBERS), near_team_ids, axis=0)
    placement = (
        near_members[:, :, None, :] == jnp.arange(team_blocks, dtype=jnp.int32)[:, None]
    ).astype(jnp.bfloat16)
    team_signs = lax.all_gather(sign_cols, "col", axis=0, tiled=True)
    near_signs = with_halo(team_signs[None], (("row", 0),), 1)
    signs_split = near_signs.reshape(3, slot_count, MEMBERS, BLOCK * own_width)
    results = []
    for side_index in range(3):
        placed = jnp.einsum(
            "cba,cam->bcm",
            placement[side_index],
            signs_split[side_index],
            preferred_element_type=jnp.float32,
        )
        team_sign = (
            placed.astype(jnp.bfloat16)
            .reshape(team_blocks, slot_count, BLOCK, own_width)
            .transpose(0, 2, 1, 3)
            .reshape(team_width, team_width)
        )
        results.append(
            jnp.dot(
                intersection_inv[:, side_index, :], team_sign, preferred_element_type=jnp.float32
            )
        )
    return jnp.stack(results, axis=1)


def solution(mesh):
    in_specs = (P("row", "col"), P("row", "col"), P("row"), P(), P(), P(("row", "col"), None, None))
    out_specs = P(("row", "col"), None, None)
    return jax.shard_map(shards, mesh=mesh, in_specs=in_specs, out_specs=out_specs, check_vma=False)
```

profile of v0, /device:TPU:0, one launch (start us, length us, event | category | flops | bytes accessed | tf_op | source)
XLA Modules:
  0.0 330.1 jit_solution(11126240515184051074)
XLA Ops:
  9.7 3.0 gather_fusion
  12.7 5.2 %bitcast_select_fusion = f32[8,1024,128]{2,1,0:T(8,128)} fusion(pred[8,1024]{1,0:T(8,128)(4,1)S(1)} %broadcast_in_dim.77, f32[8,1024,128]{2,1,0:T(8,128)} %bitcast.116), kind=kLoop, calls=%fused_computation.13 | loop fusion | flops 1048576 | bytes 8396800 | tf_op jit(solution)/shard_map/jit(_take)/select_n | solution.py:71
  17.9 7.4 %all-to-all-start = ((f32[8,1024,128]{2,1,0:T(8,128)}), f32[8,1024,128]{2,1,0:T(8,128)}, u32[]{:S(2)}, u32[]{:S(2)}) async-start(f32[8,1024,128]{2,1,0:T(8,128)} %bitcast_select_fusion), calls=%async_computation | async-start | bytes 8388608 | tf_op jit(solution)/shard_map/all_to_all | solution.py:74
  28.5 90.1 %all-to-all-done = f32[8,1024,128]{2,1,0:T(8,128)} async-done(((f32[8,1024,128]{2,1,0:T(8,128)}), f32[8,1024,128]{2,1,0:T(8,128)}, u32[]{:S(2)}, u32[]{:S(2)}) %all-to-all-start) | async-done | bytes 4194336 | tf_op jit(solution)/shard_map/all_to_all | solution.py:74
  118.7 9.6 %fusion.44 = (f32[8,1024,32]{2,1,0:T(8,128)S(1)}, f32[8,1024,32]{2,1,0:T(8,128)S(1)}, f32[8,1024,32]{2,1,0:T(8,128)S(1)}, f32[8,1024,32]{2,1,0:T(8,128)S(1)}) fusion(f32[8,1024,128]{2,1,0:T(8,128)} %all-to-all-done), kind=kLoop, calls=%fused_computation.79 | loop fusion | bytes 8388608 | tf_op jit(solution)/shard_map/slice.3
  128.3 6.0 %pad_maximum_fusion = f32[8,4096,32]{2,1,0:T(8,128)} fusion(f32[8,1024,32]{2,1,0:T(8,128)S(1)} %get-tuple-element.10, f32[8,1024,32]{2,1,0:T(8,128)S(1)} %get-tuple-element.11, f32[8,1024,32]{2,1,0:T(8,128)S(1)} %get-tuple-element.12, f32[8,1024,32]{2,1,0:T(8,128)S(1)} %get-tuple-element.9), kind=kLoop, calls=%fused_computation.4 | loop fusion | flops 3145728 | bytes 8388608 | tf_op jit(solution)/shard_map/concatenate
  134.3 11.4 %copy.46 = f32[32,1024,32]{1,2,0:T(8,128)} copy(f32[32,1024,32]{2,1,0:T(8,128)} %bitcast.114) | data formatting | bytes 8388608 | tf_op jit(solution)/shard_map/reshape | solution.py:78
  145.7 4.9 %gather_fusion.1 = f32[32,1024,32]{1,2,0:T(8,128)} fusion(f32[32,1024,32]{1,2,0:T(8,128)} %copy.46, s32[1024]{0:T(1024)S(1)} %pad_clamp_fusion.1), kind=kCustom, calls=%fused_computation.1 | custom fusion | bytes 8388736 | tf_op jit(solution)/shard_map/jit(_take)/gather | solution.py:80
  150.7 2.7 broadcast_select_fusion
  155.3 2.4 fusion
  157.7 5.4 %copy.47 = f32[1024,1024]{1,0:T(8,128)} copy(f32[1024,1024]{0,1:T(8,128)} %fusion) | data formatting | bytes 8388608 | tf_op jit(solution)/shard_map/mul | solution.py:83
  163.1 6.4 %multiply_reduce_fusion = (f32[]{:T(128)}, f32[1024,1024]{1,0:T(8,128)}) fusion(f32[1024]{0:T(1024)S(1)} %mul.77, f32[1024,1024]{1,0:T(8,128)} %copy.47, f32[1024]{0:T(1024)S(1)} %mul.71, f32[32,1024,32]{1,2,0:T(8,128)} %copy-done), kind=kLoop, calls=%fused_computation.15 | loop fusion | flops 9437183 | bytes 12591108 | tf_op jit(solution)/shard_map/reduce_sum | solution.py:25
  170.3 17.5 %fusion.5 = f32[1024,1024]{1,0:T(8,128)S(1)} fusion(f32[1024,1024]{1,0:T(8,128)} %get-tuple-element.6, f32[]{:T(128)S(6)} %sqrt.3), kind=kOutput, calls=%fused_computation.19 | convolution fusion | flops 12885950464 | bytes 8388612 | tf_op jit(solution)/shard_map/dot_general | solution.py:28
  187.7 14.1 %subtract_multiply_fusion = f32[1024,1024]{1,0:T(8,128)S(1)} fusion(f32[1024,1024]{1,0:T(8,128)S(1)} %copy-done.1, f32[1024,1024]{1,0:T(8,128)S(1)} %fusion.5, f32[]{:T(128)S(6)} %sqrt.3), kind=kOutput, calls=%fused_computation.14 | convolution fusion | flops 12890144768 | bytes 12582916 | tf_op jit(solution)/shard_map/dot_general | solution.py:33
  201.8 3.9 %fusion.31 = f32[1024,128]{1,0:T(8,128)S(1)} fusion(f32[1024,1024]{1,0:T(8,128)S(1)} %subtract_multiply_fusion), kind=kOutput, calls=%fused_computation.40 | convolution fusion | flops 1610612736 | bytes 5242880 | tf_op jit(solution)/shard_map/dot_general | solution.py:38
  205.7 4.1 %fusion.30 = bf16[1024,128]{1,0:T(8,128)(2,1)} fusion(f32[1024,1024]{1,0:T(8,128)S(1)} %subtract_multiply_fusion, f32[1024,128]{1,0:T(8,128)S(1)} %fusion.31), kind=kOutput, calls=%fused_computation.39 | convolution fusion | flops 1611137024 | bytes 5505024 | tf_op jit(solution)/shard_map/dot_general | solution.py:43
  209.9 48.5 %all-gather.2.cloned.1.call-done = bf16[8192,128]{1,0:T(8,128)(2,1)} async-done(((bf16[1024,128]{1,0:T(8,128)(2,1)}), bf16[8192,128]{1,0:T(8,128)(2,1)}) %all-gather.2.cloned.1.call-update) | async-done | bytes 2097168 | tf_op jit(solution)/shard_map/all_gather | solution.py:96
  260.9 3.0 squeeze.43
  265.0 2.4 copy.49
  269.2 35.6 %collective-permute-done = bf16[1,8192,128]{2,1,0:T(8,128)(2,1)} collective-permute-done((bf16[1,8192,128]{2,1,0:T(8,128)(2,1)}, bf16[1,8192,128]{2,1,0:T(8,128)(2,1)}, u32[]{:S(2)}, u32[]{:S(2)}) %collective-permute-start) | collective-permute-done | bytes 2097184 | tf_op jit(solution)/shard_map/ppermute | solution.py:18
  304.8 2.8 squeeze.40
  308.8 2.4 copy.48
  313.0 3.0 squeeze.46
  317.2 2.4 copy.50
  (57 shorter events, 20.4 us)
Async XLA Ops:
  6.5 3.1 copy-start.2
  17.9 7.7 %copy-start.5 = (s32[32]{0:T(128)S(1)}, s32[32]{0:T(128)}, u32[]{:S(2)}) copy-start(s32[32]{0:T(128)} %param.10) | copy-start | bytes 388
  17.9 9.7 %copy-start.4 = (f32[1024]{0:T(1024)S(1)}, f32[1024]{0:T(1024)}, u32[]{:S(2)}) copy-start(f32[1024]{0:T(1024)} %param.8) | copy-start | bytes 12292
  17.9 9.8 %copy-start.3 = (s32[32,32]{1,0:T(8,128)S(1)}, s32[32,32]{1,0:T(8,128)}, u32[]{:S(2)}) copy-start(s32[32,32]{1,0:T(8,128)} %param.9) | copy-start | bytes 12292
  17.9 100.7 %all-to-all-start = ((f32[8,1024,128]{2,1,0:T(8,128)}), f32[8,1024,128]{2,1,0:T(8,128)}, u32[]{:S(2)}, u32[]{:S(2)}) async-start(f32[8,1024,128]{2,1,0:T(8,128)} %bitcast_select_fusion), calls=%async_computation | async-start | bytes 8388608 | tf_op jit(solution)/shard_map/all_to_all | solution.py:74
  25.4 233.0 %all-gather.2.cloned.1.call-start = ((), (), s32[]{:S(2)}) async-start(), calls=%async_computation.1 | async-start | bytes 2359296 | tf_op jit(solution)/shard_map/all_gather | solution.py:96
  153.4 1.9 copy-start
  170.3 17.5 %copy-start.1 = (f32[1024,1024]{1,0:T(8,128)S(1)}, f32[1024,1024]{1,0:T(8,128)}, u32[]{:S(2)}) copy-start(f32[1024,1024]{1,0:T(8,128)} %get-tuple-element.6) | copy-start | bytes 12582916
  258.4 46.4 %collective-permute-start = (bf16[1,8192,128]{2,1,0:T(8,128)(2,1)}, bf16[1,8192,128]{2,1,0:T(8,128)(2,1)}, u32[]{:S(2)}, u32[]{:S(2)}) collective-permute-start(bf16[1,8192,128]{2,1,0:T(8,128)(2,1)} %bitcast.123), channel_id=1, source_target_pairs={{0,8},{8,16},{16,24},{24,0},{1,9},{9,17},{17,25},{25,1},{2,10},{10... | collective-permute-start | bytes 6291464 | tf_op jit(solution)/shard_map/ppermute | solution.py:18
  258.4 54.6 %collective-permute-start.1 = (bf16[1,8192,128]{2,1,0:T(8,128)(2,1)}, bf16[1,8192,128]{2,1,0:T(8,128)(2,1)}, u32[]{:S(2)}, u32[]{:S(2)}) collective-permute-start(bf16[1,8192,128]{2,1,0:T(8,128)(2,1)} %bitcast.124), channel_id=1, source_target_pairs={{8,0},{16,8},{24,16},{0,24},{9,1},{17,9},{25,17},{1,25},{10,2},{18... | collective-permute-start | bytes 6291464 | tf_op jit(solution)/shard_map/ppermute | solution.py:19
Sparse Core Ops, SparseCore 0:
  210.0 48.3 all-gather.1
where the time goes:
time: 334 us; the launch traced here: 330 us
  waiting for transfers between devices  174 us (52%)
  local copies, waits for them, and re-layouts  59.1 us (18%)
  matrix products  46.8 us (14%)
  other arithmetic  25.3 us (8%)
  between operations  15.3 us (5%)
  starting transfers between devices  9.41 us (3%)
    all_to_all x1, waiting for transfers between devices, shards(): lax.all_to_all(outgoing, 'col', split_axis=0, concat_axis=0, tiled=True)  90.1 us
    all_gather x1, waiting for transfers between devices, shards(): team_signs = lax.all_gather(sign_cols, 'col', axis=0, tiled=True)  48.5 us
    ppermute x1, waiting for transfers between devices, with_halo(): before = lax.ppermute(last, axis, up)  35.6 us
    dot_general x1, matrix products, sign_columns(): jnp.dot(initial, initial, precision=lax.Precision.HIGHEST, preferred_elem...  17.5 us
    dot_general x1, matrix products, sign_columns(): jnp.dot(initial, square, precision=lax.Precision.HIGHEST, preferred_eleme...  14.1 us
    reshape x1, local copies, waits for them, and re-layouts, shards(): by_block = incoming.reshape(slot_count, sub_width, OWN_BLOCKS, BLOCK).tra...  11.4 us
    another operation x1, local copies, waits for them, and re-layouts  9.64 us
    squeeze x3, local copies, waits for them, and re-layouts, shards(): signs_split[side_index]  8.85 us
  transfers between devices with their start and end apart: 4, of which 3 were waited for; matrix products, arithmetic and copies ran while one was open for 6% of the time, Pallas kernels for 0%

commit v1 on v0

v1 whole, which is shorter than its diff:
```python
import jax
import jax.numpy as jnp
from jax import lax
from jax.experimental import pallas as pl
from jax.experimental.pallas import tpu as pltpu
from jax.sharding import PartitionSpec as P

BLOCK = 32
OWN_BLOCKS = 4
MEMBERS = 32
INNER = 2
F32 = jnp.float32
BF16 = jnp.bfloat16
LAST = (((1,), (1,)), ((), ()))


def pairs(count, outer_shift, inner_shift):
    return [(i, i ^ (outer_shift * INNER + inner_shift)) for i in range(count)]


def gather_col(shard):
    count = lax.axis_size("col")
    parts = {}
    parts[0] = shard
    parts[1] = lax.ppermute(shard, "col", pairs(count, 0, 1))
    for shift in range(1, count // INNER):
        parts[shift * INNER] = lax.ppermute(shard, "col", pairs(count, shift, 0))
    for shift in range(1, count // INNER):
        parts[shift * INNER + 1] = lax.ppermute(parts[shift * INNER], "col", pairs(count, 0, 1))
    return [parts[k] for k in range(count)]


def sign_kernel(count, me_ref, active_ref, mask_col, mask_row, diag_row, *refs):
    shards = refs[:count]
    out_ref, ham = refs[count:]
    width = ham.shape[0]
    own = out_ref.shape[0]
    me = me_ref[0]
    squares = jnp.zeros((1, own), F32)
    rows = lax.broadcasted_iota(jnp.int32, (own, own), 0)
    cols = lax.broadcasted_iota(jnp.int32, (own, own), 1)
    eye = rows == cols
    for k in range(count):
        start = pl.multiple_of((me ^ k) * own, own)
        block = shards[k][...] * mask_col[...] * mask_row[:, pl.ds(start, own)]
        ham[:, pl.ds(start, own)] = block
        wide = block.astype(F32)
        squares += 0.5 * jnp.sum(wide * wide, axis=0, keepdims=True)
    for k in range(count):
        start = k * own
        diag = diag_row[:, start : start + own]
        across = ham[start : start + own, :]
        down = ham[:, start : start + own]
        both = jnp.dot(across, down, preferred_element_type=F32)
        here = ham[start : start + own, start : start + own].astype(F32)
        entries = 0.5 * both + 2.0 * diag * here
        squares += jnp.sum(jnp.where(eye, entries, 0.0), axis=0, keepdims=True)
        squares += diag * diag
    total = jnp.sum(squares, axis=1, keepdims=True)
    active_rows = active_ref[0].astype(F32) * BLOCK
    factor = jnp.sqrt(active_rows / (4.0 * (total + 1e-06)))
    diag_all = diag_row[...]

    def times(panel):
        high = panel.astype(BF16)
        low = (panel - high.astype(F32)).astype(BF16)
        stacked = jnp.concatenate([high, low], axis=0)
        prod = jnp.dot(stacked, ham[...], preferred_element_type=F32)
        prod += lax.dot_general(stacked, ham[...], LAST, preferred_element_type=F32)
        return factor * (0.5 * (prod[:own] + prod[own:]) + diag_all * panel)

    def cubic(panel):
        return 0.5 * (3.0 * panel - times(times(panel)))

    start = pl.multiple_of(me * own, own)
    turned = lax.dot_general(
        eye.astype(BF16), ham[:, pl.ds(start, own)], LAST, preferred_element_type=F32
    )
    across = ham[pl.ds(start, own), :].astype(F32)
    wide_rows = lax.broadcasted_iota(jnp.int32, (own, width), 0)
    wide_cols = lax.broadcasted_iota(jnp.int32, (own, width), 1)
    on_diag = wide_cols == wide_rows + start
    first = 0.5 * (turned + across) + jnp.where(on_diag, diag_all, 0.0)
    left = cubic(factor * first)
    inner = lax.fori_loop(0, 2, lambda _, panel: cubic(times(panel)), left)
    out_ref[...] = (0.5 * (3.0 * left - inner)).astype(BF16)


def sign_rows(shards, me, active, mask_row, diag_row):
    count = len(shards)
    width, own = shards[0].shape
    mask_col = jnp.broadcast_to(mask_row[:, None], (width, own)).astype(BF16)
    vmem = pl.BlockSpec(memory_space=pltpu.VMEM)
    smem = pl.BlockSpec(memory_space=pltpu.SMEM)
    return pl.pallas_call(
        lambda *refs: sign_kernel(count, *refs),
        out_shape=jax.ShapeDtypeStruct((own, width), BF16),
        in_specs=[smem, smem] + [vmem] * (3 + count),
        out_specs=vmem,
        scratch_shapes=[pltpu.VMEM((width, width), BF16)],
        compiler_params=pltpu.CompilerParams(vmem_limit_bytes=56 * 2**20),
        cost_estimate=pl.CostEstimate(
            flops=70 * own * width * width, bytes_accessed=2 * width * width, transcendentals=0
        ),
        name="sign_rows",
    )(me, active, mask_col, mask_row.astype(BF16)[None], diag_row[None], *shards)


def returned_kernel(count, above, below, *refs):
    signs = refs[:count]
    up_ref, down_ref = refs[count:]
    own = above.shape[0]
    for k in range(count):
        cols = slice(k * own, (k + 1) * own)
        up_ref[:, cols] = lax.dot_general(
            above[...], signs[k][...], LAST, preferred_element_type=F32
        )
        down_ref[:, cols] = lax.dot_general(
            below[...], signs[k][...], LAST, preferred_element_type=F32
        )


def returned(above, below, signs):
    count = len(signs)
    own, width = above.shape
    vmem = pl.BlockSpec(memory_space=pltpu.VMEM)
    shape = jax.ShapeDtypeStruct((own, count * own), F32)
    return pl.pallas_call(
        lambda *refs: returned_kernel(count, *refs),
        out_shape=(shape, shape),
        in_specs=[vmem] * (2 + count),
        out_specs=(vmem, vmem),
        compiler_params=pltpu.CompilerParams(vmem_limit_bytes=48 * 2**20),
        cost_estimate=pl.CostEstimate(
            flops=4 * own * width * own * count,
            bytes_accessed=2 * own * width * count,
            transcendentals=0,
        ),
        name="returned",
    )(above, below, *signs)


def final_kernel(count, chunks, me_ref, inv, *refs):
    signs = refs[:count]
    lower = refs[count : count + chunks]
    upper = refs[count + chunks : count + 2 * chunks]
    out_ref = refs[-1]
    own = inv.shape[0]
    per = count // chunks
    for k in range(count):
        start = pl.multiple_of((me_ref[0] ^ k) * own, own)
        cols = slice((k % per) * own, (k % per + 1) * own)
        out_ref[:, 0, pl.ds(start, own)] = lower[k // per][:, cols]
        out_ref[:, 1, pl.ds(start, own)] = lax.dot_general(
            inv[...], signs[k][...], LAST, preferred_element_type=F32
        )
        out_ref[:, 2, pl.ds(start, own)] = upper[k // per][:, cols]


def final(me, inv, signs, lower, upper):
    count = len(signs)
    own, width = inv.shape
    vmem = pl.BlockSpec(memory_space=pltpu.VMEM)
    smem = pl.BlockSpec(memory_space=pltpu.SMEM)
    return pl.pallas_call(
        lambda *refs: final_kernel(count, len(lower), *refs),
        out_shape=jax.ShapeDtypeStruct((own, 3, width), F32),
        in_specs=[smem] + [vmem] * (1 + count + 2 * len(lower)),
        out_specs=vmem,
        compiler_params=pltpu.CompilerParams(vmem_limit_bytes=48 * 2**20),
        cost_estimate=pl.CostEstimate(
            flops=2 * own * width * width, bytes_accessed=20 * own * width, transcendentals=0
        ),
        name="final",
    )(me, inv, *signs, *lower, *upper)


def shards(hamiltonian, pattern, onsite, members, orders, intersection_inv):
    slot_count = lax.axis_size("col")
    team_count = lax.axis_size("row")
    team_index = lax.axis_index("row")
    slot_index = lax.axis_index("col")
    team_blocks = slot_count * OWN_BLOCKS
    me = slot_index.astype(jnp.int32)[None]
    up = [(i, (i + 1) % team_count) for i in range(team_count)]
    down = [(j, i) for i, j in up]

    weights = jnp.broadcast_to(
        pattern.astype(F32)[:, None, :, None],
        (pattern.shape[0], BLOCK, pattern.shape[1], BLOCK),
    ).reshape(hamiltonian.shape)
    masked = (hamiltonian * weights).astype(BF16)
    parts = gather_col(masked)

    above = lax.ppermute(intersection_inv[:, 0, :], "row", down)
    below = lax.ppermute(intersection_inv[:, 2, :], "row", up)
    middle = intersection_inv[:, 1, :]

    group = team_index * slot_count + slot_index
    group_members = lax.dynamic_index_in_dim(members, group, 0, keepdims=False)
    group_order = lax.dynamic_index_in_dim(orders, group, 0, keepdims=False)
    chosen = (group_members[None, :] == jnp.arange(team_blocks, dtype=jnp.int32)[:, None]) & (
        jnp.arange(members.shape[1])[None, :] < group_order
    )
    mask_row = jnp.repeat(jnp.any(chosen, axis=1).astype(F32), BLOCK)
    diag_row = onsite * mask_row
    signs = sign_rows(parts, me, group_order[None], mask_row, diag_row)

    all_signs = gather_col(signs)
    order = [k for k in range(slot_count) if k % INNER == 0 or k == 1]
    order += [k for k in range(slot_count) if k % INNER == 1 and k != 1]
    half = slot_count // 2
    lower, upper = [], []
    for chunk in (range(half), range(half, slot_count)):
        to_up, to_down = returned(above, below, [all_signs[k] for k in chunk])
        lower.append(lax.ppermute(to_up, "row", up))
        upper.append(lax.ppermute(to_down, "row", down))
    return final(me, middle, all_signs, lower, upper)


def solution(mesh):
    in_specs = (P("row", "col"), P("row", "col"), P("row"), P(), P(), P(("row", "col"), None, None))
    out_specs = P(("row", "col"), None, None)
    return jax.shard_map(shards, mesh=mesh, in_specs=in_specs, out_specs=out_specs, check_vma=False)
```

time: 334 us -> 115 us (0.34); the launches traced: 330 us -> 115 us
  waiting for transfers between devices: 174 us -> 61.4 us
  local copies, waits for them, and re-layouts: 59.1 us -> 5.93 us
  matrix products: 46.8 us -> 0 us
  other arithmetic: 25.3 us -> 2.08 us
  Pallas kernels: 0 us -> 19.2 us
  starting transfers between devices: 9.41 us -> 25.7 us
  between operations: 15.3 us -> 0.21 us
    all_to_all x1 -> x0, waiting for transfers between devices: 90.1 us -> none  [shards(): lax.all_to_all(outgoing, 'col', split_axis=0, concat_axis=0, tiled=True)]
    all_gather x1 -> x0, waiting for transfers between devices: 48.5 us -> none  [shards(): team_signs = lax.all_gather(sign_cols, 'col', axis=0, tiled=True)]
    dot_general x10 -> x0, matrix products: 46.8 us -> none  [the longest x1 17.5 us: sign_columns(): jnp.dot(initial, initial, precision=lax.Precision.HIGHEST, preferred_elem...]
    ppermute x2 -> x20, waiting for transfers between devices: 35.6 us -> 61.4 us  [the longest x6 33.7 us: gather_col(): parts[shift * INNER] = lax.ppermute(shard, 'col', pairs(count, shift, 0))]
    ppermute x2 -> x20, starting transfers between devices: 1.75 us -> 25.7 us  [the longest x6 10.2 us: gather_col(): parts[shift * INNER] = lax.ppermute(shard, 'col', pairs(count, shift, 0))]
    pallas_call x0 -> x4, Pallas kernels: none -> 19.2 us  [the longest x1 15.2 us: sign_rows(): pl.pallas_call(lambda *refs: sign_kernel(count, *refs), out_shape=jax.Sha...]
    reshape x7 -> x1, local copies, waits for them, and re-layouts: 19.7 us -> 0.88 us  [shards(): weights = jnp.broadcast_to(pattern.astype(F32)[:, None, :, None], (patter...]
    another operation x2 -> x0, local copies, waits for them, and re-layouts: 11.3 us -> none
  transfers between devices with their start and end apart: 4 -> 20, of which waited for: 3 -> 11; matrix products, arithmetic and copies ran while one was open for 6% -> 3% of each run, Pallas kernels for 0% -> 1%
where the time goes in v1:
time: 115 us
  waiting for transfers between devices  61.4 us (53%)
  starting transfers between devices  25.7 us (22%)
  Pallas kernels  19.2 us (17%)
  local copies, waits for them, and re-layouts  5.93 us (5%)
  other arithmetic  2.08 us (2%)
    ppermute x6, waiting for transfers between devices, gather_col(): parts[shift * INNER] = lax.ppermute(shard, 'col', pairs(count, shift, 0))  33.7 us
    ppermute x6, waiting for transfers between devices, gather_col(): lax.ppermute(parts[shift * INNER], 'col', pairs(count, 0, 1))  18.7 us
    pallas_call x1, Pallas kernels, sign_rows(): pl.pallas_call(lambda *refs: sign_kernel(count, *refs), out_shape=jax.Sha...  15.2 us
    ppermute x6, starting transfers between devices, gather_col(): parts[shift * INNER] = lax.ppermute(shard, 'col', pairs(count, shift, 0))  10.2 us
    ppermute x6, starting transfers between devices, gather_col(): lax.ppermute(parts[shift * INNER], 'col', pairs(count, 0, 1))  8.32 us
    ppermute x2, waiting for transfers between devices, shards(): lower.append(lax.ppermute(to_up, 'row', up))  5 us
    ppermute x2, starting transfers between devices, shards(): upper.append(lax.ppermute(to_down, 'row', down))  3.47 us
    ppermute x2, waiting for transfers between devices, gather_col(): parts[1] = lax.ppermute(shard, 'col', pairs(count, 0, 1))  3.1 us
  transfers between devices with their start and end apart: 20, of which 11 were waited for; matrix products, arithmetic and copies ran while one was open for 3% of the time, Pallas kernels for 1%

profile of v1, /device:TPU:0, one launch (start us, length us, event | category | flops | bytes accessed | tf_op | source)
XLA Modules:
  0.0 114.6 jit_solution(9651207976705444856)
XLA Ops:
  2.1 5.1 %collective-permute-start.5 = (bf16[1024,128]{1,0:T(8,128)(2,1)S(1)}, bf16[1024,128]{1,0:T(8,128)(2,1)S(1)}, u32[]{:S(2)}, u32[]{:S(2)}) collective-permute-start(bf16[1024,128]{1,0:T(8,128)(2,1)S(1)} %multiply_convert_fusion.refs_5_), channel_id=1, source_target_pairs={{0,6},{1,7},{2,4},{3,5},{4,2},{5,3},{6,0},{7,1},{8,14},{9,15},{10,... | collective-permute-start | bytes 786440 | tf_op jit(solution)/shard_map/ppermute | solution.py:27
  7.9 1.7 %collective-permute-start = (bf16[1024,128]{1,0:T(8,128)(2,1)S(1)}, bf16[1024,128]{1,0:T(8,128)(2,1)S(1)}, u32[]{:S(2)}, u32[]{:S(2)}) collective-permute-start(bf16[1024,128]{1,0:T(8,128)(2,1)S(1)} %multiply_convert_fusion.refs_5_), channel_id=1, source_target_pairs={{0,1},{1,0},{2,3},{3,2},{4,5},{5,4},{6,7},{7,6},{8,9},{9,8},{10,11... | collective-permute-start | bytes 786440 | tf_op jit(solution)/shard_map/ppermute | solution.py:25
  11.0 3.6 %collective-permute-done.5.refs_11_ = bf16[1024,128]{1,0:T(8,128)(2,1)S(1)} collective-permute-done((bf16[1024,128]{1,0:T(8,128)(2,1)S(1)}, bf16[1024,128]{1,0:T(8,128)(2,1)S(1)}, u32[]{:S(2)}, u32[]{:S(2)}) %collective-permute-start.5) | collective-permute-done | bytes 262176 | tf_op jit(solution)/shard_map/ppermute | solution.py:27
  14.5 1.7 %collective-permute-start.6 = (bf16[1024,128]{1,0:T(8,128)(2,1)S(1)}, bf16[1024,128]{1,0:T(8,128)(2,1)S(1)}, u32[]{:S(2)}, u32[]{:S(2)}) collective-permute-start(bf16[1024,128]{1,0:T(8,128)(2,1)S(1)} %collective-permute-done.5.refs_11_), channel_id=1, source_target_pairs={{0,1},{1,0},{2,3},{3,2},{4,5},{5,4},{6,7},{7,6},{8,9},{9,8},{10,11... | collective-permute-start | bytes 786440 | tf_op jit(solution)/shard_map/ppermute | solution.py:29
  16.2 13.3 %collective-permute-done.3.refs_9_ = bf16[1024,128]{1,0:T(8,128)(2,1)S(1)} collective-permute-done((bf16[1024,128]{1,0:T(8,128)(2,1)S(1)}, bf16[1024,128]{1,0:T(8,128)(2,1)S(1)}, u32[]{:S(2)}, u32[]{:S(2)}) %collective-permute-start.3) | collective-permute-done | bytes 262176 | tf_op jit(solution)/shard_map/ppermute | solution.py:27
  29.6 1.5 %collective-permute-start.4 = (bf16[1024,128]{1,0:T(8,128)(2,1)S(1)}, bf16[1024,128]{1,0:T(8,128)(2,1)S(1)}, u32[]{:S(2)}, u32[]{:S(2)}) collective-permute-start(bf16[1024,128]{1,0:T(8,128)(2,1)S(1)} %collective-permute-done.3.refs_9_), channel_id=1, source_target_pairs={{0,1},{1,0},{2,3},{3,2},{4,5},{5,4},{6,7},{7,6},{8,9},{9,8},{10,11... | collective-permute-start | bytes 786440 | tf_op jit(solution)/shard_map/ppermute | solution.py:29
  33.1 5.7 %collective-permute-done.4.refs_10_ = bf16[1024,128]{1,0:T(8,128)(2,1)S(1)} collective-permute-done((bf16[1024,128]{1,0:T(8,128)(2,1)S(1)}, bf16[1024,128]{1,0:T(8,128)(2,1)S(1)}, u32[]{:S(2)}, u32[]{:S(2)}) %collective-permute-start.4) | collective-permute-done | bytes 262176 | tf_op jit(solution)/shard_map/ppermute | solution.py:29
  38.8 3.7 %collective-permute-done.2.refs_8_ = bf16[1024,128]{1,0:T(8,128)(2,1)S(1)} collective-permute-done((bf16[1024,128]{1,0:T(8,128)(2,1)S(1)}, bf16[1024,128]{1,0:T(8,128)(2,1)S(1)}, u32[]{:S(2)}, u32[]{:S(2)}) %collective-permute-start.2) | collective-permute-done | bytes 262176 | tf_op jit(solution)/shard_map/ppermute | solution.py:29
  43.5 15.2 %sign_rows.1.refs_2_ = bf16[128,1024]{1,0:T(8,128)(2,1)} custom-call(s32[1]{0:T(128)} %bitcast.refs_0_, s32[1]{0:T(128)} %dynamic_slice.8.refs_1_, bf16[1024,128]{1,0:T(8,128)(2,1)} %broadcast_in_dim.32.refs_2_, bf16[1,1024]{1,0:T(2,128)(2,1)} %convert_element_type.29.refs_3_, f32[1,1024]{1,0:T(1,128)} %bitcast.11, bf16[1024,128]{1,0:T(8,128)(2,1)} %copy-done.4, ...), custom_call_target="tpu_custom_call" | custom-call | flops 9395240960 | bytes 2097152 | tf_op jit(solution)/shard_map/sign_rows/pallas_call | solution.py:95
  58.7 2.3 %collective-permute-start.12 = (bf16[128,1024]{1,0:T(8,128)(2,1)}, bf16[128,1024]{1,0:T(8,128)(2,1)S(1)}, u32[]{:S(2)}, u32[]{:S(2)}) collective-permute-start(bf16[128,1024]{1,0:T(8,128)(2,1)} %sign_rows.1.refs_2_), channel_id=1, source_target_pairs={{0,6},{1,7},{2,4},{3,5},{4,2},{5,3},{6,0},{7,1},{8,14},{9,15},{10,... | collective-permute-start | bytes 786440 | tf_op jit(solution)/shard_map/ppermute | solution.py:27
  61.1 2.2 %collective-permute-start.8 = (bf16[128,1024]{1,0:T(8,128)(2,1)}, bf16[128,1024]{1,0:T(8,128)(2,1)S(1)}, u32[]{:S(2)}, u32[]{:S(2)}) collective-permute-start(bf16[128,1024]{1,0:T(8,128)(2,1)} %sign_rows.1.refs_2_), channel_id=1, source_target_pairs={{0,2},{1,3},{2,0},{3,1},{4,6},{5,7},{6,4},{7,5},{8,10},{9,11},{10,... | collective-permute-start | bytes 786440 | tf_op jit(solution)/shard_map/ppermute | solution.py:27
  64.7 5.3 %collective-permute-done.12.refs_4_.refs_8_ = bf16[128,1024]{1,0:T(8,128)(2,1)S(1)} collective-permute-done((bf16[128,1024]{1,0:T(8,128)(2,1)}, bf16[128,1024]{1,0:T(8,128)(2,1)S(1)}, u32[]{:S(2)}, u32[]{:S(2)}) %collective-permute-start.12) | collective-permute-done | bytes 262176 | tf_op jit(solution)/shard_map/ppermute | solution.py:27
  70.0 1.5 %collective-permute-start.13 = (bf16[128,1024]{1,0:T(8,128)(2,1)S(1)}, bf16[128,1024]{1,0:T(8,128)(2,1)S(1)}, u32[]{:S(2)}, u32[]{:S(2)}) collective-permute-start(bf16[128,1024]{1,0:T(8,128)(2,1)S(1)} %collective-permute-done.12.refs_4_.refs_8_), channel_id=1, source_target_pairs={{0,1},{1,0},{2,3},{3,2},{4,5},{5,4},{6,7},{7,6},{8,9},{9,8},{10,11... | collective-permute-start | bytes 786440 | tf_op jit(solution)/shard_map/ppermute | solution.py:29
  71.5 11.5 %collective-permute-done.10.refs_2_.refs_6_ = bf16[128,1024]{1,0:T(8,128)(2,1)S(1)} collective-permute-done((bf16[128,1024]{1,0:T(8,128)(2,1)}, bf16[128,1024]{1,0:T(8,128)(2,1)S(1)}, u32[]{:S(2)}, u32[]{:S(2)}) %collective-permute-start.10) | collective-permute-done | bytes 262176 | tf_op jit(solution)/shard_map/ppermute | solution.py:27
  83.1 1.5 %collective-permute-start.11 = (bf16[128,1024]{1,0:T(8,128)(2,1)S(1)}, bf16[128,1024]{1,0:T(8,128)(2,1)S(1)}, u32[]{:S(2)}, u32[]{:S(2)}) collective-permute-start(bf16[128,1024]{1,0:T(8,128)(2,1)S(1)} %collective-permute-done.10.refs_2_.refs_6_), channel_id=1, source_target_pairs={{0,1},{1,0},{2,3},{3,2},{4,5},{5,4},{6,7},{7,6},{8,9},{9,8},{10,11... | collective-permute-start | bytes 786440 | tf_op jit(solution)/shard_map/ppermute | solution.py:29
  85.1 1.5 %collective-permute-start.9 = (bf16[128,1024]{1,0:T(8,128)(2,1)S(1)}, bf16[128,1024]{1,0:T(8,128)(2,1)S(1)}, u32[]{:S(2)}, u32[]{:S(2)}) collective-permute-start(bf16[128,1024]{1,0:T(8,128)(2,1)S(1)} %collective-permute-done.8.refs_4_), channel_id=1, source_target_pairs={{0,1},{1,0},{2,3},{3,2},{4,5},{5,4},{6,7},{7,6},{8,9},{9,8},{10,11... | collective-permute-start | bytes 786440 | tf_op jit(solution)/shard_map/ppermute | solution.py:29
  86.6 5.7 %collective-permute-done.11.refs_3_.refs_7_ = bf16[128,1024]{1,0:T(8,128)(2,1)S(1)} collective-permute-done((bf16[128,1024]{1,0:T(8,128)(2,1)S(1)}, bf16[128,1024]{1,0:T(8,128)(2,1)S(1)}, u32[]{:S(2)}, u32[]{:S(2)}) %collective-permute-start.11) | collective-permute-done | bytes 262176 | tf_op jit(solution)/shard_map/ppermute | solution.py:29
  93.1 1.7 %collective-permute-start.19 = (f32[128,512]{1,0:T(8,128)S(1)}, f32[128,512]{1,0:T(8,128)S(1)}, u32[]{:S(2)}, u32[]{:S(2)}) collective-permute-start(f32[128,512]{1,0:T(8,128)S(1)} %get-tuple-element.12), channel_id=1, source_target_pairs={{8,0},{16,8},{24,16},{0,24},{9,1},{17,9},{25,17},{1,25},{10,2},{18... | collective-permute-start | bytes 786440 | tf_op jit(solution)/shard_map/ppermute | solution.py:217
  94.8 3.1 %collective-permute-done.7.refs_3_ = bf16[128,1024]{1,0:T(8,128)(2,1)S(1)} collective-permute-done((bf16[128,1024]{1,0:T(8,128)(2,1)}, bf16[128,1024]{1,0:T(8,128)(2,1)S(1)}, u32[]{:S(2)}, u32[]{:S(2)}) %collective-permute-start.7) | collective-permute-done | bytes 262176 | tf_op jit(solution)/shard_map/ppermute | solution.py:25
  97.9 3.6 %collective-permute-done.9.refs_5_ = bf16[128,1024]{1,0:T(8,128)(2,1)S(1)} collective-permute-done((bf16[128,1024]{1,0:T(8,128)(2,1)S(1)}, bf16[128,1024]{1,0:T(8,128)(2,1)S(1)}, u32[]{:S(2)}, u32[]{:S(2)}) %collective-permute-start.9) | collective-permute-done | bytes 262176 | tf_op jit(solution)/shard_map/ppermute | solution.py:29
  102.3 1.7 %collective-permute-start.18 = (f32[128,512]{1,0:T(8,128)S(1)}, f32[128,512]{1,0:T(8,128)S(1)}, u32[]{:S(2)}, u32[]{:S(2)}) collective-permute-start(f32[128,512]{1,0:T(8,128)S(1)} %get-tuple-element.11), channel_id=1, source_target_pairs={{8,0},{16,8},{24,16},{0,24},{9,1},{17,9},{25,17},{1,25},{10,2},{18... | collective-permute-start | bytes 786440 | tf_op jit(solution)/shard_map/ppermute | solution.py:217
  104.0 5.0 %collective-permute-done.16.refs_10_ = f32[128,512]{1,0:T(8,128)S(1)} collective-permute-done((f32[128,512]{1,0:T(8,128)S(1)}, f32[128,512]{1,0:T(8,128)S(1)}, u32[]{:S(2)}, u32[]{:S(2)}) %collective-permute-start.16) | collective-permute-done | bytes 262176 | tf_op jit(solution)/shard_map/ppermute | solution.py:216
  109.9 2.6 %final.1 = f32[128,3,1024]{2,1,0:T(4,128)S(1)} custom-call(s32[1]{0:T(128)} %bitcast.refs_0_, bf16[128,1024]{1,0:T(8,128)(2,1)S(1)} %get-tuple-element.14.refs_1_, bf16[128,1024]{1,0:T(8,128)(2,1)S(1)} %copy-done.1, bf16[128,1024]{1,0:T(8,128)(2,1)S(1)} %collective-permute-done.7.refs_3_, bf16[128,1024]{1,0:T(8,128)(2,1)S(1)} %collective-permute-done.8.refs_4_, ...), custom_call_target="tpu_custom_call" | custom-call | flops 268435456 | bytes 2621440 | tf_op jit(solution)/shard_map/final/pallas_call | solution.py:165
  112.5 2.1 %copy.10 = f32[128,3,1024]{2,0,1:T(8,128)} copy(f32[128,3,1024]{2,1,0:T(4,128)S(1)} %final.1) | data formatting | bytes 3145728 | tf_op jit(solution)/shard_map/final/pallas_call | solution.py:165
  (66 shorter events, 11.5 us)
Async XLA Ops:
  1.1 31.3 %copy-start.5 = (f32[1024]{0:T(1024)S(1)}, f32[1024]{0:T(1024)}, u32[]{:S(2)}) copy-start(f32[1024]{0:T(1024)} %param.8) | copy-start | bytes 12292
  2.1 41.3 %copy-start.4 = (bf16[1024,128]{1,0:T(8,128)(2,1)}, bf16[1024,128]{1,0:T(8,128)(2,1)S(1)}, u32[]{:S(2)}) copy-start(bf16[1024,128]{1,0:T(8,128)(2,1)S(1)} %multiply_convert_fusion.refs_5_) | copy-start | bytes 786436
  2.1 12.4 %collective-permute-start.5 = (bf16[1024,128]{1,0:T(8,128)(2,1)S(1)}, bf16[1024,128]{1,0:T(8,128)(2,1)S(1)}, u32[]{:S(2)}, u32[]{:S(2)}) collective-permute-start(bf16[1024,128]{1,0:T(8,128)(2,1)S(1)} %multiply_convert_fusion.refs_5_), channel_id=1, source_target_pairs={{0,6},{1,7},{2,4},{3,5},{4,2},{5,3},{6,0},{7,1},{8,14},{9,15},{10,... | collective-permute-start | bytes 786440 | tf_op jit(solution)/shard_map/ppermute | solution.py:27
  7.2 22.3 %collective-permute-start.3 = (bf16[1024,128]{1,0:T(8,128)(2,1)S(1)}, bf16[1024,128]{1,0:T(8,128)(2,1)S(1)}, u32[]{:S(2)}, u32[]{:S(2)}) collective-permute-start(bf16[1024,128]{1,0:T(8,128)(2,1)S(1)} %multiply_convert_fusion.refs_5_), channel_id=1, source_target_pairs={{0,4},{1,5},{2,6},{3,7},{4,0},{5,1},{6,2},{7,3},{8,12},{9,13},{10,... | collective-permute-start | bytes 786440 | tf_op jit(solution)/shard_map/ppermute | solution.py:27
  7.2 23.8 %collective-permute-start.1 = (bf16[1024,128]{1,0:T(8,128)(2,1)S(1)}, bf16[1024,128]{1,0:T(8,128)(2,1)S(1)}, u32[]{:S(2)}, u32[]{:S(2)}) collective-permute-start(bf16[1024,128]{1,0:T(8,128)(2,1)S(1)} %multiply_convert_fusion.refs_5_), channel_id=1, source_target_pairs={{0,2},{1,3},{2,0},{3,1},{4,6},{5,7},{6,4},{7,5},{8,10},{9,11},{10,... | collective-permute-start | bytes 786440 | tf_op jit(solution)/shard_map/ppermute | solution.py:27
  7.9 25.2 %collective-permute-start = (bf16[1024,128]{1,0:T(8,128)(2,1)S(1)}, bf16[1024,128]{1,0:T(8,128)(2,1)S(1)}, u32[]{:S(2)}, u32[]{:S(2)}) collective-permute-start(bf16[1024,128]{1,0:T(8,128)(2,1)S(1)} %multiply_convert_fusion.refs_5_), channel_id=1, source_target_pairs={{0,1},{1,0},{2,3},{3,2},{4,5},{5,4},{6,7},{7,6},{8,9},{9,8},{10,11... | collective-permute-start | bytes 786440 | tf_op jit(solution)/shard_map/ppermute | solution.py:25
  14.5 28.9 %copy-start.6 = (bf16[1024,128]{1,0:T(8,128)(2,1)}, bf16[1024,128]{1,0:T(8,128)(2,1)S(1)}, u32[]{:S(2)}) copy-start(bf16[1024,128]{1,0:T(8,128)(2,1)S(1)} %collective-permute-done.5.refs_11_) | copy-start | bytes 786436
  14.5 18.6 %collective-permute-start.6 = (bf16[1024,128]{1,0:T(8,128)(2,1)S(1)}, bf16[1024,128]{1,0:T(8,128)(2,1)S(1)}, u32[]{:S(2)}, u32[]{:S(2)}) collective-permute-start(bf16[1024,128]{1,0:T(8,128)(2,1)S(1)} %collective-permute-done.5.refs_11_), channel_id=1, source_target_pairs={{0,1},{1,0},{2,3},{3,2},{4,5},{5,4},{6,7},{7,6},{8,9},{9,8},{10,11... | collective-permute-start | bytes 786440 | tf_op jit(solution)/shard_map/ppermute | solution.py:29
  29.6 9.2 %collective-permute-start.4 = (bf16[1024,128]{1,0:T(8,128)(2,1)S(1)}, bf16[1024,128]{1,0:T(8,128)(2,1)S(1)}, u32[]{:S(2)}, u32[]{:S(2)}) collective-permute-start(bf16[1024,128]{1,0:T(8,128)(2,1)S(1)} %collective-permute-done.3.refs_9_), channel_id=1, source_target_pairs={{0,1},{1,0},{2,3},{3,2},{4,5},{5,4},{6,7},{7,6},{8,9},{9,8},{10,11... | collective-permute-start | bytes 786440 | tf_op jit(solution)/shard_map/ppermute | solution.py:29
  31.1 11.5 %collective-permute-start.2 = (bf16[1024,128]{1,0:T(8,128)(2,1)S(1)}, bf16[1024,128]{1,0:T(8,128)(2,1)S(1)}, u32[]{:S(2)}, u32[]{:S(2)}) collective-permute-start(bf16[1024,128]{1,0:T(8,128)(2,1)S(1)} %collective-permute-done.1.refs_7_), channel_id=1, source_target_pairs={{0,1},{1,0},{2,3},{3,2},{4,5},{5,4},{6,7},{7,6},{8,9},{9,8},{10,11... | collective-permute-start | bytes 786440 | tf_op jit(solution)/shard_map/ppermute | solution.py:29
  58.7 42.8 %copy-start.1 = (bf16[128,1024]{1,0:T(8,128)(2,1)S(1)}, bf16[128,1024]{1,0:T(8,128)(2,1)}, u32[]{:S(2)}) copy-start(bf16[128,1024]{1,0:T(8,128)(2,1)} %sign_rows.1.refs_2_) | copy-start | bytes 786436
  58.7 11.3 %collective-permute-start.12 = (bf16[128,1024]{1,0:T(8,128)(2,1)}, bf16[128,1024]{1,0:T(8,128)(2,1)S(1)}, u32[]{:S(2)}, u32[]{:S(2)}) collective-permute-start(bf16[128,1024]{1,0:T(8,128)(2,1)} %sign_rows.1.refs_2_), channel_id=1, source_target_pairs={{0,6},{1,7},{2,4},{3,5},{4,2},{5,3},{6,0},{7,1},{8,14},{9,15},{10,... | collective-permute-start | bytes 786440 | tf_op jit(solution)/shard_map/ppermute | solution.py:27
  61.0 22.1 %collective-permute-start.10 = (bf16[128,1024]{1,0:T(8,128)(2,1)}, bf16[128,1024]{1,0:T(8,128)(2,1)S(1)}, u32[]{:S(2)}, u32[]{:S(2)}) collective-permute-start(bf16[128,1024]{1,0:T(8,128)(2,1)} %sign_rows.1.refs_2_), channel_id=1, source_target_pairs={{0,4},{1,5},{2,6},{3,7},{4,0},{5,1},{6,2},{7,3},{8,12},{9,13},{10,... | collective-permute-start | bytes 786440 | tf_op jit(solution)/shard_map/ppermute | solution.py:27
  61.1 23.5 %collective-permute-start.15 = (bf16[128,1024]{1,0:T(8,128)(2,1)S(1)}, bf16[128,1024]{1,0:T(8,128)(2,1)S(1)}, u32[]{:S(2)}, u32[]{:S(2)}) collective-permute-start(bf16[128,1024]{1,0:T(8,128)(2,1)S(1)} %get-tuple-element.13), channel_id=1, source_target_pairs={{0,8},{8,16},{16,24},{24,0},{1,9},{9,17},{17,25},{25,1},{2,10},{10... | collective-permute-start | bytes 786440 | tf_op jit(solution)/shard_map/ppermute | solution.py:196
  61.1 24.0 %collective-permute-start.8 = (bf16[128,1024]{1,0:T(8,128)(2,1)}, bf16[128,1024]{1,0:T(8,128)(2,1)S(1)}, u32[]{:S(2)}, u32[]{:S(2)}) collective-permute-start(bf16[128,1024]{1,0:T(8,128)(2,1)} %sign_rows.1.refs_2_), channel_id=1, source_target_pairs={{0,2},{1,3},{2,0},{3,1},{4,6},{5,7},{6,4},{7,5},{8,10},{9,11},{10,... | collective-permute-start | bytes 786440 | tf_op jit(solution)/shard_map/ppermute | solution.py:27
  63.3 23.3 %collective-permute-start.14 = (bf16[128,1024]{1,0:T(8,128)(2,1)S(1)}, bf16[128,1024]{1,0:T(8,128)(2,1)S(1)}, u32[]{:S(2)}, u32[]{:S(2)}) collective-permute-start(bf16[128,1024]{1,0:T(8,128)(2,1)S(1)} %get-tuple-element.15), channel_id=1, source_target_pairs={{8,0},{16,8},{24,16},{0,24},{9,1},{17,9},{25,17},{1,25},{10,2},{18... | collective-permute-start | bytes 786440 | tf_op jit(solution)/shard_map/ppermute | solution.py:195
  70.0 16.6 %collective-permute-start.13 = (bf16[128,1024]{1,0:T(8,128)(2,1)S(1)}, bf16[128,1024]{1,0:T(8,128)(2,1)S(1)}, u32[]{:S(2)}, u32[]{:S(2)}) collective-permute-start(bf16[128,1024]{1,0:T(8,128)(2,1)S(1)} %collective-permute-done.12.refs_4_.refs_8_), channel_id=1, source_target_pairs={{0,1},{1,0},{2,3},{3,2},{4,5},{5,4},{6,7},{7,6},{8,9},{9,8},{10,11... | collective-permute-start | bytes 786440 | tf_op jit(solution)/shard_map/ppermute | solution.py:29
  83.1 9.2 %collective-permute-start.11 = (bf16[128,1024]{1,0:T(8,128)(2,1)S(1)}, bf16[128,1024]{1,0:T(8,128)(2,1)S(1)}, u32[]{:S(2)}, u32[]{:S(2)}) collective-permute-start(bf16[128,1024]{1,0:T(8,128)(2,1)S(1)} %collective-permute-done.10.refs_2_.refs_6_), channel_id=1, source_target_pairs={{0,1},{1,0},{2,3},{3,2},{4,5},{5,4},{6,7},{7,6},{8,9},{9,8},{10,11... | collective-permute-start | bytes 786440 | tf_op jit(solution)/shard_map/ppermute | solution.py:29
  84.6 13.3 %collective-permute-start.7 = (bf16[128,1024]{1,0:T(8,128)(2,1)}, bf16[128,1024]{1,0:T(8,128)(2,1)S(1)}, u32[]{:S(2)}, u32[]{:S(2)}) collective-permute-start(bf16[128,1024]{1,0:T(8,128)(2,1)} %sign_rows.1.refs_2_), channel_id=1, source_target_pairs={{0,1},{1,0},{2,3},{3,2},{4,5},{5,4},{6,7},{7,6},{8,9},{9,8},{10,11... | collective-permute-start | bytes 786440 | tf_op jit(solution)/shard_map/ppermute | solution.py:25
  85.1 16.4 %collective-permute-start.9 = (bf16[128,1024]{1,0:T(8,128)(2,1)S(1)}, bf16[128,1024]{1,0:T(8,128)(2,1)S(1)}, u32[]{:S(2)}, u32[]{:S(2)}) collective-permute-start(bf16[128,1024]{1,0:T(8,128)(2,1)S(1)} %collective-permute-done.8.refs_4_), channel_id=1, source_target_pairs={{0,1},{1,0},{2,3},{3,2},{4,5},{5,4},{6,7},{7,6},{8,9},{9,8},{10,11... | collective-permute-start | bytes 786440 | tf_op jit(solution)/shard_map/ppermute | solution.py:29
  93.0 11.0 %collective-permute-start.17 = (f32[128,512]{1,0:T(8,128)S(1)}, f32[128,512]{1,0:T(8,128)S(1)}, u32[]{:S(2)}, u32[]{:S(2)}) collective-permute-start(f32[128,512]{1,0:T(8,128)S(1)} %get-tuple-element.10), channel_id=1, source_target_pairs={{0,8},{8,16},{16,24},{24,0},{1,9},{9,17},{17,25},{25,1},{2,10},{10... | collective-permute-start | bytes 786440 | tf_op jit(solution)/shard_map/ppermute | solution.py:216
  93.1 10.9 %collective-permute-start.19 = (f32[128,512]{1,0:T(8,128)S(1)}, f32[128,512]{1,0:T(8,128)S(1)}, u32[]{:S(2)}, u32[]{:S(2)}) collective-permute-start(f32[128,512]{1,0:T(8,128)S(1)} %get-tuple-element.12), channel_id=1, source_target_pairs={{8,0},{16,8},{24,16},{0,24},{9,1},{17,9},{25,17},{1,25},{10,2},{18... | collective-permute-start | bytes 786440 | tf_op jit(solution)/shard_map/ppermute | solution.py:217
  102.2 6.8 %collective-permute-start.16 = (f32[128,512]{1,0:T(8,128)S(1)}, f32[128,512]{1,0:T(8,128)S(1)}, u32[]{:S(2)}, u32[]{:S(2)}) collective-permute-start(f32[128,512]{1,0:T(8,128)S(1)} %get-tuple-element.9), channel_id=1, source_target_pairs={{0,8},{8,16},{16,24},{24,0},{1,9},{9,17},{17,25},{25,1},{2,10},{10... | collective-permute-start | bytes 786440 | tf_op jit(solution)/shard_map/ppermute | solution.py:216
  102.3 7.6 %collective-permute-start.18 = (f32[128,512]{1,0:T(8,128)S(1)}, f32[128,512]{1,0:T(8,128)S(1)}, u32[]{:S(2)}, u32[]{:S(2)}) collective-permute-start(f32[128,512]{1,0:T(8,128)S(1)} %get-tuple-element.11), channel_id=1, source_target_pairs={{8,0},{16,8},{24,16},{0,24},{9,1},{17,9},{25,17},{1,25},{10,2},{18... | collective-permute-start | bytes 786440 | tf_op jit(solution)/shard_map/ppermute | solution.py:217
  (10 other events, 89.4 us)

commit v2 on v1

v2 whole, which is shorter than its diff:
```python
import jax
import jax.numpy as jnp
from jax import lax
from jax.experimental import pallas as pl
from jax.experimental.pallas import tpu as pltpu
from jax.sharding import PartitionSpec as P

BLOCK = 32
OWN_BLOCKS = 4
AXES = ("row", "col")
F32 = jnp.float32
BF16 = jnp.bfloat16
LAST = (((1,), (1,)), ((), ()))
VMEM = pl.BlockSpec(memory_space=pltpu.VMEM)
SMEM = pl.BlockSpec(memory_space=pltpu.SMEM)


class Place:
    def __init__(self):
        self.rows = lax.axis_size("row")
        self.cols = lax.axis_size("col")
        self.half = self.cols // 2
        self.devices = [(r, c) for r in range(self.rows) for c in range(self.cols)]

    def work(self, row, col):
        upper = col // self.half
        return (row - row % 2 + upper, col ^ ((row % 2 ^ upper) * self.half))

    def send(self, array, target):
        moves = []
        for row, col in self.devices:
            to_row, to_col = target(row, col)
            moves.append((row * self.cols + col, to_row % self.rows * self.cols + to_col))
        return lax.ppermute(array, AXES, moves)


def prepare_kernel(ham_ref, pattern_ref, out_ref):
    across, blocks = pattern_ref.shape
    width = out_ref.shape[1]
    lane = lax.broadcasted_iota(jnp.int32, (across, width), 1) // BLOCK
    spread = (lane == lax.broadcasted_iota(jnp.int32, (across, width), 0)).astype(F32)
    weights = lax.dot_general(
        pattern_ref[...].astype(F32), spread, (((0,), (0,)), ((), ())), preferred_element_type=F32
    )
    for a in range(blocks):
        rows = slice(a * BLOCK, (a + 1) * BLOCK)
        out_ref[rows, :] = (ham_ref[rows, :] * weights[a : a + 1, :]).astype(BF16)


def prepare(hamiltonian, pattern):
    return pl.pallas_call(
        prepare_kernel,
        out_shape=jax.ShapeDtypeStruct(hamiltonian.shape, BF16),
        in_specs=[VMEM, VMEM],
        out_specs=VMEM,
        name="prepare",
    )(hamiltonian, pattern.T)


def sign_kernel(count, slot_ref, active_ref, mask_row, diag_row, *refs):
    shards = refs[:count]
    out_ref, ham = refs[count:]
    width = ham.shape[0]
    own = out_ref.shape[0]
    slot = slot_ref[0]
    squares = jnp.zeros((1, own), F32)
    rows = lax.broadcasted_iota(jnp.int32, (own, own), 0)
    cols = lax.broadcasted_iota(jnp.int32, (own, own), 1)
    eye = rows == cols
    mask_col = jnp.broadcast_to(mask_row[...], (own, width)).T.astype(BF16)
    for k in range(count):
        start = pl.multiple_of((slot ^ k) * own, own)
        block = shards[k][...] * mask_col * mask_row[:, pl.ds(start, own)].astype(BF16)
        ham[:, pl.ds(start, own)] = block
        wide = block.astype(F32)
        squares += 0.5 * jnp.sum(wide * wide, axis=0, keepdims=True)
    for k in range(count):
        start = k * own
        diag = diag_row[:, start : start + own]
        across = ham[start : start + own, :]
        down = ham[:, start : start + own]
        both = jnp.dot(across, down, preferred_element_type=F32)
        here = ham[start : start + own, start : start + own].astype(F32)
        entries = 0.5 * both + 2.0 * diag * here
        squares += jnp.sum(jnp.where(eye, entries, 0.0), axis=0, keepdims=True)
        squares += diag * diag
    total = jnp.sum(squares, axis=1, keepdims=True)
    active_rows = active_ref[0].astype(F32) * BLOCK
    factor = jnp.sqrt(active_rows / (4.0 * (total + 1e-06)))
    diag_all = diag_row[...]

    def times(panel):
        high = panel.astype(BF16)
        low = (panel - high.astype(F32)).astype(BF16)
        stacked = jnp.concatenate([high, low], axis=0)
        prod = jnp.dot(stacked, ham[...], preferred_element_type=F32)
        prod += lax.dot_general(stacked, ham[...], LAST, preferred_element_type=F32)
        return factor * (0.5 * (prod[:own] + prod[own:]) + diag_all * panel)

    def cubic(panel):
        return 0.5 * (3.0 * panel - times(times(panel)))

    start = pl.multiple_of(slot * own, own)
    turned = lax.dot_general(
        eye.astype(BF16), ham[:, pl.ds(start, own)], LAST, preferred_element_type=F32
    )
    across = ham[pl.ds(start, own), :].astype(F32)
    wide_rows = lax.broadcasted_iota(jnp.int32, (own, width), 0)
    wide_cols = lax.broadcasted_iota(jnp.int32, (own, width), 1)
    on_diag = wide_cols == wide_rows + start
    first = 0.5 * (turned + across) + jnp.where(on_diag, diag_all, 0.0)
    left = cubic(factor * first)
    inner = lax.fori_loop(0, 2, lambda _, panel: cubic(times(panel)), left, unroll=count <= 8)
    out_ref[...] = (0.5 * (3.0 * left - inner)).astype(BF16)


def sign_rows(shards, slot, active, mask_row, diag_row):
    count = len(shards)
    width, own = shards[0].shape
    return pl.pallas_call(
        lambda *refs: sign_kernel(count, *refs),
        out_shape=jax.ShapeDtypeStruct((own, width), BF16),
        in_specs=[SMEM, SMEM] + [VMEM] * (2 + count),
        out_specs=VMEM,
        scratch_shapes=[pltpu.VMEM((width, width), BF16)],
        compiler_params=pltpu.CompilerParams(vmem_limit_bytes=8 * 2**20 + 11 * width * width),
        cost_estimate=pl.CostEstimate(
            flops=70 * own * width * width, bytes_accessed=2 * width * width, transcendentals=0
        ),
        name="sign_rows",
    )(slot, active, mask_row[None], diag_row[None], *shards)


def products_kernel(count, sides, *refs):
    signs, outs = refs[2 : 2 + count], refs[2 + count :]
    own = signs[0].shape[0]
    for k in range(count):
        cols = slice(k * own, (k + 1) * own)
        for j in range(2):
            prod = lax.dot_general(refs[j][...], signs[k][...], LAST, preferred_element_type=F32)
            for side in range(sides):
                outs[j * sides + side][:, cols] = prod[side * own : (side + 1) * own]


def products(trio, mates, signs):
    count = len(signs)
    own, width = signs[0].shape
    sides = trio.shape[0] // own
    shape = jax.ShapeDtypeStruct((own, count * own), F32)
    return pl.pallas_call(
        lambda *refs: products_kernel(count, sides, *refs),
        out_shape=[shape] * (2 * sides),
        in_specs=[VMEM] * (2 + count),
        out_specs=[VMEM] * (2 * sides),
        compiler_params=pltpu.CompilerParams(vmem_limit_bytes=24 * 2**20),
        cost_estimate=pl.CostEstimate(
            flops=4 * sides * own * width * own * count,
            bytes_accessed=2 * width * own * (2 * sides + count),
            transcendentals=0,
        ),
        name="products",
    )(trio, mates, *signs)


def final_kernel(groups, own, slot_ref, *refs):
    out_ref = refs[-1]
    at = 0
    for steps in groups:
        for side in range(3):
            for mate in range(2):
                part = refs[at]
                at += 1
                for k, step in enumerate(steps):
                    start = pl.multiple_of((slot_ref[0] ^ (step + mate)) * own, own)
                    out_ref[side, :, pl.ds(start, own)] = part[:, k * own : (k + 1) * own]


def final(slot, groups, parts, width):
    flat = [p for part in parts for side in part for p in side]
    own = flat[0].shape[0]
    return pl.pallas_call(
        lambda *refs: final_kernel(groups, own, *refs),
        out_shape=jax.ShapeDtypeStruct((3, own, width), F32),
        in_specs=[SMEM] + [VMEM] * len(flat),
        out_specs=VMEM,
        compiler_params=pltpu.CompilerParams(vmem_limit_bytes=24 * 2**20),
        cost_estimate=pl.CostEstimate(
            flops=0, bytes_accessed=24 * own * width, transcendentals=0
        ),
        name="final",
    )(slot, *flat)


def shards(hamiltonian, pattern, onsite, members, orders, intersection_inv):
    place = Place()
    cols, half = place.cols, place.half
    row, col = lax.axis_index("row"), lax.axis_index("col")
    team, slot = place.work(row, col)
    team_blocks = cols * OWN_BLOCKS
    send = place.send

    def home(r, c):
        return (r, c) if c // half == r % 2 else (r ^ 1, c ^ half)

    masked = prepare(hamiltonian, pattern)
    held = send(masked, home)
    parts = [held]
    for step in range(1, half):
        parts.append(send(held, lambda r, c, step=step: (r, c ^ step)))

    invs = intersection_inv.transpose(1, 0, 2)
    above = send(invs[0], lambda r, c: (r - 1, c))
    below = send(invs[2], lambda r, c: (r + 1, c))

    group = team * cols + slot
    group_members = lax.dynamic_index_in_dim(members, group, 0, keepdims=False)
    group_order = lax.dynamic_index_in_dim(orders, group, 0, keepdims=False)
    chosen = (group_members[None, :] == jnp.arange(team_blocks, dtype=jnp.int32)[:, None]) & (
        jnp.arange(members.shape[1])[None, :] < group_order
    )
    mask_row = jnp.repeat(jnp.any(chosen, axis=1).astype(F32), BLOCK)
    diag_row = onsite_of(onsite, place, team, row) * mask_row
    parts, mask_row, diag_row, above, below = lax.optimization_barrier(
        (parts, mask_row, diag_row, above, below)
    )
    trio = jnp.concatenate([above, invs[1], below], axis=0)
    mates = send(trio, lambda r, c: (r, c ^ 1))
    parts += [send(part, lambda r, c: (r ^ 1, c)) for part in parts]
    signs = sign_rows(
        parts, slot.astype(jnp.int32)[None], group_order[None], mask_row, diag_row
    )

    mine = []
    for step in range(0, cols, 2):

        def target(r, c, step=step):
            team, slot = place.work(r, c)
            return (team, slot ^ step)

        mine.append(send(signs, target))
    order = sorted(range(half), key=lambda k: k % 2)
    groups, placed = [], []
    for chosen_steps in (order[: half // 2], order[half // 2 :]):
        groups.append([2 * k for k in chosen_steps])
        out = products(trio, mates, [mine[k] for k in chosen_steps])
        placed.append(
            [
                [
                    send(out[0], lambda r, c: (r + 1, c)),
                    send(out[3], lambda r, c: (r + 1, c ^ 1)),
                ],
                [out[1], send(out[4], lambda r, c: (r, c ^ 1))],
                [
                    send(out[2], lambda r, c: (r - 1, c)),
                    send(out[5], lambda r, c: (r - 1, c ^ 1)),
                ],
            ]
        )
    width = cols * hamiltonian.shape[1]
    result = final(col.astype(jnp.int32)[None], groups, placed, width)
    return result.transpose(1, 0, 2)


def onsite_of(onsite, place, team, row):
    other = place.send(onsite, lambda r, c: (r ^ 1, c))
    return jnp.where(team == row, onsite, other)


def solution(mesh):
    in_specs = (P("row", "col"), P("row", "col"), P("row"), P(), P(), P(("row", "col"), None, None))
    out_specs = P(("row", "col"), None, None)
    return jax.shard_map(shards, mesh=mesh, in_specs=in_specs, out_specs=out_specs, check_vma=False)
```

time: 115 us -> 86.3 us (0.75)
  waiting for transfers between devices: 61.4 us -> 26.6 us
  starting transfers between devices: 25.7 us -> 39.3 us
  local copies, waits for them, and re-layouts: 5.93 us -> 1.99 us
  Pallas kernels: 19.2 us -> 17.2 us
  other arithmetic: 2.08 us -> 0.87 us
    ppermute x20 -> x26, waiting for transfers between devices: 61.4 us -> 26.6 us  [send(): return lax.ppermute(array, AXES, moves)]
    ppermute x20 -> x26, starting transfers between devices: 25.7 us -> 39.3 us  [send(): return lax.ppermute(array, AXES, moves)]
    pallas_call x1, Pallas kernels: 15.2 us -> 12 us  [sign_rows(): pl.pallas_call(lambda *refs: sign_kernel(count, *refs), out_shape=jax.Sha...]
    pallas_call x1 -> x0, local copies, waits for them, and re-layouts: 2.06 us -> none  [final(): pl.pallas_call(lambda *refs: final_kernel(count, len(lower), *refs), out_...]
    broadcast_in_dim x3 -> x0, local copies, waits for them, and re-layouts: 1.31 us -> none  [the longest x2 0.98 us: sign_rows(): mask_col = jnp.broadcast_to(mask_row[:, None], (width, own)).astype(BF16)]
    pallas_call x3 -> x4, Pallas kernels: 4.01 us -> 5.22 us  [the longest x1 1.96 us: prepare(): pl.pallas_call(prepare_kernel, out_shape=jax.ShapeDtypeStruct(hamiltonian...]
  transfers between devices with their start and end apart: 20 -> 26, of which waited for: 11 -> 12; matrix products, arithmetic and copies ran while one was open for 3% -> 3% of each run, Pallas kernels for 1% -> 18%
where the time goes in v2:
time: 86.3 us; the launch traced here: 86 us
  starting transfers between devices  39.3 us (46%)
  waiting for transfers between devices  26.6 us (31%)
  Pallas kernels  17.2 us (20%)
  local copies, waits for them, and re-layouts  1.99 us (2%)
  other arithmetic  0.87 us (1%)
    ppermute x26, starting transfers between devices, send(): return lax.ppermute(array, AXES, moves)  39.3 us
    ppermute x26, waiting for transfers between devices, send(): return lax.ppermute(array, AXES, moves)  26.6 us
    pallas_call x1, Pallas kernels, sign_rows(): pl.pallas_call(lambda *refs: sign_kernel(count, *refs), out_shape=jax.Sha...  12 us
    pallas_call x1, Pallas kernels, prepare(): pl.pallas_call(prepare_kernel, out_shape=jax.ShapeDtypeStruct(hamiltonian...  1.96 us
    pallas_call x2, Pallas kernels, products(): pl.pallas_call(lambda *refs: products_kernel(count, sides, *refs), out_sh...  1.92 us
  transfers between devices with their start and end apart: 26, of which 12 were waited for; matrix products, arithmetic and copies ran while one was open for 3% of the time, Pallas kernels for 18%

profile of v2, /device:TPU:0, one launch (start us, length us, event | category | flops | bytes accessed | tf_op | source)
XLA Modules:
  0.0 86.0 jit_solution(9368867193726539496)
XLA Ops:
  0.5 2.0 %prepare.1 = bf16[1024,128]{1,0:T(8,128)(2,1)} custom-call(f32[1024,128]{1,0:T(8,128)} %ham_ref.1, s32[4,32]{1,0:T(4,128)} %bitcast.19), custom_call_target="tpu_custom_call" | custom-call | tf_op jit(solution)/shard_map/prepare/pallas_call | solution.py:51
  2.5 1.6 %collective-permute-start = (bf16[1024,128]{1,0:T(8,128)(2,1)}, bf16[1024,128]{1,0:T(8,128)(2,1)S(1)}, u32[]{:S(2)}, u32[]{:S(2)}) collective-permute-start(bf16[1024,128]{1,0:T(8,128)(2,1)} %prepare.1), channel_id=1, source_target_pairs={{0,0},{1,1},{2,2},{3,3},{4,8},{5,9},{6,10},{7,11},{8,4},{9,5},{10,... | collective-permute-start | bytes 786440 | tf_op jit(solution)/shard_map/ppermute | solution.py:34
  4.1 1.2 %slice_bitcast_fusion = (bf16[128,1024]{1,0:T(8,128)(2,1)S(1)}, bf16[128,1024]{1,0:T(8,128)(2,1)S(1)}, bf16[128,1024]{1,0:T(8,128)(2,1)S(1)}) fusion(bf16[3,128,1024]{2,1,0:T(8,128)(2,1)} %bitcast.18), kind=kLoop, calls=%fused_computation.1 | loop fusion | bytes 1572864 | tf_op jit(solution)/shard_map/squeeze | solution.py:226
  5.2 5.2 %collective-permute-start.5 = (bf16[128,1024]{1,0:T(8,128)(2,1)S(1)}, bf16[128,1024]{1,0:T(8,128)(2,1)S(1)}, u32[]{:S(2)}, u32[]{:S(2)}) collective-permute-start(bf16[128,1024]{1,0:T(8,128)(2,1)S(1)} %get-tuple-element.47), channel_id=1, source_target_pairs={{0,24},{1,25},{2,26},{3,27},{4,28},{5,29},{6,30},{7,31},{8,0},{9,1... | collective-permute-start | bytes 786440 | tf_op jit(solution)/shard_map/ppermute | solution.py:34
  11.8 1.6 %collective-permute-start.1 = (bf16[1024,128]{1,0:T(8,128)(2,1)S(1)}, bf16[1024,128]{1,0:T(8,128)(2,1)S(1)}, u32[]{:S(2)}, u32[]{:S(2)}) collective-permute-start(bf16[1024,128]{1,0:T(8,128)(2,1)S(1)} %collective-permute-done.refs_4_), channel_id=1, source_target_pairs={{0,1},{1,0},{2,3},{3,2},{4,5},{5,4},{6,7},{7,6},{8,9},{9,8},{10,11... | collective-permute-start | bytes 786440 | tf_op jit(solution)/shard_map/ppermute | solution.py:34
  13.4 1.6 %collective-permute-start.2 = (bf16[1024,128]{1,0:T(8,128)(2,1)S(1)}, bf16[1024,128]{1,0:T(8,128)(2,1)S(1)}, u32[]{:S(2)}, u32[]{:S(2)}) collective-permute-start(bf16[1024,128]{1,0:T(8,128)(2,1)S(1)} %collective-permute-done.refs_4_), channel_id=1, source_target_pairs={{0,2},{1,3},{2,0},{3,1},{4,6},{5,7},{6,4},{7,5},{8,10},{9,11},{10,... | collective-permute-start | bytes 786440 | tf_op jit(solution)/shard_map/ppermute | solution.py:34
  15.7 1.4 %collective-permute-done.5 = bf16[128,1024]{1,0:T(8,128)(2,1)S(1)} collective-permute-done((bf16[128,1024]{1,0:T(8,128)(2,1)S(1)}, bf16[128,1024]{1,0:T(8,128)(2,1)S(1)}, u32[]{:S(2)}, u32[]{:S(2)}) %collective-permute-start.5) | collective-permute-done | bytes 262176 | tf_op jit(solution)/shard_map/ppermute | solution.py:34
  18.5 1.8 %collective-permute-done.2.refs_6_ = bf16[1024,128]{1,0:T(8,128)(2,1)S(1)} collective-permute-done((bf16[1024,128]{1,0:T(8,128)(2,1)S(1)}, bf16[1024,128]{1,0:T(8,128)(2,1)S(1)}, u32[]{:S(2)}, u32[]{:S(2)}) %collective-permute-start.2) | collective-permute-done | bytes 262176 | tf_op jit(solution)/shard_map/ppermute | solution.py:34
  20.4 5.6 %collective-permute-done.3.refs_7_ = bf16[1024,128]{1,0:T(8,128)(2,1)S(1)} collective-permute-done((bf16[1024,128]{1,0:T(8,128)(2,1)S(1)}, bf16[1024,128]{1,0:T(8,128)(2,1)S(1)}, u32[]{:S(2)}, u32[]{:S(2)}) %collective-permute-start.3) | collective-permute-done | bytes 262176 | tf_op jit(solution)/shard_map/ppermute | solution.py:34
  26.0 2.0 %collective-permute-start.10 = (bf16[1024,128]{1,0:T(8,128)(2,1)S(1)}, bf16[1024,128]{1,0:T(8,128)(2,1)S(1)}, u32[]{:S(2)}, u32[]{:S(2)}) collective-permute-start(bf16[1024,128]{1,0:T(8,128)(2,1)S(1)} %collective-permute-done.2.refs_6_), channel_id=1, source_target_pairs={{0,8},{1,9},{2,10},{3,11},{4,12},{5,13},{6,14},{7,15},{8,0},{9,1},... | collective-permute-start | bytes 786440 | tf_op jit(solution)/shard_map/ppermute | solution.py:34
  28.6 1.6 %collective-permute-start.7 = (bf16[384,1024]{1,0:T(8,128)(2,1)S(1)}, bf16[384,1024]{1,0:T(8,128)(2,1)S(1)}, u32[]{:S(2)}, u32[]{:S(2)}) collective-permute-start(bf16[384,1024]{1,0:T(8,128)(2,1)S(1)} %pad_maximum_fusion.refs_0_), channel_id=1, source_target_pairs={{0,1},{1,0},{2,3},{3,2},{4,5},{5,4},{6,7},{7,6},{8,9},{9,8},{10,11... | collective-permute-start | bytes 2359304 | tf_op jit(solution)/shard_map/ppermute | solution.py:34
  30.3 12.0 %sign_rows.1 = bf16[128,1024]{1,0:T(8,128)(2,1)S(1)} custom-call(s32[1]{0:T(128)} %bitcast.8.refs_0_, s32[1]{0:T(128)} %dynamic_slice.9.refs_1_, f32[1,1024]{1,0:T(1,128)S(1)} %bitcast.16, f32[1,1024]{1,0:T(1,128)S(1)} %bitcast.17, bf16[1024,128]{1,0:T(8,128)(2,1)S(1)} %collective-permute-done.refs_4_, bf16[1024,128]{1,0:T(8,128)(2,1)S(1)} %collective-permute-done.1.refs_5_, ...), custom_call_target="tpu_custom_call" | custom-call | flops 9395240960 | bytes 2097152 | tf_op jit(solution)/shard_map/sign_rows/pallas_call | solution.py:120
  42.3 1.7 %collective-permute-start.19 = (bf16[128,1024]{1,0:T(8,128)(2,1)S(1)}, bf16[128,1024]{1,0:T(8,128)(2,1)S(1)}, u32[]{:S(2)}, u32[]{:S(2)}) collective-permute-start(bf16[128,1024]{1,0:T(8,128)(2,1)S(1)} %sign_rows.1), channel_id=1, source_target_pairs={{0,2},{1,3},{2,0},{3,1},{4,10},{5,11},{6,8},{7,9},{8,6},{9,7},{10,... | collective-permute-start | bytes 786440 | tf_op jit(solution)/shard_map/ppermute | solution.py:34
  43.9 2.2 %collective-permute-start.20 = (bf16[128,1024]{1,0:T(8,128)(2,1)S(1)}, bf16[128,1024]{1,0:T(8,128)(2,1)S(1)}, u32[]{:S(2)}, u32[]{:S(2)}) collective-permute-start(bf16[128,1024]{1,0:T(8,128)(2,1)S(1)} %sign_rows.1), channel_id=1, source_target_pairs={{0,6},{1,7},{2,4},{3,5},{4,14},{5,15},{6,12},{7,13},{8,2},{9,3},{1... | collective-permute-start | bytes 786440 | tf_op jit(solution)/shard_map/ppermute | solution.py:34
  46.8 3.4 %collective-permute-start.13 = (bf16[128,1024]{1,0:T(8,128)(2,1)S(1)}, bf16[128,1024]{1,0:T(8,128)(2,1)S(1)}, u32[]{:S(2)}, u32[]{:S(2)}) collective-permute-start(bf16[128,1024]{1,0:T(8,128)(2,1)S(1)} %sign_rows.1), channel_id=1, source_target_pairs={{0,4},{1,5},{2,6},{3,7},{4,12},{5,13},{6,14},{7,15},{8,0},{9,1},{1... | collective-permute-start | bytes 786440 | tf_op jit(solution)/shard_map/ppermute | solution.py:34
  50.2 5.3 %collective-permute-done.19.refs_2_ = bf16[128,1024]{1,0:T(8,128)(2,1)S(1)} collective-permute-done((bf16[128,1024]{1,0:T(8,128)(2,1)S(1)}, bf16[128,1024]{1,0:T(8,128)(2,1)S(1)}, u32[]{:S(2)}, u32[]{:S(2)}) %collective-permute-start.19) | collective-permute-done | bytes 262176 | tf_op jit(solution)/shard_map/ppermute | solution.py:34
  55.5 1.6 %collective-permute-done.20.refs_3_ = bf16[128,1024]{1,0:T(8,128)(2,1)S(1)} collective-permute-done((bf16[128,1024]{1,0:T(8,128)(2,1)S(1)}, bf16[128,1024]{1,0:T(8,128)(2,1)S(1)}, u32[]{:S(2)}, u32[]{:S(2)}) %collective-permute-start.20) | collective-permute-done | bytes 262176 | tf_op jit(solution)/shard_map/ppermute | solution.py:34
  58.5 1.4 %collective-permute-start.22 = (f32[128,256]{1,0:T(8,128)S(1)}, f32[128,256]{1,0:T(8,128)S(1)}, u32[]{:S(2)}, u32[]{:S(2)}) collective-permute-start(f32[128,256]{1,0:T(8,128)S(1)} %get-tuple-element.40), channel_id=1, source_target_pairs={{0,9},{1,8},{2,11},{3,10},{4,13},{5,12},{6,15},{7,14},{8,17},{9,16... | collective-permute-start | bytes 393224 | tf_op jit(solution)/shard_map/ppermute | solution.py:34
  59.9 1.6 %collective-permute-start.23 = (f32[128,256]{1,0:T(8,128)S(1)}, f32[128,256]{1,0:T(8,128)S(1)}, u32[]{:S(2)}, u32[]{:S(2)}) collective-permute-start(f32[128,256]{1,0:T(8,128)S(1)} %get-tuple-element.42), channel_id=1, source_target_pairs={{0,1},{1,0},{2,3},{3,2},{4,5},{5,4},{6,7},{7,6},{8,9},{9,8},{10,11... | collective-permute-start | bytes 393224 | tf_op jit(solution)/shard_map/ppermute | solution.py:34
  61.6 6.9 %collective-permute-start.24 = (f32[128,256]{1,0:T(8,128)S(1)}, f32[128,256]{1,0:T(8,128)S(1)}, u32[]{:S(2)}, u32[]{:S(2)}) collective-permute-start(f32[128,256]{1,0:T(8,128)S(1)} %get-tuple-element.43), channel_id=1, source_target_pairs={{0,24},{1,25},{2,26},{3,27},{4,28},{5,29},{6,30},{7,31},{8,0},{9,1... | collective-permute-start | bytes 393224 | tf_op jit(solution)/shard_map/ppermute | solution.py:34
  68.5 1.7 %collective-permute-start.25 = (f32[128,256]{1,0:T(8,128)S(1)}, f32[128,256]{1,0:T(8,128)S(1)}, u32[]{:S(2)}, u32[]{:S(2)}) collective-permute-start(f32[128,256]{1,0:T(8,128)S(1)} %get-tuple-element.44), channel_id=1, source_target_pairs={{0,25},{1,24},{2,27},{3,26},{4,29},{5,28},{6,31},{7,30},{8,1},{9,0... | collective-permute-start | bytes 393224 | tf_op jit(solution)/shard_map/ppermute | solution.py:34
  76.5 2.5 %collective-permute-done.15.refs_2_ = f32[128,256]{1,0:T(8,128)S(1)} collective-permute-done((f32[128,256]{1,0:T(8,128)S(1)}, f32[128,256]{1,0:T(8,128)S(1)}, u32[]{:S(2)}, u32[]{:S(2)}) %collective-permute-start.15) | collective-permute-done | bytes 131104 | tf_op jit(solution)/shard_map/ppermute | solution.py:34
  79.0 5.5 %collective-permute-done.16.refs_4_ = f32[128,256]{1,0:T(8,128)S(1)} collective-permute-done((f32[128,256]{1,0:T(8,128)S(1)}, f32[128,256]{1,0:T(8,128)S(1)}, u32[]{:S(2)}, u32[]{:S(2)}) %collective-permute-start.16) | collective-permute-done | bytes 131104 | tf_op jit(solution)/shard_map/ppermute | solution.py:34
  84.7 1.3 %final.1 = f32[3,128,1024]{2,1,0:T(8,128)} custom-call(s32[1]{0:T(128)} %bitcast.refs_0_, f32[128,256]{1,0:T(8,128)S(1)} %collective-permute-done.14.refs_1_, f32[128,256]{1,0:T(8,128)S(1)} %collective-permute-done.15.refs_2_, f32[128,256]{1,0:T(8,128)S(1)} %get-tuple-element.35.refs_3_, f32[128,256]{1,0:T(8,128)S(1)} %collective-permute-done.16.refs_4_, ...), custom_call_target="tpu_custom_call" | custom-call | bytes 3145728 | tf_op jit(solution)/shard_map/final/pallas_call | solution.py:181
  (49 shorter events, 13.3 us)
Async XLA Ops:
  0.0 15.0 %collective-permute-start.4 = (f32[1024]{0:T(1024)}, f32[1024]{0:T(1024)S(1)}, u32[]{:S(2)}, u32[]{:S(2)}) collective-permute-start(f32[1024]{0:T(1024)} %param.8), channel_id=1, source_target_pairs={{0,8},{1,9},{2,10},{3,11},{4,12},{5,13},{6,14},{7,15},{8,0},{9,1},... | collective-permute-start | bytes 12296 | tf_op jit(solution)/shard_map/ppermute | solution.py:34
  2.5 9.3 %collective-permute-start = (bf16[1024,128]{1,0:T(8,128)(2,1)}, bf16[1024,128]{1,0:T(8,128)(2,1)S(1)}, u32[]{:S(2)}, u32[]{:S(2)}) collective-permute-start(bf16[1024,128]{1,0:T(8,128)(2,1)} %prepare.1), channel_id=1, source_target_pairs={{0,0},{1,1},{2,2},{3,3},{4,8},{5,9},{6,10},{7,11},{8,4},{9,5},{10,... | collective-permute-start | bytes 786440 | tf_op jit(solution)/shard_map/ppermute | solution.py:34
  5.2 11.9 %collective-permute-start.5 = (bf16[128,1024]{1,0:T(8,128)(2,1)S(1)}, bf16[128,1024]{1,0:T(8,128)(2,1)S(1)}, u32[]{:S(2)}, u32[]{:S(2)}) collective-permute-start(bf16[128,1024]{1,0:T(8,128)(2,1)S(1)} %get-tuple-element.47), channel_id=1, source_target_pairs={{0,24},{1,25},{2,26},{3,27},{4,28},{5,29},{6,30},{7,31},{8,0},{9,1... | collective-permute-start | bytes 786440 | tf_op jit(solution)/shard_map/ppermute | solution.py:34
  10.4 7.7 %collective-permute-start.6 = (bf16[128,1024]{1,0:T(8,128)(2,1)S(1)}, bf16[128,1024]{1,0:T(8,128)(2,1)S(1)}, u32[]{:S(2)}, u32[]{:S(2)}) collective-permute-start(bf16[128,1024]{1,0:T(8,128)(2,1)S(1)} %get-tuple-element.46), channel_id=1, source_target_pairs={{0,8},{1,9},{2,10},{3,11},{4,12},{5,13},{6,14},{7,15},{8,16},{9,17... | collective-permute-start | bytes 786440 | tf_op jit(solution)/shard_map/ppermute | solution.py:34
  11.8 6.7 %collective-permute-start.1 = (bf16[1024,128]{1,0:T(8,128)(2,1)S(1)}, bf16[1024,128]{1,0:T(8,128)(2,1)S(1)}, u32[]{:S(2)}, u32[]{:S(2)}) collective-permute-start(bf16[1024,128]{1,0:T(8,128)(2,1)S(1)} %collective-permute-done.refs_4_), channel_id=1, source_target_pairs={{0,1},{1,0},{2,3},{3,2},{4,5},{5,4},{6,7},{7,6},{8,9},{9,8},{10,11... | collective-permute-start | bytes 786440 | tf_op jit(solution)/shard_map/ppermute | solution.py:34
  13.4 6.9 %collective-permute-start.2 = (bf16[1024,128]{1,0:T(8,128)(2,1)S(1)}, bf16[1024,128]{1,0:T(8,128)(2,1)S(1)}, u32[]{:S(2)}, u32[]{:S(2)}) collective-permute-start(bf16[1024,128]{1,0:T(8,128)(2,1)S(1)} %collective-permute-done.refs_4_), channel_id=1, source_target_pairs={{0,2},{1,3},{2,0},{3,1},{4,6},{5,7},{6,4},{7,5},{8,10},{9,11},{10,... | collective-permute-start | bytes 786440 | tf_op jit(solution)/shard_map/ppermute | solution.py:34
  15.0 11.0 %collective-permute-start.3 = (bf16[1024,128]{1,0:T(8,128)(2,1)S(1)}, bf16[1024,128]{1,0:T(8,128)(2,1)S(1)}, u32[]{:S(2)}, u32[]{:S(2)}) collective-permute-start(bf16[1024,128]{1,0:T(8,128)(2,1)S(1)} %collective-permute-done.refs_4_), channel_id=1, source_target_pairs={{0,3},{1,2},{2,1},{3,0},{4,7},{5,6},{6,5},{7,4},{8,11},{9,10},{10,... | collective-permute-start | bytes 786440 | tf_op jit(solution)/shard_map/ppermute | solution.py:34
  26.0 4.2 %collective-permute-start.10 = (bf16[1024,128]{1,0:T(8,128)(2,1)S(1)}, bf16[1024,128]{1,0:T(8,128)(2,1)S(1)}, u32[]{:S(2)}, u32[]{:S(2)}) collective-permute-start(bf16[1024,128]{1,0:T(8,128)(2,1)S(1)} %collective-permute-done.2.refs_6_), channel_id=1, source_target_pairs={{0,8},{1,9},{2,10},{3,11},{4,12},{5,13},{6,14},{7,15},{8,0},{9,1},... | collective-permute-start | bytes 786440 | tf_op jit(solution)/shard_map/ppermute | solution.py:34
  28.0 2.2 %collective-permute-start.11 = (bf16[1024,128]{1,0:T(8,128)(2,1)S(1)}, bf16[1024,128]{1,0:T(8,128)(2,1)S(1)}, u32[]{:S(2)}, u32[]{:S(2)}) collective-permute-start(bf16[1024,128]{1,0:T(8,128)(2,1)S(1)} %collective-permute-done.3.refs_7_), channel_id=1, source_target_pairs={{0,8},{1,9},{2,10},{3,11},{4,12},{5,13},{6,14},{7,15},{8,0},{9,1},... | collective-permute-start | bytes 786440 | tf_op jit(solution)/shard_map/ppermute | solution.py:34
  28.6 28.6 %collective-permute-start.7 = (bf16[384,1024]{1,0:T(8,128)(2,1)S(1)}, bf16[384,1024]{1,0:T(8,128)(2,1)S(1)}, u32[]{:S(2)}, u32[]{:S(2)}) collective-permute-start(bf16[384,1024]{1,0:T(8,128)(2,1)S(1)} %pad_maximum_fusion.refs_0_), channel_id=1, source_target_pairs={{0,1},{1,0},{2,3},{3,2},{4,5},{5,4},{6,7},{7,6},{8,9},{9,8},{10,11... | collective-permute-start | bytes 2359304 | tf_op jit(solution)/shard_map/ppermute | solution.py:34
  42.3 13.3 %collective-permute-start.19 = (bf16[128,1024]{1,0:T(8,128)(2,1)S(1)}, bf16[128,1024]{1,0:T(8,128)(2,1)S(1)}, u32[]{:S(2)}, u32[]{:S(2)}) collective-permute-start(bf16[128,1024]{1,0:T(8,128)(2,1)S(1)} %sign_rows.1), channel_id=1, source_target_pairs={{0,2},{1,3},{2,0},{3,1},{4,10},{5,11},{6,8},{7,9},{8,6},{9,7},{10,... | collective-permute-start | bytes 786440 | tf_op jit(solution)/shard_map/ppermute | solution.py:34
  43.9 13.2 %collective-permute-start.20 = (bf16[128,1024]{1,0:T(8,128)(2,1)S(1)}, bf16[128,1024]{1,0:T(8,128)(2,1)S(1)}, u32[]{:S(2)}, u32[]{:S(2)}) collective-permute-start(bf16[128,1024]{1,0:T(8,128)(2,1)S(1)} %sign_rows.1), channel_id=1, source_target_pairs={{0,6},{1,7},{2,4},{3,5},{4,14},{5,15},{6,12},{7,13},{8,2},{9,3},{1... | collective-permute-start | bytes 786440 | tf_op jit(solution)/shard_map/ppermute | solution.py:34
  46.1 15.4 %collective-permute-start.12 = (bf16[128,1024]{1,0:T(8,128)(2,1)S(1)}, bf16[128,1024]{1,0:T(8,128)(2,1)S(1)}, u32[]{:S(2)}, u32[]{:S(2)}) collective-permute-start(bf16[128,1024]{1,0:T(8,128)(2,1)S(1)} %sign_rows.1), channel_id=1, source_target_pairs={{0,0},{1,1},{2,2},{3,3},{4,8},{5,9},{6,10},{7,11},{8,4},{9,5},{10,... | collective-permute-start | bytes 786440 | tf_op jit(solution)/shard_map/ppermute | solution.py:34
  46.8 21.6 %collective-permute-start.13 = (bf16[128,1024]{1,0:T(8,128)(2,1)S(1)}, bf16[128,1024]{1,0:T(8,128)(2,1)S(1)}, u32[]{:S(2)}, u32[]{:S(2)}) collective-permute-start(bf16[128,1024]{1,0:T(8,128)(2,1)S(1)} %sign_rows.1), channel_id=1, source_target_pairs={{0,4},{1,5},{2,6},{3,7},{4,12},{5,13},{6,14},{7,15},{8,0},{9,1},{1... | collective-permute-start | bytes 786440 | tf_op jit(solution)/shard_map/ppermute | solution.py:34
  58.1 13.0 %collective-permute-start.21 = (f32[128,256]{1,0:T(8,128)S(1)}, f32[128,256]{1,0:T(8,128)S(1)}, u32[]{:S(2)}, u32[]{:S(2)}) collective-permute-start(f32[128,256]{1,0:T(8,128)S(1)} %get-tuple-element.39), channel_id=1, source_target_pairs={{0,8},{1,9},{2,10},{3,11},{4,12},{5,13},{6,14},{7,15},{8,16},{9,17... | collective-permute-start | bytes 393224 | tf_op jit(solution)/shard_map/ppermute | solution.py:34
  58.5 13.4 %collective-permute-start.22 = (f32[128,256]{1,0:T(8,128)S(1)}, f32[128,256]{1,0:T(8,128)S(1)}, u32[]{:S(2)}, u32[]{:S(2)}) collective-permute-start(f32[128,256]{1,0:T(8,128)S(1)} %get-tuple-element.40), channel_id=1, source_target_pairs={{0,9},{1,8},{2,11},{3,10},{4,13},{5,12},{6,15},{7,14},{8,17},{9,16... | collective-permute-start | bytes 393224 | tf_op jit(solution)/shard_map/ppermute | solution.py:34
  59.9 13.1 %collective-permute-start.23 = (f32[128,256]{1,0:T(8,128)S(1)}, f32[128,256]{1,0:T(8,128)S(1)}, u32[]{:S(2)}, u32[]{:S(2)}) collective-permute-start(f32[128,256]{1,0:T(8,128)S(1)} %get-tuple-element.42), channel_id=1, source_target_pairs={{0,1},{1,0},{2,3},{3,2},{4,5},{5,4},{6,7},{7,6},{8,9},{9,8},{10,11... | collective-permute-start | bytes 393224 | tf_op jit(solution)/shard_map/ppermute | solution.py:34
  61.6 12.5 %collective-permute-start.24 = (f32[128,256]{1,0:T(8,128)S(1)}, f32[128,256]{1,0:T(8,128)S(1)}, u32[]{:S(2)}, u32[]{:S(2)}) collective-permute-start(f32[128,256]{1,0:T(8,128)S(1)} %get-tuple-element.43), channel_id=1, source_target_pairs={{0,24},{1,25},{2,26},{3,27},{4,28},{5,29},{6,30},{7,31},{8,0},{9,1... | collective-permute-start | bytes 393224 | tf_op jit(solution)/shard_map/ppermute | solution.py:34
  68.5 6.3 %collective-permute-start.25 = (f32[128,256]{1,0:T(8,128)S(1)}, f32[128,256]{1,0:T(8,128)S(1)}, u32[]{:S(2)}, u32[]{:S(2)}) collective-permute-start(f32[128,256]{1,0:T(8,128)S(1)} %get-tuple-element.44), channel_id=1, source_target_pairs={{0,25},{1,24},{2,27},{3,26},{4,29},{5,28},{6,31},{7,30},{8,1},{9,0... | collective-permute-start | bytes 393224 | tf_op jit(solution)/shard_map/ppermute | solution.py:34
  71.1 5.4 %collective-permute-start.14 = (f32[128,256]{1,0:T(8,128)S(1)}, f32[128,256]{1,0:T(8,128)S(1)}, u32[]{:S(2)}, u32[]{:S(2)}) collective-permute-start(f32[128,256]{1,0:T(8,128)S(1)} %get-tuple-element.33), channel_id=1, source_target_pairs={{0,8},{1,9},{2,10},{3,11},{4,12},{5,13},{6,14},{7,15},{8,16},{9,17... | collective-permute-start | bytes 393224 | tf_op jit(solution)/shard_map/ppermute | solution.py:34
  71.8 7.1 %collective-permute-start.15 = (f32[128,256]{1,0:T(8,128)S(1)}, f32[128,256]{1,0:T(8,128)S(1)}, u32[]{:S(2)}, u32[]{:S(2)}) collective-permute-start(f32[128,256]{1,0:T(8,128)S(1)} %get-tuple-element.34), channel_id=1, source_target_pairs={{0,9},{1,8},{2,11},{3,10},{4,13},{5,12},{6,15},{7,14},{8,17},{9,16... | collective-permute-start | bytes 393224 | tf_op jit(solution)/shard_map/ppermute | solution.py:34
  73.0 11.5 %collective-permute-start.16 = (f32[128,256]{1,0:T(8,128)S(1)}, f32[128,256]{1,0:T(8,128)S(1)}, u32[]{:S(2)}, u32[]{:S(2)}) collective-permute-start(f32[128,256]{1,0:T(8,128)S(1)} %get-tuple-element.36), channel_id=1, source_target_pairs={{0,1},{1,0},{2,3},{3,2},{4,5},{5,4},{6,7},{7,6},{8,9},{9,8},{10,11... | collective-permute-start | bytes 393224 | tf_op jit(solution)/shard_map/ppermute | solution.py:34
  74.1 10.4 %collective-permute-start.17 = (f32[128,256]{1,0:T(8,128)S(1)}, f32[128,256]{1,0:T(8,128)S(1)}, u32[]{:S(2)}, u32[]{:S(2)}) collective-permute-start(f32[128,256]{1,0:T(8,128)S(1)} %get-tuple-element.37), channel_id=1, source_target_pairs={{0,24},{1,25},{2,26},{3,27},{4,28},{5,29},{6,30},{7,31},{8,0},{9,1... | collective-permute-start | bytes 393224 | tf_op jit(solution)/shard_map/ppermute | solution.py:34
  74.8 9.9 %collective-permute-start.18 = (f32[128,256]{1,0:T(8,128)S(1)}, f32[128,256]{1,0:T(8,128)S(1)}, u32[]{:S(2)}, u32[]{:S(2)}) collective-permute-start(f32[128,256]{1,0:T(8,128)S(1)} %get-tuple-element.38), channel_id=1, source_target_pairs={{0,25},{1,24},{2,27},{3,26},{4,29},{5,28},{6,31},{7,30},{8,1},{9,0... | collective-permute-start | bytes 393224 | tf_op jit(solution)/shard_map/ppermute | solution.py:34
  (5 other events, 41.8 us)

commit v3 on v2

--- a/solution.py
+++ b/solution.py
@@ -11,6 +11,8 @@
 F32 = jnp.float32
 BF16 = jnp.bfloat16
 LAST = (((1,), (1,)), ((), ()))
+LARGEST = 0.09375
+CODES = 32766.0
 VMEM = pl.BlockSpec(memory_space=pltpu.VMEM)
 SMEM = pl.BlockSpec(memory_space=pltpu.SMEM)
 
@@ -44,73 +46,68 @@
     )
     for a in range(blocks):
         rows = slice(a * BLOCK, (a + 1) * BLOCK)
-        out_ref[rows, :] = (ham_ref[rows, :] * weights[a : a + 1, :]).astype(BF16)
+        entry = ham_ref[rows, :] * weights[a : a + 1, :]
+        root = jnp.sqrt(jnp.sqrt(jnp.abs(entry) * (1.0 / LARGEST)))
+        code = (root * CODES + 0.5).astype(jnp.int32)
+        out_ref[rows, :] = jnp.where(entry < 0.0, -code, code).astype(jnp.int16)
 
 
 def prepare(hamiltonian, pattern):
     return pl.pallas_call(
         prepare_kernel,
-        out_shape=jax.ShapeDtypeStruct(hamiltonian.shape, BF16),
+        out_shape=jax.ShapeDtypeStruct(hamiltonian.shape, jnp.int16),
         in_specs=[VMEM, VMEM],
         out_specs=VMEM,
+        compiler_params=pltpu.CompilerParams(vmem_limit_bytes=8 * 2**20),
         name="prepare",
     )(hamiltonian, pattern.T)
 
 
 def sign_kernel(count, slot_ref, active_ref, mask_row, diag_row, *refs):
     shards = refs[:count]
-    out_ref, ham = refs[count:]
+    out_ref, ham, high_ref, low_ref = refs[count:]
     width = ham.shape[0]
     own = out_ref.shape[0]
     slot = slot_ref[0]
-    squares = jnp.zeros((1, own), F32)
-    rows = lax.broadcasted_iota(jnp.int32, (own, own), 0)
-    cols = lax.broadcasted_iota(jnp.int32, (own, own), 1)
-    eye = rows == cols
-    mask_col = jnp.broadcast_to(mask_row[...], (own, width)).T.astype(BF16)
+    mask_col = jnp.broadcast_to(mask_row[...], (own, width)).T
     for k in range(count):
         start = pl.multiple_of((slot ^ k) * own, own)
-        block = shards[k][...] * mask_col * mask_row[:, pl.ds(start, own)].astype(BF16)
-        ham[:, pl.ds(start, own)] = block
-        wide = block.astype(F32)
-        squares += 0.5 * jnp.sum(wide * wide, axis=0, keepdims=True)
-    for k in range(count):
-        start = k * own
-        diag = diag_row[:, start : start + own]
-        across = ham[start : start + own, :]
-        down = ham[:, start : start + own]
-        both = jnp.dot(across, down, preferred_element_type=F32)
-        here = ham[start : start + own, start : start + own].astype(F32)
-        entries = 0.5 * both + 2.0 * diag * here
-        squares += jnp.sum(jnp.where(eye, entries, 0.0), axis=0, keepdims=True)
-        squares += diag * diag
+        root = shards[k][...].astype(F32) * (1.0 / CODES)
+        entry = (root * jnp.abs(root)) * (root * root) * LARGEST
+        ham[:, pl.ds(start, own)] = entry * mask_col * mask_row[:, pl.ds(start, own)]
+    rows = lax.broadcasted_iota(jnp.int32, (own, width), 0)
+    cols = lax.broadcasted_iota(jnp.int32, (own, width), 1)
+
+    def strip(k, squares):
+        at = pl.ds(pl.multiple_of(k * own, own), own)
+        diag = jnp.where(cols == rows + k * own, diag_row[...], 0.0)
+        both = 0.5 * (ham[at, :] + ham[:, at].T) + diag
+        high = both.astype(BF16)
+        high_ref[at, :] = high
+        low_ref[at, :] = (both - high.astype(F32)).astype(BF16)
+        return squares + jnp.sum(both * both, axis=0, keepdims=True)
+
+    small = count <= 8
+    squares = lax.fori_loop(0, count, strip, jnp.zeros((1, width), F32), unroll=small)
     total = jnp.sum(squares, axis=1, keepdims=True)
     active_rows = active_ref[0].astype(F32) * BLOCK
     factor = jnp.sqrt(active_rows / (4.0 * (total + 1e-06)))
-    diag_all = diag_row[...]
 
     def times(panel):
         high = panel.astype(BF16)
         low = (panel - high.astype(F32)).astype(BF16)
         stacked = jnp.concatenate([high, low], axis=0)
-        prod = jnp.dot(stacked, ham[...], preferred_element_type=F32)
-        prod += lax.dot_general(stacked, ham[...], LAST, preferred_element_type=F32)
-        return factor * (0.5 * (prod[:own] + prod[own:]) + diag_all * panel)
+        prod = jnp.dot(stacked, high_ref[...], preferred_element_type=F32)
+        rest = jnp.dot(high, low_ref[...], preferred_element_type=F32)
+        return factor * (prod[:own] + prod[own:] + rest)
 
     def cubic(panel):
         return 0.5 * (3.0 * panel - times(times(panel)))
 
-    start = pl.multiple_of(slot * own, own)
-    turned = lax.dot_general(
-        eye.astype(BF16), ham[:, pl.ds(start, own)], LAST, preferred_element_type=F32
-    )
-    across = ham[pl.ds(start, own), :].astype(F32)
-    wide_rows = lax.broadcasted_iota(jnp.int32, (own, width), 0)
-    wide_cols = lax.broadcasted_iota(jnp.int32, (own, width), 1)
-    on_diag = wide_cols == wide_rows + start
-    first = 0.5 * (turned + across) + jnp.where(on_diag, diag_all, 0.0)
+    at = pl.ds(pl.multiple_of(slot * own, own), own)
+    first = high_ref[at, :].astype(F32) + low_ref[at, :].astype(F32)
     left = cubic(factor * first)
-    inner = lax.fori_loop(0, 2, lambda _, panel: cubic(times(panel)), left, unroll=count <= 8)
+    inner = lax.fori_loop(0, 2, lambda _, panel: cubic(times(panel)), left, unroll=small)
     out_ref[...] = (0.5 * (3.0 * left - inner)).astype(BF16)
 
 
@@ -122,8 +119,12 @@
         out_shape=jax.ShapeDtypeStruct((own, width), BF16),
         in_specs=[SMEM, SMEM] + [VMEM] * (2 + count),
         out_specs=VMEM,
-        scratch_shapes=[pltpu.VMEM((width, width), BF16)],
-        compiler_params=pltpu.CompilerParams(vmem_limit_bytes=8 * 2**20 + 11 * width * width),
+        scratch_shapes=[
+            pltpu.VMEM((width, width), F32),
+            pltpu.VMEM((width, width), BF16),
+            pltpu.VMEM((width, width), BF16),
+        ],
+        compiler_params=pltpu.CompilerParams(vmem_limit_bytes=8 * 2**20 + 12 * width * width),
         cost_estimate=pl.CostEstimate(
             flops=70 * own * width * width, bytes_accessed=2 * width * width, transcendentals=0
         ),
@@ -139,17 +140,18 @@
         for j in range(2):
             prod = lax.dot_general(refs[j][...], signs[k][...], LAST, preferred_element_type=F32)
             for side in range(sides):
-                outs[j * sides + side][:, cols] = prod[side * own : (side + 1) * own]
+                out = outs[j * sides + side]
+                out[:, cols] = prod[side * own : (side + 1) * own].astype(out.dtype)
 
 
 def products(trio, mates, signs):
     count = len(signs)
     own, width = signs[0].shape
     sides = trio.shape[0] // own
-    shape = jax.ShapeDtypeStruct((own, count * own), F32)
+    kinds = [F32 if k == 1 else BF16 for k in range(2 * sides)]
     return pl.pallas_call(
         lambda *refs: products_kernel(count, sides, *refs),
-        out_shape=[shape] * (2 * sides),
+        out_shape=[jax.ShapeDtypeStruct((own, count * own), kind) for kind in kinds],
         in_specs=[VMEM] * (2 + count),
         out_specs=[VMEM] * (2 * sides),
         compiler_params=pltpu.CompilerParams(vmem_limit_bytes=24 * 2**20),
@@ -172,7 +174,8 @@
                 at += 1
                 for k, step in enumerate(steps):
                     start = pl.multiple_of((slot_ref[0] ^ (step + mate)) * own, own)
-                    out_ref[side, :, pl.ds(start, own)] = part[:, k * own : (k + 1) * own]
+                    block = part[:, k * own : (k + 1) * own]
+                    out_ref[side, :, pl.ds(start, own)] = block.astype(F32)
 
 
 def final(slot, groups, parts, width):
@@ -203,6 +206,7 @@
         return (r, c) if c // half == r % 2 else (r ^ 1, c ^ half)
 
     masked = prepare(hamiltonian, pattern)
+    masked, onsite = lax.optimization_barrier((masked, onsite))
     held = send(masked, home)
     parts = [held]
     for step in range(1, half):

time: 86.3 us -> 78.7 us (0.912)
  starting transfers between devices: 39.3 us -> 32.3 us
  Pallas kernels: 17.2 us -> 14.5 us
  local copies, waits for them, and re-layouts: 1.99 us -> 3.65 us
    ppermute x26, starting transfers between devices: 39.3 us -> 32.3 us  [send(): return lax.ppermute(array, AXES, moves)]
    unnamed x6 -> x10, local copies, waits for them, and re-layouts: 0.01 us -> 1.76 us
    pallas_call x1, Pallas kernels: 12 us -> 10.6 us  [sign_rows(): pl.pallas_call(lambda *refs: sign_kernel(count, *refs), out_shape=jax.Sha...]
    pallas_call x1, Pallas kernels: 1.96 us -> 0.62 us  [prepare(): pl.pallas_call(prepare_kernel, out_shape=jax.ShapeDtypeStruct(hamiltonian...]
  transfers between devices with their start and end apart: 26 -> 26, of which waited for: 12 -> 10; matrix products, arithmetic and copies ran while one was open for 3% -> 3% of each run, Pallas kernels for 18% -> 16%
where the time goes in v3:
time: 78.7 us; the launch traced here: 78.1 us
  starting transfers between devices  32.3 us (41%)
  waiting for transfers between devices  26.7 us (34%)
  Pallas kernels  14.5 us (18%)
  local copies, waits for them, and re-layouts  3.65 us (5%)
    ppermute x26, starting transfers between devices, send(): return lax.ppermute(array, AXES, moves)  32.3 us
    ppermute x26, waiting for transfers between devices, send(): return lax.ppermute(array, AXES, moves)  26.7 us
    pallas_call x1, Pallas kernels, sign_rows(): pl.pallas_call(lambda *refs: sign_kernel(count, *refs), out_shape=jax.Sha...  10.6 us
    pallas_call x2, Pallas kernels, products(): pl.pallas_call(lambda *refs: products_kernel(count, sides, *refs), out_sh...  1.92 us
    unnamed x10, local copies, waits for them, and re-layouts  1.76 us
  transfers between devices with their start and end apart: 26, of which 10 were waited for; matrix products, arithmetic and copies ran while one was open for 3% of the time, Pallas kernels for 16%

profile of v3, /device:TPU:0, one launch (start us, length us, event | category | flops | bytes accessed | tf_op | source)
XLA Modules:
  0.0 78.1 jit_solution(5238004192449628236)
XLA Ops:
  0.0 1.1 %copy-done.1 = f32[1024,128]{1,0:T(8,128)S(1)} copy-done((f32[1024,128]{1,0:T(8,128)S(1)}, f32[1024,128]{1,0:T(8,128)}, u32[]{:S(2)}) %copy-start.1) | copy-done | bytes 524312
  3.6 1.2 %slice_bitcast_fusion = (bf16[128,1024]{1,0:T(8,128)(2,1)S(1)}, bf16[128,1024]{1,0:T(8,128)(2,1)S(1)}, bf16[128,1024]{1,0:T(8,128)(2,1)S(1)}) fusion(bf16[3,128,1024]{2,1,0:T(8,128)(2,1)} %bitcast.19), kind=kLoop, calls=%fused_computation.1 | loop fusion | bytes 1572864 | tf_op jit(solution)/shard_map/squeeze | solution.py:230
  4.7 5.0 %collective-permute-start.6 = (bf16[128,1024]{1,0:T(8,128)(2,1)S(1)}, bf16[128,1024]{1,0:T(8,128)(2,1)S(1)}, u32[]{:S(2)}, u32[]{:S(2)}) collective-permute-start(bf16[128,1024]{1,0:T(8,128)(2,1)S(1)} %get-tuple-element.50), channel_id=1, source_target_pairs={{0,8},{1,9},{2,10},{3,11},{4,12},{5,13},{6,14},{7,15},{8,16},{9,17... | collective-permute-start | bytes 786440 | tf_op jit(solution)/shard_map/ppermute | solution.py:36
  9.8 1.2 %collective-permute-start.5 = (bf16[128,1024]{1,0:T(8,128)(2,1)S(1)}, bf16[128,1024]{1,0:T(8,128)(2,1)S(1)}, u32[]{:S(2)}, u32[]{:S(2)}) collective-permute-start(bf16[128,1024]{1,0:T(8,128)(2,1)S(1)} %get-tuple-element.51), channel_id=1, source_target_pairs={{0,24},{1,25},{2,26},{3,27},{4,28},{5,29},{6,30},{7,31},{8,0},{9,1... | collective-permute-start | bytes 786440 | tf_op jit(solution)/shard_map/ppermute | solution.py:36
  12.1 2.6 %collective-permute-start.3 = (s16[1024,128]{1,0:T(8,128)(2,1)S(1)}, s16[1024,128]{1,0:T(8,128)(2,1)S(1)}, u32[]{:S(2)}, u32[]{:S(2)}) collective-permute-start(s16[1024,128]{1,0:T(8,128)(2,1)S(1)} %collective-permute-done.refs_4_), channel_id=1, source_target_pairs={{0,3},{1,2},{2,1},{3,0},{4,7},{5,6},{6,5},{7,4},{8,11},{9,10},{10,... | collective-permute-start | bytes 786440 | tf_op jit(solution)/shard_map/ppermute | solution.py:36
  16.8 3.8 %collective-permute-done.3.refs_7_ = s16[1024,128]{1,0:T(8,128)(2,1)S(1)} collective-permute-done((s16[1024,128]{1,0:T(8,128)(2,1)S(1)}, s16[1024,128]{1,0:T(8,128)(2,1)S(1)}, u32[]{:S(2)}, u32[]{:S(2)}) %collective-permute-start.3) | collective-permute-done | bytes 262176 | tf_op jit(solution)/shard_map/ppermute | solution.py:36
  20.6 4.9 %collective-permute-done.2.refs_6_ = s16[1024,128]{1,0:T(8,128)(2,1)S(1)} collective-permute-done((s16[1024,128]{1,0:T(8,128)(2,1)S(1)}, s16[1024,128]{1,0:T(8,128)(2,1)S(1)}, u32[]{:S(2)}, u32[]{:S(2)}) %collective-permute-start.2) | collective-permute-done | bytes 262176 | tf_op jit(solution)/shard_map/ppermute | solution.py:36
  25.5 2.5 %collective-permute-done.1.refs_5_ = s16[1024,128]{1,0:T(8,128)(2,1)S(1)} collective-permute-done((s16[1024,128]{1,0:T(8,128)(2,1)S(1)}, s16[1024,128]{1,0:T(8,128)(2,1)S(1)}, u32[]{:S(2)}, u32[]{:S(2)}) %collective-permute-start.1) | collective-permute-done | bytes 262176 | tf_op jit(solution)/shard_map/ppermute | solution.py:36
  29.1 1.3 %collective-permute-start.7 = (bf16[384,1024]{1,0:T(8,128)(2,1)S(1)}, bf16[384,1024]{1,0:T(8,128)(2,1)S(1)}, u32[]{:S(2)}, u32[]{:S(2)}) collective-permute-start(bf16[384,1024]{1,0:T(8,128)(2,1)S(1)} %pad_maximum_fusion.refs_0_), channel_id=1, source_target_pairs={{0,1},{1,0},{2,3},{3,2},{4,5},{5,4},{6,7},{7,6},{8,9},{9,8},{10,11... | collective-permute-start | bytes 2359304 | tf_op jit(solution)/shard_map/ppermute | solution.py:36
  30.7 10.6 %sign_rows.1 = bf16[128,1024]{1,0:T(8,128)(2,1)S(1)} custom-call(s32[1]{0:T(128)} %bitcast.8.refs_0_, s32[1]{0:T(128)} %dynamic_slice.9.refs_1_, f32[1,1024]{1,0:T(1,128)S(1)} %bitcast.16, f32[1,1024]{1,0:T(1,128)S(1)} %bitcast.17, s16[1024,128]{1,0:T(8,128)(2,1)S(1)} %collective-permute-done.refs_4_, s16[1024,128]{1,0:T(8,128)(2,1)S(1)} %collective-permute-done.1.refs_5_, ...), custom_call_target="tpu_custom_call" | custom-call | flops 9395240960 | bytes 2097152 | tf_op jit(solution)/shard_map/sign_rows/pallas_call | solution.py:117
  41.3 2.2 %collective-permute-start.20 = (bf16[128,1024]{1,0:T(8,128)(2,1)S(1)}, bf16[128,1024]{1,0:T(8,128)(2,1)S(1)}, u32[]{:S(2)}, u32[]{:S(2)}) collective-permute-start(bf16[128,1024]{1,0:T(8,128)(2,1)S(1)} %sign_rows.1), channel_id=1, source_target_pairs={{0,6},{1,7},{2,4},{3,5},{4,14},{5,15},{6,12},{7,13},{8,2},{9,3},{1... | collective-permute-start | bytes 786440 | tf_op jit(solution)/shard_map/ppermute | solution.py:36
  43.5 1.1 %collective-permute-start.13 = (bf16[128,1024]{1,0:T(8,128)(2,1)S(1)}, bf16[128,1024]{1,0:T(8,128)(2,1)S(1)}, u32[]{:S(2)}, u32[]{:S(2)}) collective-permute-start(bf16[128,1024]{1,0:T(8,128)(2,1)S(1)} %sign_rows.1), channel_id=1, source_target_pairs={{0,4},{1,5},{2,6},{3,7},{4,12},{5,13},{6,14},{7,15},{8,0},{9,1},{1... | collective-permute-start | bytes 786440 | tf_op jit(solution)/shard_map/ppermute | solution.py:36
  45.2 5.0 %collective-permute-done.20.refs_3_ = bf16[128,1024]{1,0:T(8,128)(2,1)S(1)} collective-permute-done((bf16[128,1024]{1,0:T(8,128)(2,1)S(1)}, bf16[128,1024]{1,0:T(8,128)(2,1)S(1)}, u32[]{:S(2)}, u32[]{:S(2)}) %collective-permute-start.20) | collective-permute-done | bytes 262176 | tf_op jit(solution)/shard_map/ppermute | solution.py:36
  50.2 5.7 %collective-permute-done.19.refs_2_ = bf16[128,1024]{1,0:T(8,128)(2,1)S(1)} collective-permute-done((bf16[128,1024]{1,0:T(8,128)(2,1)S(1)}, bf16[128,1024]{1,0:T(8,128)(2,1)S(1)}, u32[]{:S(2)}, u32[]{:S(2)}) %collective-permute-start.19) | collective-permute-done | bytes 262176 | tf_op jit(solution)/shard_map/ppermute | solution.py:36
  55.9 1.0 %products.3 = (bf16[128,256]{1,0:T(8,128)(2,1)S(1)}, f32[128,256]{1,0:T(8,128)S(1)}, bf16[128,256]{1,0:T(8,128)(2,1)S(1)}, bf16[128,256]{1,0:T(8,128)(2,1)S(1)},...) custom-call(bf16[384,1024]{1,0:T(8,128)(2,1)S(1)} %pad_maximum_fusion.refs_0_, ...), custom_call_target="tpu_custom_call" | custom-call | flops 402653184 | bytes 2097152 | tf_op jit(solution)/shard_map/products/pallas_call | solution.py:152
  56.9 2.2 %collective-permute-start.22 = (bf16[128,256]{1,0:T(8,128)(2,1)S(1)}, bf16[128,256]{1,0:T(8,128)(2,1)S(1)}, u32[]{:S(2)}, u32[]{:S(2)}) collective-permute-start(bf16[128,256]{1,0:T(8,128)(2,1)S(1)} %get-tuple-element.44), channel_id=1, source_target_pairs={{0,9},{1,8},{2,11},{3,10},{4,13},{5,12},{6,15},{7,14},{8,17},{9,16... | collective-permute-start | bytes 196616 | tf_op jit(solution)/shard_map/ppermute | solution.py:36
  59.1 1.9 %collective-permute-start.23 = (bf16[128,256]{1,0:T(8,128)(2,1)S(1)}, bf16[128,256]{1,0:T(8,128)(2,1)S(1)}, u32[]{:S(2)}, u32[]{:S(2)}) collective-permute-start(bf16[128,256]{1,0:T(8,128)(2,1)S(1)} %get-tuple-element.46), channel_id=1, source_target_pairs={{0,1},{1,0},{2,3},{3,2},{4,5},{5,4},{6,7},{7,6},{8,9},{9,8},{10,11... | collective-permute-start | bytes 196616 | tf_op jit(solution)/shard_map/ppermute | solution.py:36
  61.0 4.1 %collective-permute-start.24 = (bf16[128,256]{1,0:T(8,128)(2,1)S(1)}, bf16[128,256]{1,0:T(8,128)(2,1)S(1)}, u32[]{:S(2)}, u32[]{:S(2)}) collective-permute-start(bf16[128,256]{1,0:T(8,128)(2,1)S(1)} %get-tuple-element.47), channel_id=1, source_target_pairs={{0,24},{1,25},{2,26},{3,27},{4,28},{5,29},{6,30},{7,31},{8,0},{9,1... | collective-permute-start | bytes 196616 | tf_op jit(solution)/shard_map/ppermute | solution.py:36
  65.1 3.1 %collective-permute-start.25 = (bf16[128,256]{1,0:T(8,128)(2,1)S(1)}, bf16[128,256]{1,0:T(8,128)(2,1)S(1)}, u32[]{:S(2)}, u32[]{:S(2)}) collective-permute-start(bf16[128,256]{1,0:T(8,128)(2,1)S(1)} %get-tuple-element.48), channel_id=1, source_target_pairs={{0,25},{1,24},{2,27},{3,26},{4,29},{5,28},{6,31},{7,30},{8,1},{9,0... | collective-permute-start | bytes 196616 | tf_op jit(solution)/shard_map/ppermute | solution.py:36
  69.3 1.7 %collective-permute-start.15 = (bf16[128,256]{1,0:T(8,128)(2,1)S(1)}, bf16[128,256]{1,0:T(8,128)(2,1)S(1)}, u32[]{:S(2)}, u32[]{:S(2)}) collective-permute-start(bf16[128,256]{1,0:T(8,128)(2,1)S(1)} %get-tuple-element.38), channel_id=1, source_target_pairs={{0,9},{1,8},{2,11},{3,10},{4,13},{5,12},{6,15},{7,14},{8,17},{9,16... | collective-permute-start | bytes 196616 | tf_op jit(solution)/shard_map/ppermute | solution.py:36
  71.0 1.5 %collective-permute-start.16 = (bf16[128,256]{1,0:T(8,128)(2,1)S(1)}, bf16[128,256]{1,0:T(8,128)(2,1)S(1)}, u32[]{:S(2)}, u32[]{:S(2)}) collective-permute-start(bf16[128,256]{1,0:T(8,128)(2,1)S(1)} %get-tuple-element.40), channel_id=1, source_target_pairs={{0,1},{1,0},{2,3},{3,2},{4,5},{5,4},{6,7},{7,6},{8,9},{9,8},{10,11... | collective-permute-start | bytes 196616 | tf_op jit(solution)/shard_map/ppermute | solution.py:36
  73.0 1.0 %collective-permute-done.15.refs_2_ = bf16[128,256]{1,0:T(8,128)(2,1)S(1)} collective-permute-done((bf16[128,256]{1,0:T(8,128)(2,1)S(1)}, bf16[128,256]{1,0:T(8,128)(2,1)S(1)}, u32[]{:S(2)}, u32[]{:S(2)}) %collective-permute-start.15) | collective-permute-done | bytes 65568 | tf_op jit(solution)/shard_map/ppermute | solution.py:36
  74.0 2.4 %collective-permute-done.16.refs_4_ = bf16[128,256]{1,0:T(8,128)(2,1)S(1)} collective-permute-done((bf16[128,256]{1,0:T(8,128)(2,1)S(1)}, bf16[128,256]{1,0:T(8,128)(2,1)S(1)}, u32[]{:S(2)}, u32[]{:S(2)}) %collective-permute-start.16) | collective-permute-done | bytes 65568 | tf_op jit(solution)/shard_map/ppermute | solution.py:36
  76.7 1.3 %final.1 = f32[3,128,1024]{2,1,0:T(8,128)} custom-call(s32[1]{0:T(128)} %bitcast.refs_0_, bf16[128,256]{1,0:T(8,128)(2,1)S(1)} %collective-permute-done.14.refs_1_, bf16[128,256]{1,0:T(8,128)(2,1)S(1)} %collective-permute-done.15.refs_2_, f32[128,256]{1,0:T(8,128)S(1)} %get-tuple-element.39.refs_3_, bf16[128,256]{1,0:T(8,128)(2,1)S(1)} %collective-permute-done.16.refs_4_, ...), custom_call_target="tpu_custom_call" | custom-call | bytes 3145728 | tf_op jit(solution)/shard_map/final/pallas_call | solution.py:184
  (53 shorter events, 9.6 us)
Async XLA Ops:
  2.4 12.8 %collective-permute-start.4 = (f32[1024]{0:T(1024)}, f32[1024]{0:T(1024)S(1)}, u32[]{:S(2)}, u32[]{:S(2)}) collective-permute-start(f32[1024]{0:T(1024)} %param.8), channel_id=1, source_target_pairs={{0,8},{1,9},{2,10},{3,11},{4,12},{5,13},{6,14},{7,15},{8,0},{9,1},... | collective-permute-start | bytes 12296 | tf_op jit(solution)/shard_map/ppermute | solution.py:36
  2.9 9.2 %collective-permute-start = (s16[1024,128]{1,0:T(8,128)(2,1)S(1)}, s16[1024,128]{1,0:T(8,128)(2,1)S(1)}, u32[]{:S(2)}, u32[]{:S(2)}) collective-permute-start(s16[1024,128]{1,0:T(8,128)(2,1)S(1)} %prepare.1), channel_id=1, source_target_pairs={{0,0},{1,1},{2,2},{3,3},{4,8},{5,9},{6,10},{7,11},{8,4},{9,5},{10,... | collective-permute-start | bytes 786440 | tf_op jit(solution)/shard_map/ppermute | solution.py:36
  4.7 12.1 %collective-permute-start.6 = (bf16[128,1024]{1,0:T(8,128)(2,1)S(1)}, bf16[128,1024]{1,0:T(8,128)(2,1)S(1)}, u32[]{:S(2)}, u32[]{:S(2)}) collective-permute-start(bf16[128,1024]{1,0:T(8,128)(2,1)S(1)} %get-tuple-element.50), channel_id=1, source_target_pairs={{0,8},{1,9},{2,10},{3,11},{4,12},{5,13},{6,14},{7,15},{8,16},{9,17... | collective-permute-start | bytes 786440 | tf_op jit(solution)/shard_map/ppermute | solution.py:36
  9.8 7.1 %collective-permute-start.5 = (bf16[128,1024]{1,0:T(8,128)(2,1)S(1)}, bf16[128,1024]{1,0:T(8,128)(2,1)S(1)}, u32[]{:S(2)}, u32[]{:S(2)}) collective-permute-start(bf16[128,1024]{1,0:T(8,128)(2,1)S(1)} %get-tuple-element.51), channel_id=1, source_target_pairs={{0,24},{1,25},{2,26},{3,27},{4,28},{5,29},{6,30},{7,31},{8,0},{9,1... | collective-permute-start | bytes 786440 | tf_op jit(solution)/shard_map/ppermute | solution.py:36
  12.1 8.5 %collective-permute-start.3 = (s16[1024,128]{1,0:T(8,128)(2,1)S(1)}, s16[1024,128]{1,0:T(8,128)(2,1)S(1)}, u32[]{:S(2)}, u32[]{:S(2)}) collective-permute-start(s16[1024,128]{1,0:T(8,128)(2,1)S(1)} %collective-permute-done.refs_4_), channel_id=1, source_target_pairs={{0,3},{1,2},{2,1},{3,0},{4,7},{5,6},{6,5},{7,4},{8,11},{9,10},{10,... | collective-permute-start | bytes 786440 | tf_op jit(solution)/shard_map/ppermute | solution.py:36
  14.7 10.9 %collective-permute-start.2 = (s16[1024,128]{1,0:T(8,128)(2,1)S(1)}, s16[1024,128]{1,0:T(8,128)(2,1)S(1)}, u32[]{:S(2)}, u32[]{:S(2)}) collective-permute-start(s16[1024,128]{1,0:T(8,128)(2,1)S(1)} %collective-permute-done.refs_4_), channel_id=1, source_target_pairs={{0,2},{1,3},{2,0},{3,1},{4,6},{5,7},{6,4},{7,5},{8,10},{9,11},{10,... | collective-permute-start | bytes 786440 | tf_op jit(solution)/shard_map/ppermute | solution.py:36
  15.1 12.9 %collective-permute-start.1 = (s16[1024,128]{1,0:T(8,128)(2,1)S(1)}, s16[1024,128]{1,0:T(8,128)(2,1)S(1)}, u32[]{:S(2)}, u32[]{:S(2)}) collective-permute-start(s16[1024,128]{1,0:T(8,128)(2,1)S(1)} %collective-permute-done.refs_4_), channel_id=1, source_target_pairs={{0,1},{1,0},{2,3},{3,2},{4,5},{5,4},{6,7},{7,6},{8,9},{9,8},{10,11... | collective-permute-start | bytes 786440 | tf_op jit(solution)/shard_map/ppermute | solution.py:36
  28.0 2.4 %collective-permute-start.8 = (s16[1024,128]{1,0:T(8,128)(2,1)S(1)}, s16[1024,128]{1,0:T(8,128)(2,1)S(1)}, u32[]{:S(2)}, u32[]{:S(2)}) collective-permute-start(s16[1024,128]{1,0:T(8,128)(2,1)S(1)} %collective-permute-done.refs_4_), channel_id=1, source_target_pairs={{0,8},{1,9},{2,10},{3,11},{4,12},{5,13},{6,14},{7,15},{8,0},{9,1},... | collective-permute-start | bytes 786440 | tf_op jit(solution)/shard_map/ppermute | solution.py:36
  28.1 2.3 %collective-permute-start.9 = (s16[1024,128]{1,0:T(8,128)(2,1)S(1)}, s16[1024,128]{1,0:T(8,128)(2,1)S(1)}, u32[]{:S(2)}, u32[]{:S(2)}) collective-permute-start(s16[1024,128]{1,0:T(8,128)(2,1)S(1)} %collective-permute-done.1.refs_5_), channel_id=1, source_target_pairs={{0,8},{1,9},{2,10},{3,11},{4,12},{5,13},{6,14},{7,15},{8,0},{9,1},... | collective-permute-start | bytes 786440 | tf_op jit(solution)/shard_map/ppermute | solution.py:36
  29.1 26.8 %collective-permute-start.7 = (bf16[384,1024]{1,0:T(8,128)(2,1)S(1)}, bf16[384,1024]{1,0:T(8,128)(2,1)S(1)}, u32[]{:S(2)}, u32[]{:S(2)}) collective-permute-start(bf16[384,1024]{1,0:T(8,128)(2,1)S(1)} %pad_maximum_fusion.refs_0_), channel_id=1, source_target_pairs={{0,1},{1,0},{2,3},{3,2},{4,5},{5,4},{6,7},{7,6},{8,9},{9,8},{10,11... | collective-permute-start | bytes 2359304 | tf_op jit(solution)/shard_map/ppermute | solution.py:36
  41.3 9.0 %collective-permute-start.20 = (bf16[128,1024]{1,0:T(8,128)(2,1)S(1)}, bf16[128,1024]{1,0:T(8,128)(2,1)S(1)}, u32[]{:S(2)}, u32[]{:S(2)}) collective-permute-start(bf16[128,1024]{1,0:T(8,128)(2,1)S(1)} %sign_rows.1), channel_id=1, source_target_pairs={{0,6},{1,7},{2,4},{3,5},{4,14},{5,15},{6,12},{7,13},{8,2},{9,3},{1... | collective-permute-start | bytes 786440 | tf_op jit(solution)/shard_map/ppermute | solution.py:36
  43.4 12.4 %collective-permute-start.19 = (bf16[128,1024]{1,0:T(8,128)(2,1)S(1)}, bf16[128,1024]{1,0:T(8,128)(2,1)S(1)}, u32[]{:S(2)}, u32[]{:S(2)}) collective-permute-start(bf16[128,1024]{1,0:T(8,128)(2,1)S(1)} %sign_rows.1), channel_id=1, source_target_pairs={{0,2},{1,3},{2,0},{3,1},{4,10},{5,11},{6,8},{7,9},{8,6},{9,7},{10,... | collective-permute-start | bytes 786440 | tf_op jit(solution)/shard_map/ppermute | solution.py:36
  43.5 17.6 %collective-permute-start.13 = (bf16[128,1024]{1,0:T(8,128)(2,1)S(1)}, bf16[128,1024]{1,0:T(8,128)(2,1)S(1)}, u32[]{:S(2)}, u32[]{:S(2)}) collective-permute-start(bf16[128,1024]{1,0:T(8,128)(2,1)S(1)} %sign_rows.1), channel_id=1, source_target_pairs={{0,4},{1,5},{2,6},{3,7},{4,12},{5,13},{6,14},{7,15},{8,0},{9,1},{1... | collective-permute-start | bytes 786440 | tf_op jit(solution)/shard_map/ppermute | solution.py:36
  44.5 20.6 %collective-permute-start.12 = (bf16[128,1024]{1,0:T(8,128)(2,1)S(1)}, bf16[128,1024]{1,0:T(8,128)(2,1)S(1)}, u32[]{:S(2)}, u32[]{:S(2)}) collective-permute-start(bf16[128,1024]{1,0:T(8,128)(2,1)S(1)} %sign_rows.1), channel_id=1, source_target_pairs={{0,0},{1,1},{2,2},{3,3},{4,8},{5,9},{6,10},{7,11},{8,4},{9,5},{10,... | collective-permute-start | bytes 786440 | tf_op jit(solution)/shard_map/ppermute | solution.py:36
  56.9 12.3 %collective-permute-start.21 = (bf16[128,256]{1,0:T(8,128)(2,1)S(1)}, bf16[128,256]{1,0:T(8,128)(2,1)S(1)}, u32[]{:S(2)}, u32[]{:S(2)}) collective-permute-start(bf16[128,256]{1,0:T(8,128)(2,1)S(1)} %get-tuple-element.43), channel_id=1, source_target_pairs={{0,8},{1,9},{2,10},{3,11},{4,12},{5,13},{6,14},{7,15},{8,16},{9,17... | collective-permute-start | bytes 196616 | tf_op jit(solution)/shard_map/ppermute | solution.py:36
  56.9 12.3 %collective-permute-start.22 = (bf16[128,256]{1,0:T(8,128)(2,1)S(1)}, bf16[128,256]{1,0:T(8,128)(2,1)S(1)}, u32[]{:S(2)}, u32[]{:S(2)}) collective-permute-start(bf16[128,256]{1,0:T(8,128)(2,1)S(1)} %get-tuple-element.44), channel_id=1, source_target_pairs={{0,9},{1,8},{2,11},{3,10},{4,13},{5,12},{6,15},{7,14},{8,17},{9,16... | collective-permute-start | bytes 196616 | tf_op jit(solution)/shard_map/ppermute | solution.py:36
  59.1 11.9 %collective-permute-start.23 = (bf16[128,256]{1,0:T(8,128)(2,1)S(1)}, bf16[128,256]{1,0:T(8,128)(2,1)S(1)}, u32[]{:S(2)}, u32[]{:S(2)}) collective-permute-start(bf16[128,256]{1,0:T(8,128)(2,1)S(1)} %get-tuple-element.46), channel_id=1, source_target_pairs={{0,1},{1,0},{2,3},{3,2},{4,5},{5,4},{6,7},{7,6},{8,9},{9,8},{10,11... | collective-permute-start | bytes 196616 | tf_op jit(solution)/shard_map/ppermute | solution.py:36
  61.0 11.5 %collective-permute-start.24 = (bf16[128,256]{1,0:T(8,128)(2,1)S(1)}, bf16[128,256]{1,0:T(8,128)(2,1)S(1)}, u32[]{:S(2)}, u32[]{:S(2)}) collective-permute-start(bf16[128,256]{1,0:T(8,128)(2,1)S(1)} %get-tuple-element.47), channel_id=1, source_target_pairs={{0,24},{1,25},{2,26},{3,27},{4,28},{5,29},{6,30},{7,31},{8,0},{9,1... | collective-permute-start | bytes 196616 | tf_op jit(solution)/shard_map/ppermute | solution.py:36
  65.1 7.4 %collective-permute-start.25 = (bf16[128,256]{1,0:T(8,128)(2,1)S(1)}, bf16[128,256]{1,0:T(8,128)(2,1)S(1)}, u32[]{:S(2)}, u32[]{:S(2)}) collective-permute-start(bf16[128,256]{1,0:T(8,128)(2,1)S(1)} %get-tuple-element.48), channel_id=1, source_target_pairs={{0,25},{1,24},{2,27},{3,26},{4,29},{5,28},{6,31},{7,30},{8,1},{9,0... | collective-permute-start | bytes 196616 | tf_op jit(solution)/shard_map/ppermute | solution.py:36
  69.2 3.8 %collective-permute-start.14 = (bf16[128,256]{1,0:T(8,128)(2,1)S(1)}, bf16[128,256]{1,0:T(8,128)(2,1)S(1)}, u32[]{:S(2)}, u32[]{:S(2)}) collective-permute-start(bf16[128,256]{1,0:T(8,128)(2,1)S(1)} %get-tuple-element.37), channel_id=1, source_target_pairs={{0,8},{1,9},{2,10},{3,11},{4,12},{5,13},{6,14},{7,15},{8,16},{9,17... | collective-permute-start | bytes 196616 | tf_op jit(solution)/shard_map/ppermute | solution.py:36
  69.3 4.7 %collective-permute-start.15 = (bf16[128,256]{1,0:T(8,128)(2,1)S(1)}, bf16[128,256]{1,0:T(8,128)(2,1)S(1)}, u32[]{:S(2)}, u32[]{:S(2)}) collective-permute-start(bf16[128,256]{1,0:T(8,128)(2,1)S(1)} %get-tuple-element.38), channel_id=1, source_target_pairs={{0,9},{1,8},{2,11},{3,10},{4,13},{5,12},{6,15},{7,14},{8,17},{9,16... | collective-permute-start | bytes 196616 | tf_op jit(solution)/shard_map/ppermute | solution.py:36
  71.0 5.4 %collective-permute-start.16 = (bf16[128,256]{1,0:T(8,128)(2,1)S(1)}, bf16[128,256]{1,0:T(8,128)(2,1)S(1)}, u32[]{:S(2)}, u32[]{:S(2)}) collective-permute-start(bf16[128,256]{1,0:T(8,128)(2,1)S(1)} %get-tuple-element.40), channel_id=1, source_target_pairs={{0,1},{1,0},{2,3},{3,2},{4,5},{5,4},{6,7},{7,6},{8,9},{9,8},{10,11... | collective-permute-start | bytes 196616 | tf_op jit(solution)/shard_map/ppermute | solution.py:36
  72.5 3.9 %collective-permute-start.17 = (bf16[128,256]{1,0:T(8,128)(2,1)S(1)}, bf16[128,256]{1,0:T(8,128)(2,1)S(1)}, u32[]{:S(2)}, u32[]{:S(2)}) collective-permute-start(bf16[128,256]{1,0:T(8,128)(2,1)S(1)} %get-tuple-element.41), channel_id=1, source_target_pairs={{0,24},{1,25},{2,26},{3,27},{4,28},{5,29},{6,30},{7,31},{8,0},{9,1... | collective-permute-start | bytes 196616 | tf_op jit(solution)/shard_map/ppermute | solution.py:36
  72.5 4.2 %collective-permute-start.18 = (bf16[128,256]{1,0:T(8,128)(2,1)S(1)}, bf16[128,256]{1,0:T(8,128)(2,1)S(1)}, u32[]{:S(2)}, u32[]{:S(2)}) collective-permute-start(bf16[128,256]{1,0:T(8,128)(2,1)S(1)} %get-tuple-element.42), channel_id=1, source_target_pairs={{0,25},{1,24},{2,27},{3,26},{4,29},{5,28},{6,31},{7,30},{8,1},{9,0... | collective-permute-start | bytes 196616 | tf_op jit(solution)/shard_map/ppermute | solution.py:36
  (7 other events, 42.3 us)

commit v4 on v3

--- a/solution.py
+++ b/solution.py
@@ -14,6 +14,7 @@
 LARGEST = 0.09375
 CODES = 32766.0
 VMEM = pl.BlockSpec(memory_space=pltpu.VMEM)
+HBM = pl.BlockSpec(memory_space=pltpu.HBM)
 SMEM = pl.BlockSpec(memory_space=pltpu.SMEM)
 
 
@@ -31,34 +32,58 @@
     def send(self, array, target):
         moves = []
         for row, col in self.devices:
+            if target(row, col) is None:
+                continue
             to_row, to_col = target(row, col)
             moves.append((row * self.cols + col, to_row % self.rows * self.cols + to_col))
         return lax.ppermute(array, AXES, moves)
 
 
-def prepare_kernel(ham_ref, pattern_ref, out_ref):
-    across, blocks = pattern_ref.shape
-    width = out_ref.shape[1]
+def prepare_kernel(pieces, ham_hbm, pattern_hbm, out_hbm, ham, pattern, out, in_sems, out_sems):
+    across, blocks = pattern.shape
+    height, width = ham.shape
+    part = height // pieces
+    incoming = [pltpu.make_async_copy(pattern_hbm, pattern, in_sems.at[pieces])]
+    outgoing = []
+    for p in range(pieces):
+        rows = pl.ds(p * part, part)
+        incoming.append(pltpu.make_async_copy(ham_hbm.at[rows], ham.at[rows], in_sems.at[p]))
+        outgoing.append(pltpu.make_async_copy(out.at[rows], out_hbm.at[rows], out_sems.at[p]))
+    for copy in incoming:
+        copy.start()
+    incoming[0].wait()
     lane = lax.broadcasted_iota(jnp.int32, (across, width), 1) // BLOCK
     spread = (lane == lax.broadcasted_iota(jnp.int32, (across, width), 0)).astype(F32)
     weights = lax.dot_general(
-        pattern_ref[...].astype(F32), spread, (((0,), (0,)), ((), ())), preferred_element_type=F32
-    )
-    for a in range(blocks):
-        rows = slice(a * BLOCK, (a + 1) * BLOCK)
-        entry = ham_ref[rows, :] * weights[a : a + 1, :]
-        root = jnp.sqrt(jnp.sqrt(jnp.abs(entry) * (1.0 / LARGEST)))
-        code = (root * CODES + 0.5).astype(jnp.int32)
-        out_ref[rows, :] = jnp.where(entry < 0.0, -code, code).astype(jnp.int16)
+        pattern[...].astype(F32), spread, (((0,), (0,)), ((), ())), preferred_element_type=F32
+    )
+    for p in range(pieces):
+        incoming[p + 1].wait()
+        for a in range(p * blocks // pieces, (p + 1) * blocks // pieces):
+            rows = slice(a * BLOCK, (a + 1) * BLOCK)
+            entry = ham[rows, :] * weights[a : a + 1, :]
+            root = jnp.sqrt(jnp.sqrt(jnp.abs(entry) * (1.0 / LARGEST)))
+            code = (root * CODES + 0.5).astype(jnp.int32)
+            out[rows, :] = jnp.where(entry < 0.0, -code, code).astype(jnp.int16)
+        outgoing[p].start()
+    for copy in outgoing:
+        copy.wait()
 
 
 def prepare(hamiltonian, pattern):
+    pieces = 4
     return pl.pallas_call(
-        prepare_kernel,
+        lambda *refs: prepare_kernel(pieces, *refs),
         out_shape=jax.ShapeDtypeStruct(hamiltonian.shape, jnp.int16),
-        in_specs=[VMEM, VMEM],
-        out_specs=VMEM,
-        compiler_params=pltpu.CompilerParams(vmem_limit_bytes=8 * 2**20),
+        in_specs=[HBM, HBM],
+        out_specs=HBM,
+        scratch_shapes=[
+            pltpu.VMEM(hamiltonian.shape, F32),
+            pltpu.VMEM(pattern.shape[::-1], jnp.int32),
+            pltpu.VMEM(hamiltonian.shape, jnp.int16),
+            pltpu.SemaphoreType.DMA((pieces + 1,)),
+            pltpu.SemaphoreType.DMA((pieces,)),
+        ],
         name="prepare",
     )(hamiltonian, pattern.T)
 
@@ -132,27 +157,34 @@
     )(slot, active, mask_row[None], diag_row[None], *shards)
 
 
-def products_kernel(count, sides, *refs):
-    signs, outs = refs[2 : 2 + count], refs[2 + count :]
-    own = signs[0].shape[0]
-    for k in range(count):
+def products_kernel(sources, sides, *refs):
+    signs, outs = refs[2 : -2 * sides], refs[-2 * sides :]
+    own = outs[0].shape[0]
+    for k, source in enumerate(sources):
         cols = slice(k * own, (k + 1) * own)
+        shard = sum(signs[i][j * own : (j + 1) * own, :] for i, j in source)
         for j in range(2):
-            prod = lax.dot_general(refs[j][...], signs[k][...], LAST, preferred_element_type=F32)
+            prod = lax.dot_general(refs[j][...], shard, LAST, preferred_element_type=F32)
             for side in range(sides):
                 out = outs[j * sides + side]
                 out[:, cols] = prod[side * own : (side + 1) * own].astype(out.dtype)
 
 
-def products(trio, mates, signs):
-    count = len(signs)
-    own, width = signs[0].shape
+def products(trio, mates, sources, own):
+    arrays = []
+    for source in sources:
+        arrays += [a for a, _ in source if all(a is not b for b in arrays)]
+    indices = [
+        [(next(i for i, b in enumerate(arrays) if b is a), j) for a, j in source]
+        for source in sources
+    ]
+    count, width = len(sources), trio.shape[1]
     sides = trio.shape[0] // own
     kinds = [F32 if k == 1 else BF16 for k in range(2 * sides)]
     return pl.pallas_call(
-        lambda *refs: products_kernel(count, sides, *refs),
+        lambda *refs: products_kernel(indices, sides, *refs),
         out_shape=[jax.ShapeDtypeStruct((own, count * own), kind) for kind in kinds],
-        in_specs=[VMEM] * (2 + count),
+        in_specs=[VMEM] * (2 + len(arrays)),
         out_specs=[VMEM] * (2 * sides),
         compiler_params=pltpu.CompilerParams(vmem_limit_bytes=24 * 2**20),
         cost_estimate=pl.CostEstimate(
@@ -161,21 +193,24 @@
             transcendentals=0,
         ),
         name="products",
-    )(trio, mates, *signs)
+    )(trio, mates, *arrays)
 
 
 def final_kernel(groups, own, slot_ref, *refs):
-    out_ref = refs[-1]
-    at = 0
-    for steps in groups:
-        for side in range(3):
+    out_hbm, out_ref, sems = refs[-3:]
+    copies = []
+    for side in range(3):
+        for group, steps in enumerate(groups):
             for mate in range(2):
-                part = refs[at]
-                at += 1
+                part = refs[(group * 3 + side) * 2 + mate]
                 for k, step in enumerate(steps):
                     start = pl.multiple_of((slot_ref[0] ^ (step + mate)) * own, own)
                     block = part[:, k * own : (k + 1) * own]
                     out_ref[side, :, pl.ds(start, own)] = block.astype(F32)
+        copies.append(pltpu.make_async_copy(out_ref.at[side], out_hbm.at[side], sems.at[side]))
+        copies[side].start()
+    for copy in copies:
+        copy.wait()
 
 
 def final(slot, groups, parts, width):
@@ -185,7 +220,8 @@
         lambda *refs: final_kernel(groups, own, *refs),
         out_shape=jax.ShapeDtypeStruct((3, own, width), F32),
         in_specs=[SMEM] + [VMEM] * len(flat),
-        out_specs=VMEM,
+        out_specs=HBM,
+        scratch_shapes=[pltpu.VMEM((3, own, width), F32), pltpu.SemaphoreType.DMA((3,))],
         compiler_params=pltpu.CompilerParams(vmem_limit_bytes=24 * 2**20),
         cost_estimate=pl.CostEstimate(
             flops=0, bytes_accessed=24 * own * width, transcendentals=0
@@ -206,8 +242,8 @@
         return (r, c) if c // half == r % 2 else (r ^ 1, c ^ half)
 
     masked = prepare(hamiltonian, pattern)
-    masked, onsite = lax.optimization_barrier((masked, onsite))
     held = send(masked, home)
+    held, onsite = lax.optimization_barrier((held, onsite))
     parts = [held]
     for step in range(1, half):
         parts.append(send(held, lambda r, c, step=step: (r, c ^ step)))
@@ -224,29 +260,42 @@
     )
     mask_row = jnp.repeat(jnp.any(chosen, axis=1).astype(F32), BLOCK)
     diag_row = onsite_of(onsite, place, team, row) * mask_row
-    parts, mask_row, diag_row, above, below = lax.optimization_barrier(
-        (parts, mask_row, diag_row, above, below)
-    )
+    parts += [send(part, lambda r, c: (r ^ 1, c)) for part in parts]
+    last, mask_row, diag_row, above, below = lax.optimization_barrier(
+        (parts[half - 1], mask_row, diag_row, above, below)
+    )
+    parts[half - 1] = last
     trio = jnp.concatenate([above, invs[1], below], axis=0)
     mates = send(trio, lambda r, c: (r, c ^ 1))
-    parts += [send(part, lambda r, c: (r ^ 1, c)) for part in parts]
     signs = sign_rows(
         parts, slot.astype(jnp.int32)[None], group_order[None], mask_row, diag_row
     )
 
-    mine = []
-    for step in range(0, cols, 2):
-
-        def target(r, c, step=step):
+    def at_step(step, within):
+        def target(r, c):
             team, slot = place.work(r, c)
-            return (team, slot ^ step)
-
-        mine.append(send(signs, target))
-    order = sorted(range(half), key=lambda k: k % 2)
-    groups, placed = [], []
-    for chosen_steps in (order[: half // 2], order[half // 2 :]):
-        groups.append([2 * k for k in chosen_steps])
-        out = products(trio, mates, [mine[k] for k in chosen_steps])
+            same = (slot ^ step) // half == c // half
+            return (team, slot ^ step) if same or not within else None
+
+        return target
+
+    def onward(step):
+        return lambda r, c: (r, c ^ step) if c // half != r % 2 else None
+
+    steps = range(2, half, 2)
+    first = [send(signs, at_step(0, False)), send(signs, at_step(half, False))]
+    near = [[send(signs, at_step(k ^ j, True)) for j in (0, half)] for k in steps]
+    pair, near, mates = lax.optimization_barrier((jnp.concatenate(first, axis=0), near, mates))
+    far = [send(pair, onward(k)) for k in steps]
+    own = signs.shape[0]
+    groups, sources = [[0, half]], [[[(part, 0)] for part in first]]
+    groups.append([k ^ j for k in steps for j in (0, half)])
+    sources.append(
+        [[(near[i][j], 0), (far[i], j)] for i in range(len(near)) for j in range(2)]
+    )
+    placed = []
+    for source in sources:
+        out = products(trio, mates, source, own)
         placed.append(
             [
                 [

time: 78.7 us -> 76.8 us (0.976)
  waiting for transfers between devices: 26.7 us -> 17 us
  starting transfers between devices: 32.3 us -> 40.6 us
  local copies, waits for them, and re-layouts: 3.65 us -> 1.91 us
  Pallas kernels: 14.5 us -> 16 us
    ppermute x26 -> x27, waiting for transfers between devices: 26.7 us -> 17 us  [send(): return lax.ppermute(array, AXES, moves)]
    ppermute x26 -> x27, starting transfers between devices: 32.3 us -> 40.6 us  [send(): return lax.ppermute(array, AXES, moves)]
    unnamed x10 -> x6, local copies, waits for them, and re-layouts: 1.76 us -> 0.01 us
    pallas_call x3, Pallas kernels: 2.54 us -> 4.08 us  [the longest x1 2.15 us: prepare(): pl.pallas_call(lambda *refs: prepare_kernel(pieces, *refs), out_shape=jax...]
  transfers between devices with their start and end apart: 26 -> 27, of which waited for: 10 -> 8; matrix products, arithmetic and copies ran while one was open for 3% -> 4% of each run, Pallas kernels for 16% -> 16%
where the time goes in v4:
time: 76.8 us; the launch traced here: 76.5 us
  starting transfers between devices  40.6 us (53%)
  waiting for transfers between devices  17 us (22%)
  Pallas kernels  16 us (21%)
  local copies, waits for them, and re-layouts  1.91 us (2%)
  other arithmetic  0.86 us (1%)
    ppermute x27, starting transfers between devices, send(): return lax.ppermute(array, AXES, moves)  40.6 us
    ppermute x27, waiting for transfers between devices, send(): return lax.ppermute(array, AXES, moves)  17 us
    pallas_call x1, Pallas kernels, sign_rows(): pl.pallas_call(lambda *refs: sign_kernel(count, *refs), out_shape=jax.Sha...  10.7 us
    pallas_call x1, Pallas kernels, prepare(): pl.pallas_call(lambda *refs: prepare_kernel(pieces, *refs), out_shape=jax...  2.15 us
    pallas_call x2, Pallas kernels, products(): pl.pallas_call(lambda *refs: products_kernel(indices, sides, *refs), out_...  1.93 us
  transfers between devices with their start and end apart: 27, of which 8 were waited for; matrix products, arithmetic and copies ran while one was open for 4% of the time, Pallas kernels for 16%

profile of v4, /device:TPU:0, one launch (start us, length us, event | category | flops | bytes accessed | tf_op | source)
XLA Modules:
  0.0 76.5 jit_solution(1511638729030287030)
XLA Ops:
  0.0 2.1 %prepare.1 = s16[1024,128]{1,0:T(8,128)(2,1)} custom-call(f32[1024,128]{1,0:T(8,128)} %refs_0_.1, s32[4,32]{1,0:T(4,128)} %bitcast.19), custom_call_target="tpu_custom_call" | custom-call | tf_op jit(solution)/shard_map/prepare/pallas_call | solution.py:75
  2.2 1.6 %collective-permute-start = (s16[1024,128]{1,0:T(8,128)(2,1)}, s16[1024,128]{1,0:T(8,128)(2,1)S(1)}, u32[]{:S(2)}, u32[]{:S(2)}) collective-permute-start(s16[1024,128]{1,0:T(8,128)(2,1)} %prepare.1), channel_id=1, source_target_pairs={{0,0},{1,1},{2,2},{3,3},{4,8},{5,9},{6,10},{7,11},{8,4},{9,5},{10,... | collective-permute-start | bytes 786440 | tf_op jit(solution)/shard_map/ppermute | solution.py:39
  4.9 4.5 %collective-permute-start.4 = (bf16[128,1024]{1,0:T(8,128)(2,1)S(1)}, bf16[128,1024]{1,0:T(8,128)(2,1)S(1)}, u32[]{:S(2)}, u32[]{:S(2)}) collective-permute-start(bf16[128,1024]{1,0:T(8,128)(2,1)S(1)} %get-tuple-element.52), channel_id=1, source_target_pairs={{0,8},{1,9},{2,10},{3,11},{4,12},{5,13},{6,14},{7,15},{8,16},{9,17... | collective-permute-start | bytes 786440 | tf_op jit(solution)/shard_map/ppermute | solution.py:39
  9.4 1.2 %collective-permute-start.3 = (bf16[128,1024]{1,0:T(8,128)(2,1)S(1)}, bf16[128,1024]{1,0:T(8,128)(2,1)S(1)}, u32[]{:S(2)}, u32[]{:S(2)}) collective-permute-start(bf16[128,1024]{1,0:T(8,128)(2,1)S(1)} %get-tuple-element.53), channel_id=1, source_target_pairs={{0,24},{1,25},{2,26},{3,27},{4,28},{5,29},{6,30},{7,31},{8,0},{9,1... | collective-permute-start | bytes 786440 | tf_op jit(solution)/shard_map/ppermute | solution.py:39
  10.6 1.6 %collective-permute-start.6 = (s16[1024,128]{1,0:T(8,128)(2,1)S(1)}, s16[1024,128]{1,0:T(8,128)(2,1)S(1)}, u32[]{:S(2)}, u32[]{:S(2)}) collective-permute-start(s16[1024,128]{1,0:T(8,128)(2,1)S(1)} %collective-permute-done.refs_4_), channel_id=1, source_target_pairs={{0,2},{1,3},{2,0},{3,1},{4,6},{5,7},{6,4},{7,5},{8,10},{9,11},{10,... | collective-permute-start | bytes 786440 | tf_op jit(solution)/shard_map/ppermute | solution.py:39
  12.2 1.5 %collective-permute-start.5 = (s16[1024,128]{1,0:T(8,128)(2,1)S(1)}, s16[1024,128]{1,0:T(8,128)(2,1)S(1)}, u32[]{:S(2)}, u32[]{:S(2)}) collective-permute-start(s16[1024,128]{1,0:T(8,128)(2,1)S(1)} %collective-permute-done.refs_4_), channel_id=1, source_target_pairs={{0,1},{1,0},{2,3},{3,2},{4,5},{5,4},{6,7},{7,6},{8,9},{9,8},{10,11... | collective-permute-start | bytes 786440 | tf_op jit(solution)/shard_map/ppermute | solution.py:39
  15.4 1.2 %collective-permute-done.4 = bf16[128,1024]{1,0:T(8,128)(2,1)S(1)} collective-permute-done((bf16[128,1024]{1,0:T(8,128)(2,1)S(1)}, bf16[128,1024]{1,0:T(8,128)(2,1)S(1)}, u32[]{:S(2)}, u32[]{:S(2)}) %collective-permute-start.4) | collective-permute-done | bytes 262176 | tf_op jit(solution)/shard_map/ppermute | solution.py:39
  16.5 2.8 %collective-permute-start.2 = (f32[1024]{0:T(1024)S(1)}, f32[1024]{0:T(1024)S(1)}, u32[]{:S(2)}, u32[]{:S(2)}) collective-permute-start(f32[1024]{0:T(1024)S(1)} %copy-done.1), channel_id=1, source_target_pairs={{0,8},{1,9},{2,10},{3,11},{4,12},{5,13},{6,14},{7,15},{8,0},{9,1},... | collective-permute-start | bytes 12296 | tf_op jit(solution)/shard_map/ppermute | solution.py:39
  20.6 3.2 %collective-permute-start.9 = (s16[1024,128]{1,0:T(8,128)(2,1)S(1)}, s16[1024,128]{1,0:T(8,128)(2,1)S(1)}, u32[]{:S(2)}, u32[]{:S(2)}) collective-permute-start(s16[1024,128]{1,0:T(8,128)(2,1)S(1)} %collective-permute-done.6.refs_6_), channel_id=1, source_target_pairs={{0,8},{1,9},{2,10},{3,11},{4,12},{5,13},{6,14},{7,15},{8,0},{9,1},... | collective-permute-start | bytes 786440 | tf_op jit(solution)/shard_map/ppermute | solution.py:39
  23.8 2.4 %collective-permute-start.8 = (s16[1024,128]{1,0:T(8,128)(2,1)S(1)}, s16[1024,128]{1,0:T(8,128)(2,1)S(1)}, u32[]{:S(2)}, u32[]{:S(2)}) collective-permute-start(s16[1024,128]{1,0:T(8,128)(2,1)S(1)} %collective-permute-done.5.refs_5_), channel_id=1, source_target_pairs={{0,8},{1,9},{2,10},{3,11},{4,12},{5,13},{6,14},{7,15},{8,0},{9,1},... | collective-permute-start | bytes 786440 | tf_op jit(solution)/shard_map/ppermute | solution.py:39
  26.1 1.2 %collective-permute-start.10 = (s16[1024,128]{1,0:T(8,128)(2,1)S(1)}, s16[1024,128]{1,0:T(8,128)(2,1)S(1)}, u32[]{:S(2)}, u32[]{:S(2)}) collective-permute-start(s16[1024,128]{1,0:T(8,128)(2,1)S(1)} %collective-permute-done.1.refs_7_), channel_id=1, source_target_pairs={{0,8},{1,9},{2,10},{3,11},{4,12},{5,13},{6,14},{7,15},{8,0},{9,1},... | collective-permute-start | bytes 786440 | tf_op jit(solution)/shard_map/ppermute | solution.py:39
  28.5 10.7 %sign_rows.1 = bf16[128,1024]{1,0:T(8,128)(2,1)S(1)} custom-call(s32[1]{0:T(128)} %bitcast.8.refs_0_, s32[1]{0:T(128)} %dynamic_slice.9.refs_1_, f32[1,1024]{1,0:T(1,128)S(1)} %bitcast.16, f32[1,1024]{1,0:T(1,128)S(1)} %bitcast.17, s16[1024,128]{1,0:T(8,128)(2,1)S(1)} %collective-permute-done.refs_4_, s16[1024,128]{1,0:T(8,128)(2,1)S(1)} %collective-permute-done.5.refs_5_, ...), custom_call_target="tpu_custom_call" | custom-call | flops 9395240960 | bytes 2097152 | tf_op jit(solution)/shard_map/sign_rows/pallas_call | solution.py:142
  39.2 2.3 %collective-permute-start.12 = (bf16[128,1024]{1,0:T(8,128)(2,1)S(1)}, bf16[128,1024]{1,0:T(8,128)(2,1)S(1)}, u32[]{:S(2)}, u32[]{:S(2)}) collective-permute-start(bf16[128,1024]{1,0:T(8,128)(2,1)S(1)} %sign_rows.1), channel_id=1, source_target_pairs={{0,4},{1,5},{2,6},{3,7},{4,12},{5,13},{6,14},{7,15},{8,0},{9,1},{1... | collective-permute-start | bytes 786440 | tf_op jit(solution)/shard_map/ppermute | solution.py:39
  42.2 1.3 %collective-permute-start.14 = (bf16[128,1024]{1,0:T(8,128)(2,1)S(1)}, bf16[128,1024]{1,0:T(8,128)(2,1)S(1)}, u32[]{:S(2)}, u32[]{:S(2)}) collective-permute-start(bf16[128,1024]{1,0:T(8,128)(2,1)S(1)} %sign_rows.1), channel_id=1, source_target_pairs={{4,14},{5,15},{6,12},{7,13},{8,2},{9,3},{10,0},{11,1},{20,30},{21,... | collective-permute-start | bytes 786440 | tf_op jit(solution)/shard_map/ppermute | solution.py:39
  43.5 2.7 %collective-permute-start.13 = (bf16[128,1024]{1,0:T(8,128)(2,1)S(1)}, bf16[128,1024]{1,0:T(8,128)(2,1)S(1)}, u32[]{:S(2)}, u32[]{:S(2)}) collective-permute-start(bf16[128,1024]{1,0:T(8,128)(2,1)S(1)} %sign_rows.1), channel_id=1, source_target_pairs={{0,2},{1,3},{2,0},{3,1},{12,14},{13,15},{14,12},{15,13},{16,18},{1... | collective-permute-start | bytes 786440 | tf_op jit(solution)/shard_map/ppermute | solution.py:39
  46.9 9.6 %collective-permute-done.14.refs_4_ = bf16[128,1024]{1,0:T(8,128)(2,1)S(1)} collective-permute-done((bf16[128,1024]{1,0:T(8,128)(2,1)S(1)}, bf16[128,1024]{1,0:T(8,128)(2,1)S(1)}, u32[]{:S(2)}, u32[]{:S(2)}) %collective-permute-start.14) | collective-permute-done | bytes 262176 | tf_op jit(solution)/shard_map/ppermute | solution.py:39
  56.5 1.7 %collective-permute-done.13.refs_2_ = bf16[128,1024]{1,0:T(8,128)(2,1)S(1)} collective-permute-done((bf16[128,1024]{1,0:T(8,128)(2,1)S(1)}, bf16[128,1024]{1,0:T(8,128)(2,1)S(1)}, u32[]{:S(2)}, u32[]{:S(2)}) %collective-permute-start.13) | collective-permute-done | bytes 262176 | tf_op jit(solution)/shard_map/ppermute | solution.py:39
  59.9 2.5 %collective-permute-start.17 = (bf16[128,256]{1,0:T(8,128)(2,1)S(1)}, bf16[128,256]{1,0:T(8,128)(2,1)S(1)}, u32[]{:S(2)}, u32[]{:S(2)}) collective-permute-start(bf16[128,256]{1,0:T(8,128)(2,1)S(1)} %get-tuple-element.37), channel_id=1, source_target_pairs={{0,9},{1,8},{2,11},{3,10},{4,13},{5,12},{6,15},{7,14},{8,17},{9,16... | collective-permute-start | bytes 196616 | tf_op jit(solution)/shard_map/ppermute | solution.py:39
  63.2 3.7 %collective-permute-start.20 = (bf16[128,256]{1,0:T(8,128)(2,1)S(1)}, bf16[128,256]{1,0:T(8,128)(2,1)S(1)}, u32[]{:S(2)}, u32[]{:S(2)}) collective-permute-start(bf16[128,256]{1,0:T(8,128)(2,1)S(1)} %get-tuple-element.41), channel_id=1, source_target_pairs={{0,25},{1,24},{2,27},{3,26},{4,29},{5,28},{6,31},{7,30},{8,1},{9,0... | collective-permute-start | bytes 196616 | tf_op jit(solution)/shard_map/ppermute | solution.py:39
  68.5 1.2 %collective-permute-start.24 = (bf16[128,256]{1,0:T(8,128)(2,1)S(1)}, bf16[128,256]{1,0:T(8,128)(2,1)S(1)}, u32[]{:S(2)}, u32[]{:S(2)}) collective-permute-start(bf16[128,256]{1,0:T(8,128)(2,1)S(1)} %get-tuple-element.48), channel_id=1, source_target_pairs={{0,1},{1,0},{2,3},{3,2},{4,5},{5,4},{6,7},{7,6},{8,9},{9,8},{10,11... | collective-permute-start | bytes 196616 | tf_op jit(solution)/shard_map/ppermute | solution.py:39
  70.9 1.2 %collective-permute-start.26 = (bf16[128,256]{1,0:T(8,128)(2,1)S(1)}, bf16[128,256]{1,0:T(8,128)(2,1)S(1)}, u32[]{:S(2)}, u32[]{:S(2)}) collective-permute-start(bf16[128,256]{1,0:T(8,128)(2,1)S(1)} %get-tuple-element.50), channel_id=1, source_target_pairs={{0,25},{1,24},{2,27},{3,26},{4,29},{5,28},{6,31},{7,30},{8,1},{9,0... | collective-permute-start | bytes 196616 | tf_op jit(solution)/shard_map/ppermute | solution.py:39
  72.7 1.2 %collective-permute-done.24.refs_10_ = bf16[128,256]{1,0:T(8,128)(2,1)S(1)} collective-permute-done((bf16[128,256]{1,0:T(8,128)(2,1)S(1)}, bf16[128,256]{1,0:T(8,128)(2,1)S(1)}, u32[]{:S(2)}, u32[]{:S(2)}) %collective-permute-start.24) | collective-permute-done | bytes 65568 | tf_op jit(solution)/shard_map/ppermute | solution.py:39
  73.8 1.4 %collective-permute-done.26.refs_12_ = bf16[128,256]{1,0:T(8,128)(2,1)S(1)} collective-permute-done((bf16[128,256]{1,0:T(8,128)(2,1)S(1)}, bf16[128,256]{1,0:T(8,128)(2,1)S(1)}, u32[]{:S(2)}, u32[]{:S(2)}) %collective-permute-start.26) | collective-permute-done | bytes 65568 | tf_op jit(solution)/shard_map/ppermute | solution.py:39
  75.3 1.2 %final.1 = f32[3,128,1024]{2,1,0:T(8,128)} custom-call(s32[1]{0:T(128)} %bitcast.refs_0_, bf16[128,256]{1,0:T(8,128)(2,1)S(1)} %collective-permute-done.16.refs_1_, bf16[128,256]{1,0:T(8,128)(2,1)S(1)} %collective-permute-done.17.refs_2_, f32[128,256]{1,0:T(8,128)S(1)} %get-tuple-element.38.refs_3_, bf16[128,256]{1,0:T(8,128)(2,1)S(1)} %collective-permute-done.18.refs_4_, ...), custom_call_target="tpu_custom_call" | custom-call | bytes 3145728 | tf_op jit(solution)/shard_map/final/pallas_call | solution.py:219
  (52 shorter events, 12.4 us)
Async XLA Ops:
  2.2 8.4 %collective-permute-start = (s16[1024,128]{1,0:T(8,128)(2,1)}, s16[1024,128]{1,0:T(8,128)(2,1)S(1)}, u32[]{:S(2)}, u32[]{:S(2)}) collective-permute-start(s16[1024,128]{1,0:T(8,128)(2,1)} %prepare.1), channel_id=1, source_target_pairs={{0,0},{1,1},{2,2},{3,3},{4,8},{5,9},{6,10},{7,11},{8,4},{9,5},{10,... | collective-permute-start | bytes 786440 | tf_op jit(solution)/shard_map/ppermute | solution.py:39
  4.9 11.6 %collective-permute-start.4 = (bf16[128,1024]{1,0:T(8,128)(2,1)S(1)}, bf16[128,1024]{1,0:T(8,128)(2,1)S(1)}, u32[]{:S(2)}, u32[]{:S(2)}) collective-permute-start(bf16[128,1024]{1,0:T(8,128)(2,1)S(1)} %get-tuple-element.52), channel_id=1, source_target_pairs={{0,8},{1,9},{2,10},{3,11},{4,12},{5,13},{6,14},{7,15},{8,16},{9,17... | collective-permute-start | bytes 786440 | tf_op jit(solution)/shard_map/ppermute | solution.py:39
  9.4 17.9 %collective-permute-start.3 = (bf16[128,1024]{1,0:T(8,128)(2,1)S(1)}, bf16[128,1024]{1,0:T(8,128)(2,1)S(1)}, u32[]{:S(2)}, u32[]{:S(2)}) collective-permute-start(bf16[128,1024]{1,0:T(8,128)(2,1)S(1)} %get-tuple-element.53), channel_id=1, source_target_pairs={{0,24},{1,25},{2,26},{3,27},{4,28},{5,29},{6,30},{7,31},{8,0},{9,1... | collective-permute-start | bytes 786440 | tf_op jit(solution)/shard_map/ppermute | solution.py:39
  10.6 9.9 %collective-permute-start.6 = (s16[1024,128]{1,0:T(8,128)(2,1)S(1)}, s16[1024,128]{1,0:T(8,128)(2,1)S(1)}, u32[]{:S(2)}, u32[]{:S(2)}) collective-permute-start(s16[1024,128]{1,0:T(8,128)(2,1)S(1)} %collective-permute-done.refs_4_), channel_id=1, source_target_pairs={{0,2},{1,3},{2,0},{3,1},{4,6},{5,7},{6,4},{7,5},{8,10},{9,11},{10,... | collective-permute-start | bytes 786440 | tf_op jit(solution)/shard_map/ppermute | solution.py:39
  12.2 11.6 %collective-permute-start.5 = (s16[1024,128]{1,0:T(8,128)(2,1)S(1)}, s16[1024,128]{1,0:T(8,128)(2,1)S(1)}, u32[]{:S(2)}, u32[]{:S(2)}) collective-permute-start(s16[1024,128]{1,0:T(8,128)(2,1)S(1)} %collective-permute-done.refs_4_), channel_id=1, source_target_pairs={{0,1},{1,0},{2,3},{3,2},{4,5},{5,4},{6,7},{7,6},{8,9},{9,8},{10,11... | collective-permute-start | bytes 786440 | tf_op jit(solution)/shard_map/ppermute | solution.py:39
  13.7 12.4 %collective-permute-start.1 = (s16[1024,128]{1,0:T(8,128)(2,1)S(1)}, s16[1024,128]{1,0:T(8,128)(2,1)S(1)}, u32[]{:S(2)}, u32[]{:S(2)}) collective-permute-start(s16[1024,128]{1,0:T(8,128)(2,1)S(1)} %collective-permute-done.refs_4_), channel_id=1, source_target_pairs={{0,3},{1,2},{2,1},{3,0},{4,7},{5,6},{6,5},{7,4},{8,11},{9,10},{10,... | collective-permute-start | bytes 786440 | tf_op jit(solution)/shard_map/ppermute | solution.py:39
  20.2 8.3 %collective-permute-start.7 = (s16[1024,128]{1,0:T(8,128)(2,1)S(1)}, s16[1024,128]{1,0:T(8,128)(2,1)S(1)}, u32[]{:S(2)}, u32[]{:S(2)}) collective-permute-start(s16[1024,128]{1,0:T(8,128)(2,1)S(1)} %collective-permute-done.refs_4_), channel_id=1, source_target_pairs={{0,8},{1,9},{2,10},{3,11},{4,12},{5,13},{6,14},{7,15},{8,0},{9,1},... | collective-permute-start | bytes 786440 | tf_op jit(solution)/shard_map/ppermute | solution.py:39
  20.6 7.9 %collective-permute-start.9 = (s16[1024,128]{1,0:T(8,128)(2,1)S(1)}, s16[1024,128]{1,0:T(8,128)(2,1)S(1)}, u32[]{:S(2)}, u32[]{:S(2)}) collective-permute-start(s16[1024,128]{1,0:T(8,128)(2,1)S(1)} %collective-permute-done.6.refs_6_), channel_id=1, source_target_pairs={{0,8},{1,9},{2,10},{3,11},{4,12},{5,13},{6,14},{7,15},{8,0},{9,1},... | collective-permute-start | bytes 786440 | tf_op jit(solution)/shard_map/ppermute | solution.py:39
  23.8 4.7 %collective-permute-start.8 = (s16[1024,128]{1,0:T(8,128)(2,1)S(1)}, s16[1024,128]{1,0:T(8,128)(2,1)S(1)}, u32[]{:S(2)}, u32[]{:S(2)}) collective-permute-start(s16[1024,128]{1,0:T(8,128)(2,1)S(1)} %collective-permute-done.5.refs_5_), channel_id=1, source_target_pairs={{0,8},{1,9},{2,10},{3,11},{4,12},{5,13},{6,14},{7,15},{8,0},{9,1},... | collective-permute-start | bytes 786440 | tf_op jit(solution)/shard_map/ppermute | solution.py:39
  27.4 30.7 %collective-permute-start.15 = (bf16[384,1024]{1,0:T(8,128)(2,1)S(1)}, bf16[384,1024]{1,0:T(8,128)(2,1)S(1)}, u32[]{:S(2)}, u32[]{:S(2)}) collective-permute-start(bf16[384,1024]{1,0:T(8,128)(2,1)S(1)} %pad_maximum_fusion.refs_0_), channel_id=1, source_target_pairs={{0,1},{1,0},{2,3},{3,2},{4,5},{5,4},{6,7},{7,6},{8,9},{9,8},{10,11... | collective-permute-start | bytes 2359304 | tf_op jit(solution)/shard_map/ppermute | solution.py:39
  39.2 7.7 %collective-permute-start.12 = (bf16[128,1024]{1,0:T(8,128)(2,1)S(1)}, bf16[128,1024]{1,0:T(8,128)(2,1)S(1)}, u32[]{:S(2)}, u32[]{:S(2)}) collective-permute-start(bf16[128,1024]{1,0:T(8,128)(2,1)S(1)} %sign_rows.1), channel_id=1, source_target_pairs={{0,4},{1,5},{2,6},{3,7},{4,12},{5,13},{6,14},{7,15},{8,0},{9,1},{1... | collective-permute-start | bytes 786440 | tf_op jit(solution)/shard_map/ppermute | solution.py:39
  41.5 5.4 %collective-permute-start.11 = (bf16[128,1024]{1,0:T(8,128)(2,1)S(1)}, bf16[128,1024]{1,0:T(8,128)(2,1)S(1)}, u32[]{:S(2)}, u32[]{:S(2)}) collective-permute-start(bf16[128,1024]{1,0:T(8,128)(2,1)S(1)} %sign_rows.1), channel_id=1, source_target_pairs={{0,0},{1,1},{2,2},{3,3},{4,8},{5,9},{6,10},{7,11},{8,4},{9,5},{10,... | collective-permute-start | bytes 786440 | tf_op jit(solution)/shard_map/ppermute | solution.py:39
  42.2 14.4 %collective-permute-start.14 = (bf16[128,1024]{1,0:T(8,128)(2,1)S(1)}, bf16[128,1024]{1,0:T(8,128)(2,1)S(1)}, u32[]{:S(2)}, u32[]{:S(2)}) collective-permute-start(bf16[128,1024]{1,0:T(8,128)(2,1)S(1)} %sign_rows.1), channel_id=1, source_target_pairs={{4,14},{5,15},{6,12},{7,13},{8,2},{9,3},{10,0},{11,1},{20,30},{21,... | collective-permute-start | bytes 786440 | tf_op jit(solution)/shard_map/ppermute | solution.py:39
  43.5 14.7 %collective-permute-start.13 = (bf16[128,1024]{1,0:T(8,128)(2,1)S(1)}, bf16[128,1024]{1,0:T(8,128)(2,1)S(1)}, u32[]{:S(2)}, u32[]{:S(2)}) collective-permute-start(bf16[128,1024]{1,0:T(8,128)(2,1)S(1)} %sign_rows.1), channel_id=1, source_target_pairs={{0,2},{1,3},{2,0},{3,1},{12,14},{13,15},{14,12},{15,13},{16,18},{1... | collective-permute-start | bytes 786440 | tf_op jit(solution)/shard_map/ppermute | solution.py:39
  58.2 5.0 %collective-permute-start.21 = (bf16[256,1024]{1,0:T(8,128)(2,1)S(1)}, bf16[256,1024]{1,0:T(8,128)(2,1)S(1)}, u32[]{:S(2)}, u32[]{:S(2)}) collective-permute-start(bf16[256,1024]{1,0:T(8,128)(2,1)S(1)} %pad_maximum_fusion.1), channel_id=1, source_target_pairs={{4,6},{5,7},{6,4},{7,5},{8,10},{9,11},{10,8},{11,9},{20,22},{21,23... | collective-permute-start | bytes 1572872 | tf_op jit(solution)/shard_map/ppermute | solution.py:39
  59.9 7.9 %collective-permute-start.16 = (bf16[128,256]{1,0:T(8,128)(2,1)S(1)}, bf16[128,256]{1,0:T(8,128)(2,1)S(1)}, u32[]{:S(2)}, u32[]{:S(2)}) collective-permute-start(bf16[128,256]{1,0:T(8,128)(2,1)S(1)} %get-tuple-element.36), channel_id=1, source_target_pairs={{0,8},{1,9},{2,10},{3,11},{4,12},{5,13},{6,14},{7,15},{8,16},{9,17... | collective-permute-start | bytes 196616 | tf_op jit(solution)/shard_map/ppermute | solution.py:39
  59.9 8.0 %collective-permute-start.17 = (bf16[128,256]{1,0:T(8,128)(2,1)S(1)}, bf16[128,256]{1,0:T(8,128)(2,1)S(1)}, u32[]{:S(2)}, u32[]{:S(2)}) collective-permute-start(bf16[128,256]{1,0:T(8,128)(2,1)S(1)} %get-tuple-element.37), channel_id=1, source_target_pairs={{0,9},{1,8},{2,11},{3,10},{4,13},{5,12},{6,15},{7,14},{8,17},{9,16... | collective-permute-start | bytes 196616 | tf_op jit(solution)/shard_map/ppermute | solution.py:39
  62.4 6.1 %collective-permute-start.18 = (bf16[128,256]{1,0:T(8,128)(2,1)S(1)}, bf16[128,256]{1,0:T(8,128)(2,1)S(1)}, u32[]{:S(2)}, u32[]{:S(2)}) collective-permute-start(bf16[128,256]{1,0:T(8,128)(2,1)S(1)} %get-tuple-element.39), channel_id=1, source_target_pairs={{0,1},{1,0},{2,3},{3,2},{4,5},{5,4},{6,7},{7,6},{8,9},{9,8},{10,11... | collective-permute-start | bytes 196616 | tf_op jit(solution)/shard_map/ppermute | solution.py:39
  63.1 6.6 %collective-permute-start.19 = (bf16[128,256]{1,0:T(8,128)(2,1)S(1)}, bf16[128,256]{1,0:T(8,128)(2,1)S(1)}, u32[]{:S(2)}, u32[]{:S(2)}) collective-permute-start(bf16[128,256]{1,0:T(8,128)(2,1)S(1)} %get-tuple-element.40), channel_id=1, source_target_pairs={{0,24},{1,25},{2,26},{3,27},{4,28},{5,29},{6,30},{7,31},{8,0},{9,1... | collective-permute-start | bytes 196616 | tf_op jit(solution)/shard_map/ppermute | solution.py:39
  63.2 7.7 %collective-permute-start.20 = (bf16[128,256]{1,0:T(8,128)(2,1)S(1)}, bf16[128,256]{1,0:T(8,128)(2,1)S(1)}, u32[]{:S(2)}, u32[]{:S(2)}) collective-permute-start(bf16[128,256]{1,0:T(8,128)(2,1)S(1)} %get-tuple-element.41), channel_id=1, source_target_pairs={{0,25},{1,24},{2,27},{3,26},{4,29},{5,28},{6,31},{7,30},{8,1},{9,0... | collective-permute-start | bytes 196616 | tf_op jit(solution)/shard_map/ppermute | solution.py:39
  67.8 4.3 %collective-permute-start.22 = (bf16[128,256]{1,0:T(8,128)(2,1)S(1)}, bf16[128,256]{1,0:T(8,128)(2,1)S(1)}, u32[]{:S(2)}, u32[]{:S(2)}) collective-permute-start(bf16[128,256]{1,0:T(8,128)(2,1)S(1)} %get-tuple-element.45), channel_id=1, source_target_pairs={{0,8},{1,9},{2,10},{3,11},{4,12},{5,13},{6,14},{7,15},{8,16},{9,17... | collective-permute-start | bytes 196616 | tf_op jit(solution)/shard_map/ppermute | solution.py:39
  67.9 4.8 %collective-permute-start.23 = (bf16[128,256]{1,0:T(8,128)(2,1)S(1)}, bf16[128,256]{1,0:T(8,128)(2,1)S(1)}, u32[]{:S(2)}, u32[]{:S(2)}) collective-permute-start(bf16[128,256]{1,0:T(8,128)(2,1)S(1)} %get-tuple-element.46), channel_id=1, source_target_pairs={{0,9},{1,8},{2,11},{3,10},{4,13},{5,12},{6,15},{7,14},{8,17},{9,16... | collective-permute-start | bytes 196616 | tf_op jit(solution)/shard_map/ppermute | solution.py:39
  68.5 5.3 %collective-permute-start.24 = (bf16[128,256]{1,0:T(8,128)(2,1)S(1)}, bf16[128,256]{1,0:T(8,128)(2,1)S(1)}, u32[]{:S(2)}, u32[]{:S(2)}) collective-permute-start(bf16[128,256]{1,0:T(8,128)(2,1)S(1)} %get-tuple-element.48), channel_id=1, source_target_pairs={{0,1},{1,0},{2,3},{3,2},{4,5},{5,4},{6,7},{7,6},{8,9},{9,8},{10,11... | collective-permute-start | bytes 196616 | tf_op jit(solution)/shard_map/ppermute | solution.py:39
  70.9 4.4 %collective-permute-start.26 = (bf16[128,256]{1,0:T(8,128)(2,1)S(1)}, bf16[128,256]{1,0:T(8,128)(2,1)S(1)}, u32[]{:S(2)}, u32[]{:S(2)}) collective-permute-start(bf16[128,256]{1,0:T(8,128)(2,1)S(1)} %get-tuple-element.50), channel_id=1, source_target_pairs={{0,25},{1,24},{2,27},{3,26},{4,29},{5,28},{6,31},{7,30},{8,1},{9,0... | collective-permute-start | bytes 196616 | tf_op jit(solution)/shard_map/ppermute | solution.py:39
  (6 other events, 54.9 us)

commit v5 on v4

--- a/solution.py
+++ b/solution.py
@@ -149,7 +149,7 @@
             pltpu.VMEM((width, width), BF16),
             pltpu.VMEM((width, width), BF16),
         ],
-        compiler_params=pltpu.CompilerParams(vmem_limit_bytes=8 * 2**20 + 12 * width * width),
+        compiler_params=pltpu.CompilerParams(vmem_limit_bytes=6 * 2**20 + 10 * width * width),
         cost_estimate=pl.CostEstimate(
             flops=70 * own * width * width, bytes_accessed=2 * width * width, transcendentals=0
         ),
@@ -157,20 +157,26 @@
     )(slot, active, mask_row[None], diag_row[None], *shards)
 
 
-def products_kernel(sources, sides, *refs):
-    signs, outs = refs[2 : -2 * sides], refs[-2 * sides :]
+def products_kernel(sources, sides, widths, *refs):
+    outs = refs[-2 * sides :]
+    before = refs[-2 * sides - len(widths) : -2 * sides]
+    signs = refs[2 : len(refs) - 2 * sides - len(widths)]
     own = outs[0].shape[0]
+    shift = [0] * len(outs)
+    for part, side, width in zip(before, (0, 2), widths):
+        outs[side][:, :width] = part[...]
+        shift[side] = width
     for k, source in enumerate(sources):
-        cols = slice(k * own, (k + 1) * own)
         shard = sum(signs[i][j * own : (j + 1) * own, :] for i, j in source)
         for j in range(2):
             prod = lax.dot_general(refs[j][...], shard, LAST, preferred_element_type=F32)
             for side in range(sides):
-                out = outs[j * sides + side]
-                out[:, cols] = prod[side * own : (side + 1) * own].astype(out.dtype)
-
-
-def products(trio, mates, sources, own):
+                out, start = outs[j * sides + side], shift[j * sides + side] + k * own
+                block = prod[side * own : (side + 1) * own]
+                out[:, start : start + own] = block.astype(out.dtype)
+
+
+def products(trio, mates, sources, own, before):
     arrays = []
     for source in sources:
         arrays += [a for a, _ in source if all(a is not b for b in arrays)]
@@ -180,11 +186,16 @@
     ]
     count, width = len(sources), trio.shape[1]
     sides = trio.shape[0] // own
-    kinds = [F32 if k == 1 else BF16 for k in range(2 * sides)]
+    shapes = [
+        jax.ShapeDtypeStruct((own, count * own), F32 if k == 1 else BF16) for k in range(2 * sides)
+    ]
+    widths = [part.shape[1] for part in before]
+    for part, side in zip(before, (0, 2)):
+        shapes[side] = jax.ShapeDtypeStruct((own, count * own + part.shape[1]), BF16)
     return pl.pallas_call(
-        lambda *refs: products_kernel(indices, sides, *refs),
-        out_shape=[jax.ShapeDtypeStruct((own, count * own), kind) for kind in kinds],
-        in_specs=[VMEM] * (2 + len(arrays)),
+        lambda *refs: products_kernel(indices, sides, widths, *refs),
+        out_shape=shapes,
+        in_specs=[VMEM] * (2 + len(arrays) + len(before)),
         out_specs=[VMEM] * (2 * sides),
         compiler_params=pltpu.CompilerParams(vmem_limit_bytes=24 * 2**20),
         cost_estimate=pl.CostEstimate(
@@ -193,31 +204,31 @@
             transcendentals=0,
         ),
         name="products",
-    )(trio, mates, *arrays)
-
-
-def final_kernel(groups, own, slot_ref, *refs):
+    )(trio, mates, *arrays, *before)
+
+
+def final_kernel(places, own, slot_ref, *refs):
     out_hbm, out_ref, sems = refs[-3:]
     copies = []
-    for side in range(3):
-        for group, steps in enumerate(groups):
-            for mate in range(2):
-                part = refs[(group * 3 + side) * 2 + mate]
-                for k, step in enumerate(steps):
-                    start = pl.multiple_of((slot_ref[0] ^ (step + mate)) * own, own)
+    for side in (1, 0, 2):
+        for part, (at, steps) in zip(refs, places):
+            for k, step in enumerate(steps):
+                if at == side:
+                    start = pl.multiple_of((slot_ref[0] ^ step) * own, own)
                     block = part[:, k * own : (k + 1) * own]
                     out_ref[side, :, pl.ds(start, own)] = block.astype(F32)
         copies.append(pltpu.make_async_copy(out_ref.at[side], out_hbm.at[side], sems.at[side]))
-        copies[side].start()
+        copies[-1].start()
     for copy in copies:
         copy.wait()
 
 
-def final(slot, groups, parts, width):
-    flat = [p for part in parts for side in part for p in side]
+def final(slot, pieces, width):
+    places = [(side, steps) for side, steps, _ in pieces]
+    flat = [array for _, _, array in pieces]
     own = flat[0].shape[0]
     return pl.pallas_call(
-        lambda *refs: final_kernel(groups, own, *refs),
+        lambda *refs: final_kernel(places, own, *refs),
         out_shape=jax.ShapeDtypeStruct((3, own, width), F32),
         in_specs=[SMEM] + [VMEM] * len(flat),
         out_specs=HBM,
@@ -293,24 +304,22 @@
     sources.append(
         [[(near[i][j], 0), (far[i], j)] for i in range(len(near)) for j in range(2)]
     )
-    placed = []
-    for source in sources:
-        out = products(trio, mates, source, own)
-        placed.append(
-            [
-                [
-                    send(out[0], lambda r, c: (r + 1, c)),
-                    send(out[3], lambda r, c: (r + 1, c ^ 1)),
-                ],
-                [out[1], send(out[4], lambda r, c: (r, c ^ 1))],
-                [
-                    send(out[2], lambda r, c: (r - 1, c)),
-                    send(out[5], lambda r, c: (r - 1, c ^ 1)),
-                ],
-            ]
-        )
+    pieces, every, before = [], [], []
+    for steps, source in zip(groups, sources):
+        out = products(trio, mates, source, own, before)
+        beside = [k ^ 1 for k in steps]
+        every += steps
+        before = [out[0], out[2]]
+        pieces += [
+            (0, beside, send(out[3], lambda r, c: (r + 1, c ^ 1))),
+            (2, beside, send(out[5], lambda r, c: (r - 1, c ^ 1))),
+            (1, beside, send(out[4], lambda r, c: (r, c ^ 1))),
+            (1, steps, out[1]),
+        ]
+    pieces.append((0, every, send(before[0], lambda r, c: (r + 1, c))))
+    pieces.append((2, every, send(before[1], lambda r, c: (r - 1, c))))
     width = cols * hamiltonian.shape[1]
-    result = final(col.astype(jnp.int32)[None], groups, placed, width)
+    result = final(col.astype(jnp.int32)[None], pieces, width)
     return result.transpose(1, 0, 2)
 
 

time: 76.8 us -> 75.7 us (0.986)
  starting transfers between devices: 40.6 us -> 39.7 us
    ppermute x27 -> x25, starting transfers between devices: 40.6 us -> 39.7 us  [send(): return lax.ppermute(array, AXES, moves)]
    ppermute x27 -> x25, waiting for transfers between devices: 17 us -> 16.9 us  [send(): return lax.ppermute(array, AXES, moves)]
  transfers between devices with their start and end apart: 27 -> 25, of which waited for: 8 -> 7; matrix products, arithmetic and copies ran while one was open for 4% -> 4% of each run, Pallas kernels for 16% -> 17%
where the time goes in v5:
time: 75.7 us; the launch traced here: 75.5 us
  starting transfers between devices  39.7 us (52%)
  waiting for transfers between devices  16.9 us (22%)
  Pallas kernels  16 us (21%)
  local copies, waits for them, and re-layouts  1.91 us (3%)
  other arithmetic  0.86 us (1%)
    ppermute x25, starting transfers between devices, send(): return lax.ppermute(array, AXES, moves)  39.7 us
    ppermute x25, waiting for transfers between devices, send(): return lax.ppermute(array, AXES, moves)  16.9 us
    pallas_call x1, Pallas kernels, sign_rows(): pl.pallas_call(lambda *refs: sign_kernel(count, *refs), out_shape=jax.Sha...  10.7 us
    pallas_call x1, Pallas kernels, prepare(): pl.pallas_call(lambda *refs: prepare_kernel(pieces, *refs), out_shape=jax...  2.15 us
    pallas_call x2, Pallas kernels, products(): pl.pallas_call(lambda *refs: products_kernel(indices, sides, widths, *ref...  1.94 us
  transfers between devices with their start and end apart: 25, of which 7 were waited for; matrix products, arithmetic and copies ran while one was open for 4% of the time, Pallas kernels for 17%

profile of v5, /device:TPU:0, one launch (start us, length us, event | category | flops | bytes accessed | tf_op | source)
XLA Modules:
  0.0 75.5 jit_solution(2507775323412153362)
XLA Ops:
  0.0 2.1 %prepare.1 = s16[1024,128]{1,0:T(8,128)(2,1)} custom-call(f32[1024,128]{1,0:T(8,128)} %refs_0_.1, s32[4,32]{1,0:T(4,128)} %bitcast.19), custom_call_target="tpu_custom_call" | custom-call | tf_op jit(solution)/shard_map/prepare/pallas_call | solution.py:75
  2.2 1.6 %collective-permute-start = (s16[1024,128]{1,0:T(8,128)(2,1)}, s16[1024,128]{1,0:T(8,128)(2,1)S(1)}, u32[]{:S(2)}, u32[]{:S(2)}) collective-permute-start(s16[1024,128]{1,0:T(8,128)(2,1)} %prepare.1), channel_id=1, source_target_pairs={{0,0},{1,1},{2,2},{3,3},{4,8},{5,9},{6,10},{7,11},{8,4},{9,5},{10,... | collective-permute-start | bytes 786440 | tf_op jit(solution)/shard_map/ppermute | solution.py:39
  4.9 4.5 %collective-permute-start.4 = (bf16[128,1024]{1,0:T(8,128)(2,1)S(1)}, bf16[128,1024]{1,0:T(8,128)(2,1)S(1)}, u32[]{:S(2)}, u32[]{:S(2)}) collective-permute-start(bf16[128,1024]{1,0:T(8,128)(2,1)S(1)} %get-tuple-element.52), channel_id=1, source_target_pairs={{0,8},{1,9},{2,10},{3,11},{4,12},{5,13},{6,14},{7,15},{8,16},{9,17... | collective-permute-start | bytes 786440 | tf_op jit(solution)/shard_map/ppermute | solution.py:39
  10.6 1.6 %collective-permute-start.6 = (s16[1024,128]{1,0:T(8,128)(2,1)S(1)}, s16[1024,128]{1,0:T(8,128)(2,1)S(1)}, u32[]{:S(2)}, u32[]{:S(2)}) collective-permute-start(s16[1024,128]{1,0:T(8,128)(2,1)S(1)} %collective-permute-done.refs_4_), channel_id=1, source_target_pairs={{0,2},{1,3},{2,0},{3,1},{4,6},{5,7},{6,4},{7,5},{8,10},{9,11},{10,... | collective-permute-start | bytes 786440 | tf_op jit(solution)/shard_map/ppermute | solution.py:39
  12.2 1.5 %collective-permute-start.5 = (s16[1024,128]{1,0:T(8,128)(2,1)S(1)}, s16[1024,128]{1,0:T(8,128)(2,1)S(1)}, u32[]{:S(2)}, u32[]{:S(2)}) collective-permute-start(s16[1024,128]{1,0:T(8,128)(2,1)S(1)} %collective-permute-done.refs_4_), channel_id=1, source_target_pairs={{0,1},{1,0},{2,3},{3,2},{4,5},{5,4},{6,7},{7,6},{8,9},{9,8},{10,11... | collective-permute-start | bytes 786440 | tf_op jit(solution)/shard_map/ppermute | solution.py:39
  15.4 1.2 %collective-permute-done.4 = bf16[128,1024]{1,0:T(8,128)(2,1)S(1)} collective-permute-done((bf16[128,1024]{1,0:T(8,128)(2,1)S(1)}, bf16[128,1024]{1,0:T(8,128)(2,1)S(1)}, u32[]{:S(2)}, u32[]{:S(2)}) %collective-permute-start.4) | collective-permute-done | bytes 262176 | tf_op jit(solution)/shard_map/ppermute | solution.py:39
  16.5 2.8 %collective-permute-start.2 = (f32[1024]{0:T(1024)S(1)}, f32[1024]{0:T(1024)S(1)}, u32[]{:S(2)}, u32[]{:S(2)}) collective-permute-start(f32[1024]{0:T(1024)S(1)} %copy-done.1), channel_id=1, source_target_pairs={{0,8},{1,9},{2,10},{3,11},{4,12},{5,13},{6,14},{7,15},{8,0},{9,1},... | collective-permute-start | bytes 12296 | tf_op jit(solution)/shard_map/ppermute | solution.py:39
  20.6 3.2 %collective-permute-start.9 = (s16[1024,128]{1,0:T(8,128)(2,1)S(1)}, s16[1024,128]{1,0:T(8,128)(2,1)S(1)}, u32[]{:S(2)}, u32[]{:S(2)}) collective-permute-start(s16[1024,128]{1,0:T(8,128)(2,1)S(1)} %collective-permute-done.6.refs_6_), channel_id=1, source_target_pairs={{0,8},{1,9},{2,10},{3,11},{4,12},{5,13},{6,14},{7,15},{8,0},{9,1},... | collective-permute-start | bytes 786440 | tf_op jit(solution)/shard_map/ppermute | solution.py:39
  23.8 2.4 %collective-permute-start.8 = (s16[1024,128]{1,0:T(8,128)(2,1)S(1)}, s16[1024,128]{1,0:T(8,128)(2,1)S(1)}, u32[]{:S(2)}, u32[]{:S(2)}) collective-permute-start(s16[1024,128]{1,0:T(8,128)(2,1)S(1)} %collective-permute-done.5.refs_5_), channel_id=1, source_target_pairs={{0,8},{1,9},{2,10},{3,11},{4,12},{5,13},{6,14},{7,15},{8,0},{9,1},... | collective-permute-start | bytes 786440 | tf_op jit(solution)/shard_map/ppermute | solution.py:39
  26.1 1.2 %collective-permute-start.10 = (s16[1024,128]{1,0:T(8,128)(2,1)S(1)}, s16[1024,128]{1,0:T(8,128)(2,1)S(1)}, u32[]{:S(2)}, u32[]{:S(2)}) collective-permute-start(s16[1024,128]{1,0:T(8,128)(2,1)S(1)} %collective-permute-done.1.refs_7_), channel_id=1, source_target_pairs={{0,8},{1,9},{2,10},{3,11},{4,12},{5,13},{6,14},{7,15},{8,0},{9,1},... | collective-permute-start | bytes 786440 | tf_op jit(solution)/shard_map/ppermute | solution.py:39
  28.5 10.7 %sign_rows.1 = bf16[128,1024]{1,0:T(8,128)(2,1)S(1)} custom-call(s32[1]{0:T(128)} %bitcast.8.refs_0_, s32[1]{0:T(128)} %dynamic_slice.9.refs_1_, f32[1,1024]{1,0:T(1,128)S(1)} %bitcast.16, f32[1,1024]{1,0:T(1,128)S(1)} %bitcast.17, s16[1024,128]{1,0:T(8,128)(2,1)S(1)} %collective-permute-done.refs_4_, s16[1024,128]{1,0:T(8,128)(2,1)S(1)} %collective-permute-done.5.refs_5_, ...), custom_call_target="tpu_custom_call" | custom-call | flops 9395240960 | bytes 2097152 | tf_op jit(solution)/shard_map/sign_rows/pallas_call | solution.py:142
  39.2 2.3 %collective-permute-start.12 = (bf16[128,1024]{1,0:T(8,128)(2,1)S(1)}, bf16[128,1024]{1,0:T(8,128)(2,1)S(1)}, u32[]{:S(2)}, u32[]{:S(2)}) collective-permute-start(bf16[128,1024]{1,0:T(8,128)(2,1)S(1)} %sign_rows.1), channel_id=1, source_target_pairs={{0,4},{1,5},{2,6},{3,7},{4,12},{5,13},{6,14},{7,15},{8,0},{9,1},{1... | collective-permute-start | bytes 786440 | tf_op jit(solution)/shard_map/ppermute | solution.py:39
  42.2 1.3 %collective-permute-start.14 = (bf16[128,1024]{1,0:T(8,128)(2,1)S(1)}, bf16[128,1024]{1,0:T(8,128)(2,1)S(1)}, u32[]{:S(2)}, u32[]{:S(2)}) collective-permute-start(bf16[128,1024]{1,0:T(8,128)(2,1)S(1)} %sign_rows.1), channel_id=1, source_target_pairs={{4,14},{5,15},{6,12},{7,13},{8,2},{9,3},{10,0},{11,1},{20,30},{21,... | collective-permute-start | bytes 786440 | tf_op jit(solution)/shard_map/ppermute | solution.py:39
  43.5 2.7 %collective-permute-start.13 = (bf16[128,1024]{1,0:T(8,128)(2,1)S(1)}, bf16[128,1024]{1,0:T(8,128)(2,1)S(1)}, u32[]{:S(2)}, u32[]{:S(2)}) collective-permute-start(bf16[128,1024]{1,0:T(8,128)(2,1)S(1)} %sign_rows.1), channel_id=1, source_target_pairs={{0,2},{1,3},{2,0},{3,1},{12,14},{13,15},{14,12},{15,13},{16,18},{1... | collective-permute-start | bytes 786440 | tf_op jit(solution)/shard_map/ppermute | solution.py:39
  46.9 9.6 %collective-permute-done.14.refs_4_ = bf16[128,1024]{1,0:T(8,128)(2,1)S(1)} collective-permute-done((bf16[128,1024]{1,0:T(8,128)(2,1)S(1)}, bf16[128,1024]{1,0:T(8,128)(2,1)S(1)}, u32[]{:S(2)}, u32[]{:S(2)}) %collective-permute-start.14) | collective-permute-done | bytes 262176 | tf_op jit(solution)/shard_map/ppermute | solution.py:39
  56.5 1.7 %collective-permute-done.13.refs_2_ = bf16[128,1024]{1,0:T(8,128)(2,1)S(1)} collective-permute-done((bf16[128,1024]{1,0:T(8,128)(2,1)S(1)}, bf16[128,1024]{1,0:T(8,128)(2,1)S(1)}, u32[]{:S(2)}, u32[]{:S(2)}) %collective-permute-start.13) | collective-permute-done | bytes 262176 | tf_op jit(solution)/shard_map/ppermute | solution.py:39
  59.9 2.6 %collective-permute-start.17 = (bf16[128,256]{1,0:T(8,128)(2,1)S(1)}, bf16[128,256]{1,0:T(8,128)(2,1)S(1)}, u32[]{:S(2)}, u32[]{:S(2)}) collective-permute-start(bf16[128,256]{1,0:T(8,128)(2,1)S(1)} %get-tuple-element.37), channel_id=1, source_target_pairs={{0,25},{1,24},{2,27},{3,26},{4,29},{5,28},{6,31},{7,30},{8,1},{9,0... | collective-permute-start | bytes 196616 | tf_op jit(solution)/shard_map/ppermute | solution.py:39
  62.6 1.2 %collective-permute-start.18 = (bf16[128,256]{1,0:T(8,128)(2,1)S(1)}, bf16[128,256]{1,0:T(8,128)(2,1)S(1)}, u32[]{:S(2)}, u32[]{:S(2)}) collective-permute-start(bf16[128,256]{1,0:T(8,128)(2,1)S(1)} %get-tuple-element.38), channel_id=1, source_target_pairs={{0,1},{1,0},{2,3},{3,2},{4,5},{5,4},{6,7},{7,6},{8,9},{9,8},{10,11... | collective-permute-start | bytes 196616 | tf_op jit(solution)/shard_map/ppermute | solution.py:39
  65.7 1.5 %collective-permute-start.24 = (bf16[128,512]{1,0:T(8,128)(2,1)S(1)}, bf16[128,512]{1,0:T(8,128)(2,1)S(1)}, u32[]{:S(2)}, u32[]{:S(2)}) collective-permute-start(bf16[128,512]{1,0:T(8,128)(2,1)S(1)} %get-tuple-element.50), channel_id=1, source_target_pairs={{0,24},{1,25},{2,26},{3,27},{4,28},{5,29},{6,30},{7,31},{8,0},{9,1... | collective-permute-start | bytes 393224 | tf_op jit(solution)/shard_map/ppermute | solution.py:39
  67.2 2.6 %collective-permute-start.21 = (bf16[128,256]{1,0:T(8,128)(2,1)S(1)}, bf16[128,256]{1,0:T(8,128)(2,1)S(1)}, u32[]{:S(2)}, u32[]{:S(2)}) collective-permute-start(bf16[128,256]{1,0:T(8,128)(2,1)S(1)} %get-tuple-element.46), channel_id=1, source_target_pairs={{0,25},{1,24},{2,27},{3,26},{4,29},{5,28},{6,31},{7,30},{8,1},{9,0... | collective-permute-start | bytes 196616 | tf_op jit(solution)/shard_map/ppermute | solution.py:39
  69.8 1.3 %collective-permute-start.22 = (bf16[128,256]{1,0:T(8,128)(2,1)S(1)}, bf16[128,256]{1,0:T(8,128)(2,1)S(1)}, u32[]{:S(2)}, u32[]{:S(2)}) collective-permute-start(bf16[128,256]{1,0:T(8,128)(2,1)S(1)} %get-tuple-element.47), channel_id=1, source_target_pairs={{0,1},{1,0},{2,3},{3,2},{4,5},{5,4},{6,7},{7,6},{8,9},{9,8},{10,11... | collective-permute-start | bytes 196616 | tf_op jit(solution)/shard_map/ppermute | solution.py:39
  71.1 1.6 %collective-permute-done.20.refs_5_ = bf16[128,256]{1,0:T(8,128)(2,1)S(1)} collective-permute-done((bf16[128,256]{1,0:T(8,128)(2,1)S(1)}, bf16[128,256]{1,0:T(8,128)(2,1)S(1)}, u32[]{:S(2)}, u32[]{:S(2)}) %collective-permute-start.20) | collective-permute-done | bytes 65568 | tf_op jit(solution)/shard_map/ppermute | solution.py:39
  72.7 1.5 %collective-permute-done.22.refs_7_ = bf16[128,256]{1,0:T(8,128)(2,1)S(1)} collective-permute-done((bf16[128,256]{1,0:T(8,128)(2,1)S(1)}, bf16[128,256]{1,0:T(8,128)(2,1)S(1)}, u32[]{:S(2)}, u32[]{:S(2)}) %collective-permute-start.22) | collective-permute-done | bytes 65568 | tf_op jit(solution)/shard_map/ppermute | solution.py:39
  74.2 1.2 %final.1 = f32[3,128,1024]{2,1,0:T(8,128)} custom-call(s32[1]{0:T(128)} %bitcast.refs_0_, bf16[128,256]{1,0:T(8,128)(2,1)S(1)} %collective-permute-done.16.refs_1_, bf16[128,256]{1,0:T(8,128)(2,1)S(1)} %collective-permute-done.17.refs_2_, bf16[128,256]{1,0:T(8,128)(2,1)S(1)} %collective-permute-done.18.refs_3_, f32[128,256]{1,0:T(8,128)S(1)} %get-tuple-element.39.refs_4_, ...), custom_call_target="tpu_custom_call" | custom-call | bytes 3145728 | tf_op jit(solution)/shard_map/final/pallas_call | solution.py:230
  (48 shorter events, 11.3 us)
Async XLA Ops:
  2.2 8.4 %collective-permute-start = (s16[1024,128]{1,0:T(8,128)(2,1)}, s16[1024,128]{1,0:T(8,128)(2,1)S(1)}, u32[]{:S(2)}, u32[]{:S(2)}) collective-permute-start(s16[1024,128]{1,0:T(8,128)(2,1)} %prepare.1), channel_id=1, source_target_pairs={{0,0},{1,1},{2,2},{3,3},{4,8},{5,9},{6,10},{7,11},{8,4},{9,5},{10,... | collective-permute-start | bytes 786440 | tf_op jit(solution)/shard_map/ppermute | solution.py:39
  4.9 11.6 %collective-permute-start.4 = (bf16[128,1024]{1,0:T(8,128)(2,1)S(1)}, bf16[128,1024]{1,0:T(8,128)(2,1)S(1)}, u32[]{:S(2)}, u32[]{:S(2)}) collective-permute-start(bf16[128,1024]{1,0:T(8,128)(2,1)S(1)} %get-tuple-element.52), channel_id=1, source_target_pairs={{0,8},{1,9},{2,10},{3,11},{4,12},{5,13},{6,14},{7,15},{8,16},{9,17... | collective-permute-start | bytes 786440 | tf_op jit(solution)/shard_map/ppermute | solution.py:39
  9.4 17.9 %collective-permute-start.3 = (bf16[128,1024]{1,0:T(8,128)(2,1)S(1)}, bf16[128,1024]{1,0:T(8,128)(2,1)S(1)}, u32[]{:S(2)}, u32[]{:S(2)}) collective-permute-start(bf16[128,1024]{1,0:T(8,128)(2,1)S(1)} %get-tuple-element.53), channel_id=1, source_target_pairs={{0,24},{1,25},{2,26},{3,27},{4,28},{5,29},{6,30},{7,31},{8,0},{9,1... | collective-permute-start | bytes 786440 | tf_op jit(solution)/shard_map/ppermute | solution.py:39
  10.6 9.9 %collective-permute-start.6 = (s16[1024,128]{1,0:T(8,128)(2,1)S(1)}, s16[1024,128]{1,0:T(8,128)(2,1)S(1)}, u32[]{:S(2)}, u32[]{:S(2)}) collective-permute-start(s16[1024,128]{1,0:T(8,128)(2,1)S(1)} %collective-permute-done.refs_4_), channel_id=1, source_target_pairs={{0,2},{1,3},{2,0},{3,1},{4,6},{5,7},{6,4},{7,5},{8,10},{9,11},{10,... | collective-permute-start | bytes 786440 | tf_op jit(solution)/shard_map/ppermute | solution.py:39
  12.2 11.6 %collective-permute-start.5 = (s16[1024,128]{1,0:T(8,128)(2,1)S(1)}, s16[1024,128]{1,0:T(8,128)(2,1)S(1)}, u32[]{:S(2)}, u32[]{:S(2)}) collective-permute-start(s16[1024,128]{1,0:T(8,128)(2,1)S(1)} %collective-permute-done.refs_4_), channel_id=1, source_target_pairs={{0,1},{1,0},{2,3},{3,2},{4,5},{5,4},{6,7},{7,6},{8,9},{9,8},{10,11... | collective-permute-start | bytes 786440 | tf_op jit(solution)/shard_map/ppermute | solution.py:39
  13.7 12.4 %collective-permute-start.1 = (s16[1024,128]{1,0:T(8,128)(2,1)S(1)}, s16[1024,128]{1,0:T(8,128)(2,1)S(1)}, u32[]{:S(2)}, u32[]{:S(2)}) collective-permute-start(s16[1024,128]{1,0:T(8,128)(2,1)S(1)} %collective-permute-done.refs_4_), channel_id=1, source_target_pairs={{0,3},{1,2},{2,1},{3,0},{4,7},{5,6},{6,5},{7,4},{8,11},{9,10},{10,... | collective-permute-start | bytes 786440 | tf_op jit(solution)/shard_map/ppermute | solution.py:39
  16.5 3.7 %collective-permute-start.2 = (f32[1024]{0:T(1024)S(1)}, f32[1024]{0:T(1024)S(1)}, u32[]{:S(2)}, u32[]{:S(2)}) collective-permute-start(f32[1024]{0:T(1024)S(1)} %copy-done.1), channel_id=1, source_target_pairs={{0,8},{1,9},{2,10},{3,11},{4,12},{5,13},{6,14},{7,15},{8,0},{9,1},... | collective-permute-start | bytes 12296 | tf_op jit(solution)/shard_map/ppermute | solution.py:39
  20.2 8.3 %collective-permute-start.7 = (s16[1024,128]{1,0:T(8,128)(2,1)S(1)}, s16[1024,128]{1,0:T(8,128)(2,1)S(1)}, u32[]{:S(2)}, u32[]{:S(2)}) collective-permute-start(s16[1024,128]{1,0:T(8,128)(2,1)S(1)} %collective-permute-done.refs_4_), channel_id=1, source_target_pairs={{0,8},{1,9},{2,10},{3,11},{4,12},{5,13},{6,14},{7,15},{8,0},{9,1},... | collective-permute-start | bytes 786440 | tf_op jit(solution)/shard_map/ppermute | solution.py:39
  20.6 7.9 %collective-permute-start.9 = (s16[1024,128]{1,0:T(8,128)(2,1)S(1)}, s16[1024,128]{1,0:T(8,128)(2,1)S(1)}, u32[]{:S(2)}, u32[]{:S(2)}) collective-permute-start(s16[1024,128]{1,0:T(8,128)(2,1)S(1)} %collective-permute-done.6.refs_6_), channel_id=1, source_target_pairs={{0,8},{1,9},{2,10},{3,11},{4,12},{5,13},{6,14},{7,15},{8,0},{9,1},... | collective-permute-start | bytes 786440 | tf_op jit(solution)/shard_map/ppermute | solution.py:39
  23.8 4.7 %collective-permute-start.8 = (s16[1024,128]{1,0:T(8,128)(2,1)S(1)}, s16[1024,128]{1,0:T(8,128)(2,1)S(1)}, u32[]{:S(2)}, u32[]{:S(2)}) collective-permute-start(s16[1024,128]{1,0:T(8,128)(2,1)S(1)} %collective-permute-done.5.refs_5_), channel_id=1, source_target_pairs={{0,8},{1,9},{2,10},{3,11},{4,12},{5,13},{6,14},{7,15},{8,0},{9,1},... | collective-permute-start | bytes 786440 | tf_op jit(solution)/shard_map/ppermute | solution.py:39
  27.4 30.7 %collective-permute-start.15 = (bf16[384,1024]{1,0:T(8,128)(2,1)S(1)}, bf16[384,1024]{1,0:T(8,128)(2,1)S(1)}, u32[]{:S(2)}, u32[]{:S(2)}) collective-permute-start(bf16[384,1024]{1,0:T(8,128)(2,1)S(1)} %pad_maximum_fusion.refs_0_), channel_id=1, source_target_pairs={{0,1},{1,0},{2,3},{3,2},{4,5},{5,4},{6,7},{7,6},{8,9},{9,8},{10,11... | collective-permute-start | bytes 2359304 | tf_op jit(solution)/shard_map/ppermute | solution.py:39
  39.2 7.7 %collective-permute-start.12 = (bf16[128,1024]{1,0:T(8,128)(2,1)S(1)}, bf16[128,1024]{1,0:T(8,128)(2,1)S(1)}, u32[]{:S(2)}, u32[]{:S(2)}) collective-permute-start(bf16[128,1024]{1,0:T(8,128)(2,1)S(1)} %sign_rows.1), channel_id=1, source_target_pairs={{0,4},{1,5},{2,6},{3,7},{4,12},{5,13},{6,14},{7,15},{8,0},{9,1},{1... | collective-permute-start | bytes 786440 | tf_op jit(solution)/shard_map/ppermute | solution.py:39
  41.5 5.4 %collective-permute-start.11 = (bf16[128,1024]{1,0:T(8,128)(2,1)S(1)}, bf16[128,1024]{1,0:T(8,128)(2,1)S(1)}, u32[]{:S(2)}, u32[]{:S(2)}) collective-permute-start(bf16[128,1024]{1,0:T(8,128)(2,1)S(1)} %sign_rows.1), channel_id=1, source_target_pairs={{0,0},{1,1},{2,2},{3,3},{4,8},{5,9},{6,10},{7,11},{8,4},{9,5},{10,... | collective-permute-start | bytes 786440 | tf_op jit(solution)/shard_map/ppermute | solution.py:39
  42.2 14.4 %collective-permute-start.14 = (bf16[128,1024]{1,0:T(8,128)(2,1)S(1)}, bf16[128,1024]{1,0:T(8,128)(2,1)S(1)}, u32[]{:S(2)}, u32[]{:S(2)}) collective-permute-start(bf16[128,1024]{1,0:T(8,128)(2,1)S(1)} %sign_rows.1), channel_id=1, source_target_pairs={{4,14},{5,15},{6,12},{7,13},{8,2},{9,3},{10,0},{11,1},{20,30},{21,... | collective-permute-start | bytes 786440 | tf_op jit(solution)/shard_map/ppermute | solution.py:39
  43.5 14.7 %collective-permute-start.13 = (bf16[128,1024]{1,0:T(8,128)(2,1)S(1)}, bf16[128,1024]{1,0:T(8,128)(2,1)S(1)}, u32[]{:S(2)}, u32[]{:S(2)}) collective-permute-start(bf16[128,1024]{1,0:T(8,128)(2,1)S(1)} %sign_rows.1), channel_id=1, source_target_pairs={{0,2},{1,3},{2,0},{3,1},{12,14},{13,15},{14,12},{15,13},{16,18},{1... | collective-permute-start | bytes 786440 | tf_op jit(solution)/shard_map/ppermute | solution.py:39
  58.2 5.6 %collective-permute-start.19 = (bf16[256,1024]{1,0:T(8,128)(2,1)S(1)}, bf16[256,1024]{1,0:T(8,128)(2,1)S(1)}, u32[]{:S(2)}, u32[]{:S(2)}) collective-permute-start(bf16[256,1024]{1,0:T(8,128)(2,1)S(1)} %pad_maximum_fusion.1), channel_id=1, source_target_pairs={{4,6},{5,7},{6,4},{7,5},{8,10},{9,11},{10,8},{11,9},{20,22},{21,23... | collective-permute-start | bytes 1572872 | tf_op jit(solution)/shard_map/ppermute | solution.py:39
  59.9 7.3 %collective-permute-start.16 = (bf16[128,256]{1,0:T(8,128)(2,1)S(1)}, bf16[128,256]{1,0:T(8,128)(2,1)S(1)}, u32[]{:S(2)}, u32[]{:S(2)}) collective-permute-start(bf16[128,256]{1,0:T(8,128)(2,1)S(1)} %get-tuple-element.36), channel_id=1, source_target_pairs={{0,9},{1,8},{2,11},{3,10},{4,13},{5,12},{6,15},{7,14},{8,17},{9,16... | collective-permute-start | bytes 196616 | tf_op jit(solution)/shard_map/ppermute | solution.py:39
  59.9 7.3 %collective-permute-start.17 = (bf16[128,256]{1,0:T(8,128)(2,1)S(1)}, bf16[128,256]{1,0:T(8,128)(2,1)S(1)}, u32[]{:S(2)}, u32[]{:S(2)}) collective-permute-start(bf16[128,256]{1,0:T(8,128)(2,1)S(1)} %get-tuple-element.37), channel_id=1, source_target_pairs={{0,25},{1,24},{2,27},{3,26},{4,29},{5,28},{6,31},{7,30},{8,1},{9,0... | collective-permute-start | bytes 196616 | tf_op jit(solution)/shard_map/ppermute | solution.py:39
  62.6 7.3 %collective-permute-start.18 = (bf16[128,256]{1,0:T(8,128)(2,1)S(1)}, bf16[128,256]{1,0:T(8,128)(2,1)S(1)}, u32[]{:S(2)}, u32[]{:S(2)}) collective-permute-start(bf16[128,256]{1,0:T(8,128)(2,1)S(1)} %get-tuple-element.38), channel_id=1, source_target_pairs={{0,1},{1,0},{2,3},{3,2},{4,5},{5,4},{6,7},{7,6},{8,9},{9,8},{10,11... | collective-permute-start | bytes 196616 | tf_op jit(solution)/shard_map/ppermute | solution.py:39
  64.8 9.5 %collective-permute-start.23 = (bf16[128,512]{1,0:T(8,128)(2,1)S(1)}, bf16[128,512]{1,0:T(8,128)(2,1)S(1)}, u32[]{:S(2)}, u32[]{:S(2)}) collective-permute-start(bf16[128,512]{1,0:T(8,128)(2,1)S(1)} %get-tuple-element.49), channel_id=1, source_target_pairs={{0,8},{1,9},{2,10},{3,11},{4,12},{5,13},{6,14},{7,15},{8,16},{9,17... | collective-permute-start | bytes 393224 | tf_op jit(solution)/shard_map/ppermute | solution.py:39
  65.7 8.6 %collective-permute-start.24 = (bf16[128,512]{1,0:T(8,128)(2,1)S(1)}, bf16[128,512]{1,0:T(8,128)(2,1)S(1)}, u32[]{:S(2)}, u32[]{:S(2)}) collective-permute-start(bf16[128,512]{1,0:T(8,128)(2,1)S(1)} %get-tuple-element.50), channel_id=1, source_target_pairs={{0,24},{1,25},{2,26},{3,27},{4,28},{5,29},{6,30},{7,31},{8,0},{9,1... | collective-permute-start | bytes 393224 | tf_op jit(solution)/shard_map/ppermute | solution.py:39
  67.2 5.5 %collective-permute-start.20 = (bf16[128,256]{1,0:T(8,128)(2,1)S(1)}, bf16[128,256]{1,0:T(8,128)(2,1)S(1)}, u32[]{:S(2)}, u32[]{:S(2)}) collective-permute-start(bf16[128,256]{1,0:T(8,128)(2,1)S(1)} %get-tuple-element.45), channel_id=1, source_target_pairs={{0,9},{1,8},{2,11},{3,10},{4,13},{5,12},{6,15},{7,14},{8,17},{9,16... | collective-permute-start | bytes 196616 | tf_op jit(solution)/shard_map/ppermute | solution.py:39
  67.2 5.5 %collective-permute-start.21 = (bf16[128,256]{1,0:T(8,128)(2,1)S(1)}, bf16[128,256]{1,0:T(8,128)(2,1)S(1)}, u32[]{:S(2)}, u32[]{:S(2)}) collective-permute-start(bf16[128,256]{1,0:T(8,128)(2,1)S(1)} %get-tuple-element.46), channel_id=1, source_target_pairs={{0,25},{1,24},{2,27},{3,26},{4,29},{5,28},{6,31},{7,30},{8,1},{9,0... | collective-permute-start | bytes 196616 | tf_op jit(solution)/shard_map/ppermute | solution.py:39
  69.8 4.4 %collective-permute-start.22 = (bf16[128,256]{1,0:T(8,128)(2,1)S(1)}, bf16[128,256]{1,0:T(8,128)(2,1)S(1)}, u32[]{:S(2)}, u32[]{:S(2)}) collective-permute-start(bf16[128,256]{1,0:T(8,128)(2,1)S(1)} %get-tuple-element.47), channel_id=1, source_target_pairs={{0,1},{1,0},{2,3},{3,2},{4,5},{5,4},{6,7},{7,6},{8,9},{9,8},{10,11... | collective-permute-start | bytes 196616 | tf_op jit(solution)/shard_map/ppermute | solution.py:39
  (4 other events, 47.1 us)

commit v6 on v5

--- a/solution.py
+++ b/solution.py
@@ -94,11 +94,12 @@
     width = ham.shape[0]
     own = out_ref.shape[0]
     slot = slot_ref[0]
-    mask_col = jnp.broadcast_to(mask_row[...], (own, width)).T
+    half_scale = 0.5 * LARGEST / CODES**4
+    mask_col = jnp.broadcast_to(mask_row[...] * half_scale, (own, width)).T
     for k in range(count):
         start = pl.multiple_of((slot ^ k) * own, own)
-        root = shards[k][...].astype(F32) * (1.0 / CODES)
-        entry = (root * jnp.abs(root)) * (root * root) * LARGEST
+        root = shards[k][...].astype(F32)
+        entry = (root * jnp.abs(root)) * (root * root)
         ham[:, pl.ds(start, own)] = entry * mask_col * mask_row[:, pl.ds(start, own)]
     rows = lax.broadcasted_iota(jnp.int32, (own, width), 0)
     cols = lax.broadcasted_iota(jnp.int32, (own, width), 1)
@@ -106,7 +107,7 @@
     def strip(k, squares):
         at = pl.ds(pl.multiple_of(k * own, own), own)
         diag = jnp.where(cols == rows + k * own, diag_row[...], 0.0)
-        both = 0.5 * (ham[at, :] + ham[:, at].T) + diag
+        both = ham[at, :] + ham[:, at].T + diag
         high = both.astype(BF16)
         high_ref[at, :] = high
         low_ref[at, :] = (both - high.astype(F32)).astype(BF16)

time: 75.7 us -> 75.3 us (level)
  transfers between devices with their start and end apart: 25 -> 25, of which waited for: 7 -> 7; matrix products, arithmetic and copies ran while one was open for 4% -> 4% of each run, Pallas kernels for 17% -> 16%
where the time goes in v6:
time: 75.3 us; the launch traced here: 75 us
  starting transfers between devices  39.7 us (53%)
  waiting for transfers between devices  16.9 us (22%)
  Pallas kernels  15.6 us (21%)
  local copies, waits for them, and re-layouts  1.91 us (3%)
  other arithmetic  0.86 us (1%)
    ppermute x25, starting transfers between devices, send(): return lax.ppermute(array, AXES, moves)  39.7 us
    ppermute x25, waiting for transfers between devices, send(): return lax.ppermute(array, AXES, moves)  16.9 us
    pallas_call x1, Pallas kernels, sign_rows(): pl.pallas_call(lambda *refs: sign_kernel(count, *refs), out_shape=jax.Sha...  10.3 us
    pallas_call x1, Pallas kernels, prepare(): pl.pallas_call(lambda *refs: prepare_kernel(pieces, *refs), out_shape=jax...  2.15 us
    pallas_call x2, Pallas kernels, products(): pl.pallas_call(lambda *refs: products_kernel(indices, sides, widths, *ref...  1.93 us
  transfers between devices with their start and end apart: 25, of which 7 were waited for; matrix products, arithmetic and copies ran while one was open for 4% of the time, Pallas kernels for 16%

profile of v6, /device:TPU:0, one launch (start us, length us, event | category | flops | bytes accessed | tf_op | source)
XLA Modules:
  0.0 75.0 jit_solution(18336783576340551489)
XLA Ops:
  0.0 2.1 %prepare.1 = s16[1024,128]{1,0:T(8,128)(2,1)} custom-call(f32[1024,128]{1,0:T(8,128)} %refs_0_.1, s32[4,32]{1,0:T(4,128)} %bitcast.19), custom_call_target="tpu_custom_call" | custom-call | tf_op jit(solution)/shard_map/prepare/pallas_call | solution.py:75
  2.2 1.6 %collective-permute-start = (s16[1024,128]{1,0:T(8,128)(2,1)}, s16[1024,128]{1,0:T(8,128)(2,1)S(1)}, u32[]{:S(2)}, u32[]{:S(2)}) collective-permute-start(s16[1024,128]{1,0:T(8,128)(2,1)} %prepare.1), channel_id=1, source_target_pairs={{0,0},{1,1},{2,2},{3,3},{4,8},{5,9},{6,10},{7,11},{8,4},{9,5},{10,... | collective-permute-start | bytes 786440 | tf_op jit(solution)/shard_map/ppermute | solution.py:39
  4.9 4.5 %collective-permute-start.4 = (bf16[128,1024]{1,0:T(8,128)(2,1)S(1)}, bf16[128,1024]{1,0:T(8,128)(2,1)S(1)}, u32[]{:S(2)}, u32[]{:S(2)}) collective-permute-start(bf16[128,1024]{1,0:T(8,128)(2,1)S(1)} %get-tuple-element.52), channel_id=1, source_target_pairs={{0,8},{1,9},{2,10},{3,11},{4,12},{5,13},{6,14},{7,15},{8,16},{9,17... | collective-permute-start | bytes 786440 | tf_op jit(solution)/shard_map/ppermute | solution.py:39
  10.6 1.6 %collective-permute-start.6 = (s16[1024,128]{1,0:T(8,128)(2,1)S(1)}, s16[1024,128]{1,0:T(8,128)(2,1)S(1)}, u32[]{:S(2)}, u32[]{:S(2)}) collective-permute-start(s16[1024,128]{1,0:T(8,128)(2,1)S(1)} %collective-permute-done.refs_4_), channel_id=1, source_target_pairs={{0,2},{1,3},{2,0},{3,1},{4,6},{5,7},{6,4},{7,5},{8,10},{9,11},{10,... | collective-permute-start | bytes 786440 | tf_op jit(solution)/shard_map/ppermute | solution.py:39
  12.2 1.5 %collective-permute-start.5 = (s16[1024,128]{1,0:T(8,128)(2,1)S(1)}, s16[1024,128]{1,0:T(8,128)(2,1)S(1)}, u32[]{:S(2)}, u32[]{:S(2)}) collective-permute-start(s16[1024,128]{1,0:T(8,128)(2,1)S(1)} %collective-permute-done.refs_4_), channel_id=1, source_target_pairs={{0,1},{1,0},{2,3},{3,2},{4,5},{5,4},{6,7},{7,6},{8,9},{9,8},{10,11... | collective-permute-start | bytes 786440 | tf_op jit(solution)/shard_map/ppermute | solution.py:39
  15.4 1.2 %collective-permute-done.4 = bf16[128,1024]{1,0:T(8,128)(2,1)S(1)} collective-permute-done((bf16[128,1024]{1,0:T(8,128)(2,1)S(1)}, bf16[128,1024]{1,0:T(8,128)(2,1)S(1)}, u32[]{:S(2)}, u32[]{:S(2)}) %collective-permute-start.4) | collective-permute-done | bytes 262176 | tf_op jit(solution)/shard_map/ppermute | solution.py:39
  16.5 2.8 %collective-permute-start.2 = (f32[1024]{0:T(1024)S(1)}, f32[1024]{0:T(1024)S(1)}, u32[]{:S(2)}, u32[]{:S(2)}) collective-permute-start(f32[1024]{0:T(1024)S(1)} %copy-done.1), channel_id=1, source_target_pairs={{0,8},{1,9},{2,10},{3,11},{4,12},{5,13},{6,14},{7,15},{8,0},{9,1},... | collective-permute-start | bytes 12296 | tf_op jit(solution)/shard_map/ppermute | solution.py:39
  20.6 3.2 %collective-permute-start.9 = (s16[1024,128]{1,0:T(8,128)(2,1)S(1)}, s16[1024,128]{1,0:T(8,128)(2,1)S(1)}, u32[]{:S(2)}, u32[]{:S(2)}) collective-permute-start(s16[1024,128]{1,0:T(8,128)(2,1)S(1)} %collective-permute-done.6.refs_6_), channel_id=1, source_target_pairs={{0,8},{1,9},{2,10},{3,11},{4,12},{5,13},{6,14},{7,15},{8,0},{9,1},... | collective-permute-start | bytes 786440 | tf_op jit(solution)/shard_map/ppermute | solution.py:39
  23.8 2.4 %collective-permute-start.8 = (s16[1024,128]{1,0:T(8,128)(2,1)S(1)}, s16[1024,128]{1,0:T(8,128)(2,1)S(1)}, u32[]{:S(2)}, u32[]{:S(2)}) collective-permute-start(s16[1024,128]{1,0:T(8,128)(2,1)S(1)} %collective-permute-done.5.refs_5_), channel_id=1, source_target_pairs={{0,8},{1,9},{2,10},{3,11},{4,12},{5,13},{6,14},{7,15},{8,0},{9,1},... | collective-permute-start | bytes 786440 | tf_op jit(solution)/shard_map/ppermute | solution.py:39
  26.1 1.2 %collective-permute-start.10 = (s16[1024,128]{1,0:T(8,128)(2,1)S(1)}, s16[1024,128]{1,0:T(8,128)(2,1)S(1)}, u32[]{:S(2)}, u32[]{:S(2)}) collective-permute-start(s16[1024,128]{1,0:T(8,128)(2,1)S(1)} %collective-permute-done.1.refs_7_), channel_id=1, source_target_pairs={{0,8},{1,9},{2,10},{3,11},{4,12},{5,13},{6,14},{7,15},{8,0},{9,1},... | collective-permute-start | bytes 786440 | tf_op jit(solution)/shard_map/ppermute | solution.py:39
  28.5 10.3 %sign_rows.1 = bf16[128,1024]{1,0:T(8,128)(2,1)S(1)} custom-call(s32[1]{0:T(128)} %bitcast.8.refs_0_, s32[1]{0:T(128)} %dynamic_slice.9.refs_1_, f32[1,1024]{1,0:T(1,128)S(1)} %bitcast.16, f32[1,1024]{1,0:T(1,128)S(1)} %bitcast.17, s16[1024,128]{1,0:T(8,128)(2,1)S(1)} %collective-permute-done.refs_4_, s16[1024,128]{1,0:T(8,128)(2,1)S(1)} %collective-permute-done.5.refs_5_, ...), custom_call_target="tpu_custom_call" | custom-call | flops 9395240960 | bytes 2097152 | tf_op jit(solution)/shard_map/sign_rows/pallas_call | solution.py:143
  38.8 2.3 %collective-permute-start.12 = (bf16[128,1024]{1,0:T(8,128)(2,1)S(1)}, bf16[128,1024]{1,0:T(8,128)(2,1)S(1)}, u32[]{:S(2)}, u32[]{:S(2)}) collective-permute-start(bf16[128,1024]{1,0:T(8,128)(2,1)S(1)} %sign_rows.1), channel_id=1, source_target_pairs={{0,4},{1,5},{2,6},{3,7},{4,12},{5,13},{6,14},{7,15},{8,0},{9,1},{1... | collective-permute-start | bytes 786440 | tf_op jit(solution)/shard_map/ppermute | solution.py:39
  41.8 1.3 %collective-permute-start.14 = (bf16[128,1024]{1,0:T(8,128)(2,1)S(1)}, bf16[128,1024]{1,0:T(8,128)(2,1)S(1)}, u32[]{:S(2)}, u32[]{:S(2)}) collective-permute-start(bf16[128,1024]{1,0:T(8,128)(2,1)S(1)} %sign_rows.1), channel_id=1, source_target_pairs={{4,14},{5,15},{6,12},{7,13},{8,2},{9,3},{10,0},{11,1},{20,30},{21,... | collective-permute-start | bytes 786440 | tf_op jit(solution)/shard_map/ppermute | solution.py:39
  43.1 2.7 %collective-permute-start.13 = (bf16[128,1024]{1,0:T(8,128)(2,1)S(1)}, bf16[128,1024]{1,0:T(8,128)(2,1)S(1)}, u32[]{:S(2)}, u32[]{:S(2)}) collective-permute-start(bf16[128,1024]{1,0:T(8,128)(2,1)S(1)} %sign_rows.1), channel_id=1, source_target_pairs={{0,2},{1,3},{2,0},{3,1},{12,14},{13,15},{14,12},{15,13},{16,18},{1... | collective-permute-start | bytes 786440 | tf_op jit(solution)/shard_map/ppermute | solution.py:39
  46.5 9.6 %collective-permute-done.14.refs_4_ = bf16[128,1024]{1,0:T(8,128)(2,1)S(1)} collective-permute-done((bf16[128,1024]{1,0:T(8,128)(2,1)S(1)}, bf16[128,1024]{1,0:T(8,128)(2,1)S(1)}, u32[]{:S(2)}, u32[]{:S(2)}) %collective-permute-start.14) | collective-permute-done | bytes 262176 | tf_op jit(solution)/shard_map/ppermute | solution.py:39
  56.1 1.7 %collective-permute-done.13.refs_2_ = bf16[128,1024]{1,0:T(8,128)(2,1)S(1)} collective-permute-done((bf16[128,1024]{1,0:T(8,128)(2,1)S(1)}, bf16[128,1024]{1,0:T(8,128)(2,1)S(1)}, u32[]{:S(2)}, u32[]{:S(2)}) %collective-permute-start.13) | collective-permute-done | bytes 262176 | tf_op jit(solution)/shard_map/ppermute | solution.py:39
  59.5 2.6 %collective-permute-start.17 = (bf16[128,256]{1,0:T(8,128)(2,1)S(1)}, bf16[128,256]{1,0:T(8,128)(2,1)S(1)}, u32[]{:S(2)}, u32[]{:S(2)}) collective-permute-start(bf16[128,256]{1,0:T(8,128)(2,1)S(1)} %get-tuple-element.37), channel_id=1, source_target_pairs={{0,25},{1,24},{2,27},{3,26},{4,29},{5,28},{6,31},{7,30},{8,1},{9,0... | collective-permute-start | bytes 196616 | tf_op jit(solution)/shard_map/ppermute | solution.py:39
  62.1 1.3 %collective-permute-start.18 = (bf16[128,256]{1,0:T(8,128)(2,1)S(1)}, bf16[128,256]{1,0:T(8,128)(2,1)S(1)}, u32[]{:S(2)}, u32[]{:S(2)}) collective-permute-start(bf16[128,256]{1,0:T(8,128)(2,1)S(1)} %get-tuple-element.38), channel_id=1, source_target_pairs={{0,1},{1,0},{2,3},{3,2},{4,5},{5,4},{6,7},{7,6},{8,9},{9,8},{10,11... | collective-permute-start | bytes 196616 | tf_op jit(solution)/shard_map/ppermute | solution.py:39
  65.3 1.5 %collective-permute-start.24 = (bf16[128,512]{1,0:T(8,128)(2,1)S(1)}, bf16[128,512]{1,0:T(8,128)(2,1)S(1)}, u32[]{:S(2)}, u32[]{:S(2)}) collective-permute-start(bf16[128,512]{1,0:T(8,128)(2,1)S(1)} %get-tuple-element.50), channel_id=1, source_target_pairs={{0,24},{1,25},{2,26},{3,27},{4,28},{5,29},{6,30},{7,31},{8,0},{9,1... | collective-permute-start | bytes 393224 | tf_op jit(solution)/shard_map/ppermute | solution.py:39
  66.8 2.6 %collective-permute-start.21 = (bf16[128,256]{1,0:T(8,128)(2,1)S(1)}, bf16[128,256]{1,0:T(8,128)(2,1)S(1)}, u32[]{:S(2)}, u32[]{:S(2)}) collective-permute-start(bf16[128,256]{1,0:T(8,128)(2,1)S(1)} %get-tuple-element.46), channel_id=1, source_target_pairs={{0,25},{1,24},{2,27},{3,26},{4,29},{5,28},{6,31},{7,30},{8,1},{9,0... | collective-permute-start | bytes 196616 | tf_op jit(solution)/shard_map/ppermute | solution.py:39
  69.4 1.3 %collective-permute-start.22 = (bf16[128,256]{1,0:T(8,128)(2,1)S(1)}, bf16[128,256]{1,0:T(8,128)(2,1)S(1)}, u32[]{:S(2)}, u32[]{:S(2)}) collective-permute-start(bf16[128,256]{1,0:T(8,128)(2,1)S(1)} %get-tuple-element.47), channel_id=1, source_target_pairs={{0,1},{1,0},{2,3},{3,2},{4,5},{5,4},{6,7},{7,6},{8,9},{9,8},{10,11... | collective-permute-start | bytes 196616 | tf_op jit(solution)/shard_map/ppermute | solution.py:39
  70.7 1.5 %collective-permute-done.20.refs_5_ = bf16[128,256]{1,0:T(8,128)(2,1)S(1)} collective-permute-done((bf16[128,256]{1,0:T(8,128)(2,1)S(1)}, bf16[128,256]{1,0:T(8,128)(2,1)S(1)}, u32[]{:S(2)}, u32[]{:S(2)}) %collective-permute-start.20) | collective-permute-done | bytes 65568 | tf_op jit(solution)/shard_map/ppermute | solution.py:39
  72.2 1.6 %collective-permute-done.22.refs_7_ = bf16[128,256]{1,0:T(8,128)(2,1)S(1)} collective-permute-done((bf16[128,256]{1,0:T(8,128)(2,1)S(1)}, bf16[128,256]{1,0:T(8,128)(2,1)S(1)}, u32[]{:S(2)}, u32[]{:S(2)}) %collective-permute-start.22) | collective-permute-done | bytes 65568 | tf_op jit(solution)/shard_map/ppermute | solution.py:39
  73.8 1.2 %final.1 = f32[3,128,1024]{2,1,0:T(8,128)} custom-call(s32[1]{0:T(128)} %bitcast.refs_0_, bf16[128,256]{1,0:T(8,128)(2,1)S(1)} %collective-permute-done.16.refs_1_, bf16[128,256]{1,0:T(8,128)(2,1)S(1)} %collective-permute-done.17.refs_2_, bf16[128,256]{1,0:T(8,128)(2,1)S(1)} %collective-permute-done.18.refs_3_, f32[128,256]{1,0:T(8,128)S(1)} %get-tuple-element.39.refs_4_, ...), custom_call_target="tpu_custom_call" | custom-call | bytes 3145728 | tf_op jit(solution)/shard_map/final/pallas_call | solution.py:231
  (48 shorter events, 11.3 us)
Async XLA Ops:
  2.2 8.4 %collective-permute-start = (s16[1024,128]{1,0:T(8,128)(2,1)}, s16[1024,128]{1,0:T(8,128)(2,1)S(1)}, u32[]{:S(2)}, u32[]{:S(2)}) collective-permute-start(s16[1024,128]{1,0:T(8,128)(2,1)} %prepare.1), channel_id=1, source_target_pairs={{0,0},{1,1},{2,2},{3,3},{4,8},{5,9},{6,10},{7,11},{8,4},{9,5},{10,... | collective-permute-start | bytes 786440 | tf_op jit(solution)/shard_map/ppermute | solution.py:39
  4.9 11.6 %collective-permute-start.4 = (bf16[128,1024]{1,0:T(8,128)(2,1)S(1)}, bf16[128,1024]{1,0:T(8,128)(2,1)S(1)}, u32[]{:S(2)}, u32[]{:S(2)}) collective-permute-start(bf16[128,1024]{1,0:T(8,128)(2,1)S(1)} %get-tuple-element.52), channel_id=1, source_target_pairs={{0,8},{1,9},{2,10},{3,11},{4,12},{5,13},{6,14},{7,15},{8,16},{9,17... | collective-permute-start | bytes 786440 | tf_op jit(solution)/shard_map/ppermute | solution.py:39
  9.4 17.9 %collective-permute-start.3 = (bf16[128,1024]{1,0:T(8,128)(2,1)S(1)}, bf16[128,1024]{1,0:T(8,128)(2,1)S(1)}, u32[]{:S(2)}, u32[]{:S(2)}) collective-permute-start(bf16[128,1024]{1,0:T(8,128)(2,1)S(1)} %get-tuple-element.53), channel_id=1, source_target_pairs={{0,24},{1,25},{2,26},{3,27},{4,28},{5,29},{6,30},{7,31},{8,0},{9,1... | collective-permute-start | bytes 786440 | tf_op jit(solution)/shard_map/ppermute | solution.py:39
  10.6 9.9 %collective-permute-start.6 = (s16[1024,128]{1,0:T(8,128)(2,1)S(1)}, s16[1024,128]{1,0:T(8,128)(2,1)S(1)}, u32[]{:S(2)}, u32[]{:S(2)}) collective-permute-start(s16[1024,128]{1,0:T(8,128)(2,1)S(1)} %collective-permute-done.refs_4_), channel_id=1, source_target_pairs={{0,2},{1,3},{2,0},{3,1},{4,6},{5,7},{6,4},{7,5},{8,10},{9,11},{10,... | collective-permute-start | bytes 786440 | tf_op jit(solution)/shard_map/ppermute | solution.py:39
  12.2 11.6 %collective-permute-start.5 = (s16[1024,128]{1,0:T(8,128)(2,1)S(1)}, s16[1024,128]{1,0:T(8,128)(2,1)S(1)}, u32[]{:S(2)}, u32[]{:S(2)}) collective-permute-start(s16[1024,128]{1,0:T(8,128)(2,1)S(1)} %collective-permute-done.refs_4_), channel_id=1, source_target_pairs={{0,1},{1,0},{2,3},{3,2},{4,5},{5,4},{6,7},{7,6},{8,9},{9,8},{10,11... | collective-permute-start | bytes 786440 | tf_op jit(solution)/shard_map/ppermute | solution.py:39
  13.7 12.4 %collective-permute-start.1 = (s16[1024,128]{1,0:T(8,128)(2,1)S(1)}, s16[1024,128]{1,0:T(8,128)(2,1)S(1)}, u32[]{:S(2)}, u32[]{:S(2)}) collective-permute-start(s16[1024,128]{1,0:T(8,128)(2,1)S(1)} %collective-permute-done.refs_4_), channel_id=1, source_target_pairs={{0,3},{1,2},{2,1},{3,0},{4,7},{5,6},{6,5},{7,4},{8,11},{9,10},{10,... | collective-permute-start | bytes 786440 | tf_op jit(solution)/shard_map/ppermute | solution.py:39
  16.5 3.7 %collective-permute-start.2 = (f32[1024]{0:T(1024)S(1)}, f32[1024]{0:T(1024)S(1)}, u32[]{:S(2)}, u32[]{:S(2)}) collective-permute-start(f32[1024]{0:T(1024)S(1)} %copy-done.1), channel_id=1, source_target_pairs={{0,8},{1,9},{2,10},{3,11},{4,12},{5,13},{6,14},{7,15},{8,0},{9,1},... | collective-permute-start | bytes 12296 | tf_op jit(solution)/shard_map/ppermute | solution.py:39
  20.2 8.3 %collective-permute-start.7 = (s16[1024,128]{1,0:T(8,128)(2,1)S(1)}, s16[1024,128]{1,0:T(8,128)(2,1)S(1)}, u32[]{:S(2)}, u32[]{:S(2)}) collective-permute-start(s16[1024,128]{1,0:T(8,128)(2,1)S(1)} %collective-permute-done.refs_4_), channel_id=1, source_target_pairs={{0,8},{1,9},{2,10},{3,11},{4,12},{5,13},{6,14},{7,15},{8,0},{9,1},... | collective-permute-start | bytes 786440 | tf_op jit(solution)/shard_map/ppermute | solution.py:39
  20.6 7.9 %collective-permute-start.9 = (s16[1024,128]{1,0:T(8,128)(2,1)S(1)}, s16[1024,128]{1,0:T(8,128)(2,1)S(1)}, u32[]{:S(2)}, u32[]{:S(2)}) collective-permute-start(s16[1024,128]{1,0:T(8,128)(2,1)S(1)} %collective-permute-done.6.refs_6_), channel_id=1, source_target_pairs={{0,8},{1,9},{2,10},{3,11},{4,12},{5,13},{6,14},{7,15},{8,0},{9,1},... | collective-permute-start | bytes 786440 | tf_op jit(solution)/shard_map/ppermute | solution.py:39
  23.8 4.7 %collective-permute-start.8 = (s16[1024,128]{1,0:T(8,128)(2,1)S(1)}, s16[1024,128]{1,0:T(8,128)(2,1)S(1)}, u32[]{:S(2)}, u32[]{:S(2)}) collective-permute-start(s16[1024,128]{1,0:T(8,128)(2,1)S(1)} %collective-permute-done.5.refs_5_), channel_id=1, source_target_pairs={{0,8},{1,9},{2,10},{3,11},{4,12},{5,13},{6,14},{7,15},{8,0},{9,1},... | collective-permute-start | bytes 786440 | tf_op jit(solution)/shard_map/ppermute | solution.py:39
  27.4 30.3 %collective-permute-start.15 = (bf16[384,1024]{1,0:T(8,128)(2,1)S(1)}, bf16[384,1024]{1,0:T(8,128)(2,1)S(1)}, u32[]{:S(2)}, u32[]{:S(2)}) collective-permute-start(bf16[384,1024]{1,0:T(8,128)(2,1)S(1)} %pad_maximum_fusion.refs_0_), channel_id=1, source_target_pairs={{0,1},{1,0},{2,3},{3,2},{4,5},{5,4},{6,7},{7,6},{8,9},{9,8},{10,11... | collective-permute-start | bytes 2359304 | tf_op jit(solution)/shard_map/ppermute | solution.py:39
  38.8 7.7 %collective-permute-start.12 = (bf16[128,1024]{1,0:T(8,128)(2,1)S(1)}, bf16[128,1024]{1,0:T(8,128)(2,1)S(1)}, u32[]{:S(2)}, u32[]{:S(2)}) collective-permute-start(bf16[128,1024]{1,0:T(8,128)(2,1)S(1)} %sign_rows.1), channel_id=1, source_target_pairs={{0,4},{1,5},{2,6},{3,7},{4,12},{5,13},{6,14},{7,15},{8,0},{9,1},{1... | collective-permute-start | bytes 786440 | tf_op jit(solution)/shard_map/ppermute | solution.py:39
  41.1 5.4 %collective-permute-start.11 = (bf16[128,1024]{1,0:T(8,128)(2,1)S(1)}, bf16[128,1024]{1,0:T(8,128)(2,1)S(1)}, u32[]{:S(2)}, u32[]{:S(2)}) collective-permute-start(bf16[128,1024]{1,0:T(8,128)(2,1)S(1)} %sign_rows.1), channel_id=1, source_target_pairs={{0,0},{1,1},{2,2},{3,3},{4,8},{5,9},{6,10},{7,11},{8,4},{9,5},{10,... | collective-permute-start | bytes 786440 | tf_op jit(solution)/shard_map/ppermute | solution.py:39
  41.8 14.4 %collective-permute-start.14 = (bf16[128,1024]{1,0:T(8,128)(2,1)S(1)}, bf16[128,1024]{1,0:T(8,128)(2,1)S(1)}, u32[]{:S(2)}, u32[]{:S(2)}) collective-permute-start(bf16[128,1024]{1,0:T(8,128)(2,1)S(1)} %sign_rows.1), channel_id=1, source_target_pairs={{4,14},{5,15},{6,12},{7,13},{8,2},{9,3},{10,0},{11,1},{20,30},{21,... | collective-permute-start | bytes 786440 | tf_op jit(solution)/shard_map/ppermute | solution.py:39
  43.1 14.7 %collective-permute-start.13 = (bf16[128,1024]{1,0:T(8,128)(2,1)S(1)}, bf16[128,1024]{1,0:T(8,128)(2,1)S(1)}, u32[]{:S(2)}, u32[]{:S(2)}) collective-permute-start(bf16[128,1024]{1,0:T(8,128)(2,1)S(1)} %sign_rows.1), channel_id=1, source_target_pairs={{0,2},{1,3},{2,0},{3,1},{12,14},{13,15},{14,12},{15,13},{16,18},{1... | collective-permute-start | bytes 786440 | tf_op jit(solution)/shard_map/ppermute | solution.py:39
  57.8 5.6 %collective-permute-start.19 = (bf16[256,1024]{1,0:T(8,128)(2,1)S(1)}, bf16[256,1024]{1,0:T(8,128)(2,1)S(1)}, u32[]{:S(2)}, u32[]{:S(2)}) collective-permute-start(bf16[256,1024]{1,0:T(8,128)(2,1)S(1)} %pad_maximum_fusion.1), channel_id=1, source_target_pairs={{4,6},{5,7},{6,4},{7,5},{8,10},{9,11},{10,8},{11,9},{20,22},{21,23... | collective-permute-start | bytes 1572872 | tf_op jit(solution)/shard_map/ppermute | solution.py:39
  59.4 7.3 %collective-permute-start.16 = (bf16[128,256]{1,0:T(8,128)(2,1)S(1)}, bf16[128,256]{1,0:T(8,128)(2,1)S(1)}, u32[]{:S(2)}, u32[]{:S(2)}) collective-permute-start(bf16[128,256]{1,0:T(8,128)(2,1)S(1)} %get-tuple-element.36), channel_id=1, source_target_pairs={{0,9},{1,8},{2,11},{3,10},{4,13},{5,12},{6,15},{7,14},{8,17},{9,16... | collective-permute-start | bytes 196616 | tf_op jit(solution)/shard_map/ppermute | solution.py:39
  59.5 7.3 %collective-permute-start.17 = (bf16[128,256]{1,0:T(8,128)(2,1)S(1)}, bf16[128,256]{1,0:T(8,128)(2,1)S(1)}, u32[]{:S(2)}, u32[]{:S(2)}) collective-permute-start(bf16[128,256]{1,0:T(8,128)(2,1)S(1)} %get-tuple-element.37), channel_id=1, source_target_pairs={{0,25},{1,24},{2,27},{3,26},{4,29},{5,28},{6,31},{7,30},{8,1},{9,0... | collective-permute-start | bytes 196616 | tf_op jit(solution)/shard_map/ppermute | solution.py:39
  62.1 7.3 %collective-permute-start.18 = (bf16[128,256]{1,0:T(8,128)(2,1)S(1)}, bf16[128,256]{1,0:T(8,128)(2,1)S(1)}, u32[]{:S(2)}, u32[]{:S(2)}) collective-permute-start(bf16[128,256]{1,0:T(8,128)(2,1)S(1)} %get-tuple-element.38), channel_id=1, source_target_pairs={{0,1},{1,0},{2,3},{3,2},{4,5},{5,4},{6,7},{7,6},{8,9},{9,8},{10,11... | collective-permute-start | bytes 196616 | tf_op jit(solution)/shard_map/ppermute | solution.py:39
  64.4 9.4 %collective-permute-start.23 = (bf16[128,512]{1,0:T(8,128)(2,1)S(1)}, bf16[128,512]{1,0:T(8,128)(2,1)S(1)}, u32[]{:S(2)}, u32[]{:S(2)}) collective-permute-start(bf16[128,512]{1,0:T(8,128)(2,1)S(1)} %get-tuple-element.49), channel_id=1, source_target_pairs={{0,8},{1,9},{2,10},{3,11},{4,12},{5,13},{6,14},{7,15},{8,16},{9,17... | collective-permute-start | bytes 393224 | tf_op jit(solution)/shard_map/ppermute | solution.py:39
  65.3 8.5 %collective-permute-start.24 = (bf16[128,512]{1,0:T(8,128)(2,1)S(1)}, bf16[128,512]{1,0:T(8,128)(2,1)S(1)}, u32[]{:S(2)}, u32[]{:S(2)}) collective-permute-start(bf16[128,512]{1,0:T(8,128)(2,1)S(1)} %get-tuple-element.50), channel_id=1, source_target_pairs={{0,24},{1,25},{2,26},{3,27},{4,28},{5,29},{6,30},{7,31},{8,0},{9,1... | collective-permute-start | bytes 393224 | tf_op jit(solution)/shard_map/ppermute | solution.py:39
  66.8 5.4 %collective-permute-start.20 = (bf16[128,256]{1,0:T(8,128)(2,1)S(1)}, bf16[128,256]{1,0:T(8,128)(2,1)S(1)}, u32[]{:S(2)}, u32[]{:S(2)}) collective-permute-start(bf16[128,256]{1,0:T(8,128)(2,1)S(1)} %get-tuple-element.45), channel_id=1, source_target_pairs={{0,9},{1,8},{2,11},{3,10},{4,13},{5,12},{6,15},{7,14},{8,17},{9,16... | collective-permute-start | bytes 196616 | tf_op jit(solution)/shard_map/ppermute | solution.py:39
  66.8 5.4 %collective-permute-start.21 = (bf16[128,256]{1,0:T(8,128)(2,1)S(1)}, bf16[128,256]{1,0:T(8,128)(2,1)S(1)}, u32[]{:S(2)}, u32[]{:S(2)}) collective-permute-start(bf16[128,256]{1,0:T(8,128)(2,1)S(1)} %get-tuple-element.46), channel_id=1, source_target_pairs={{0,25},{1,24},{2,27},{3,26},{4,29},{5,28},{6,31},{7,30},{8,1},{9,0... | collective-permute-start | bytes 196616 | tf_op jit(solution)/shard_map/ppermute | solution.py:39
  69.4 4.4 %collective-permute-start.22 = (bf16[128,256]{1,0:T(8,128)(2,1)S(1)}, bf16[128,256]{1,0:T(8,128)(2,1)S(1)}, u32[]{:S(2)}, u32[]{:S(2)}) collective-permute-start(bf16[128,256]{1,0:T(8,128)(2,1)S(1)} %get-tuple-element.47), channel_id=1, source_target_pairs={{0,1},{1,0},{2,3},{3,2},{4,5},{5,4},{6,7},{7,6},{8,9},{9,8},{10,11... | collective-permute-start | bytes 196616 | tf_op jit(solution)/shard_map/ppermute | solution.py:39
  (4 other events, 47.1 us)
